TPU v7x, 128 devices: a whole 4x4x4 slice. The times are simulated.
128 devices in a mesh: lon: 16 (over y_lo, x, core), sub: 8 (over z, y_hi).
Axes of the slice: x: 4, y: 4 (y_hi: 2, y_lo: 2; y = y_hi * 2 + y_lo), z: 4, core: 2. Of those that a mesh axis runs over, the one named last changes fastest.
Arguments:
- atm_tracer: float32 [128, 128, 4096], P('sub', None, 'lon'), may hold values from -6 to 6
- courant: float32 [128, 128, 4096], P('sub', None, 'lon'), may hold values from -0.9 to 0.9
- column_inverse: float32 [8, 128, 128], replicated
- heat_exchange_factor: float32 [128, 4096], P(None, 'lon'), may hold values from 0.3 to 3
- ocean_temp: float32 [32, 64, 2048], P(None, 'sub', 'lon'), may hold values from -6 to 6
- diffusivity: float32 [64, 2048], P('sub', 'lon'), may hold values from 0.04 to 0.2
- ocean_inverse: float32 [32, 32], replicated
- land_mask: int32 [64, 2048], P('sub', 'lon'), may hold values 0 or 1
- regrid_weight_blocks: float32 [64, 128, 128], replicated, may hold values from -0.25 to 0.25
- a2o_src: int32 [64, 16, 4], P('sub', 'lon'), may hold values from 0 to 4095, as said below
- a2o_wgt: int32 [64, 16, 4], P('sub', 'lon'), may hold values from 0 to 63
- ocean_to_atmos_source: int32 [128, 32, 4], P(None, 'lon'), may hold values from 0 to 1023, as said below
- ocean_to_atmos_weight: int32 [128, 32, 4], P(None, 'lon'), may hold values from 0 to 63
Outputs:
- atmos_temp_updated: float32 [128, 128, 4096], P('sub', None, 'lon')
- ocean_new: float32 [32, 64, 2048], P(None, 'sub', 'lon')
- atmos_heat_flux: float32 [128, 4096], P('sub', 'lon')
Inputs may be any that keep to these rules, and one draw needn't show every extreme that they name: `a2o_src`: for ocean block row r in tile column t, every entry names an atmosphere block of a row in r // 8 * 16 to (r // 8 + 1) * 16 - 1 and of a column group g with (g - t * 2) mod 32 below 4. `ocean_to_atmos_source`: for atmosphere block row r and column group g, every entry names an ocean block of a row in r // 16 * 8 to (r // 16 + 1) * 8 - 1 and of tile column s or s - 1 (mod 16), where s = g // 2.
All inputs are finite; a program needn't handle non-finite values. No bound on the sum of `land_mask` on one device may be relied on, other than what follows from the above.
Results may differ from a plain program's by a relative error of at most 0.000096.
Values sent between devices are 32-bit elements; how exact they have to be, the bound alone decides.
No kernel may reach another device: no remote copies, remote signals or barrier semaphores. Data moves between devices by JAX's collectives and lax.ppermute only.
A program may use at most 64 MiB of HBM per device.

v0:
```python
import math

import jax
import jax.numpy as jnp
from jax import lax
from jax.sharding import PartitionSpec as P


def passed_along(value, axis, steps):
    count = lax.axis_size(axis)
    pairs = [(source, (source + steps) % count) for source in range(count)]
    return lax.ppermute(value, axis, pairs)


def with_halo(cells, sides, width):
    for axis, dim in sides:
        count = lax.axis_size(axis)
        head = lax.slice_in_dim(cells, 0, width, axis=dim)
        tail = lax.slice_in_dim(cells, cells.shape[dim] - width, cells.shape[dim], axis=dim)
        cells = jnp.concatenate(
            [
                lax.ppermute(tail, axis, [(i, (i + 1) % count) for i in range(count)]),
                cells,
                lax.ppermute(head, axis, [((i + 1) % count, i) for i in range(count)]),
            ],
            axis=dim,
        )
    return cells


def padded_2(value, sides, width):
    edges = {}
    for axis, dim in sides:
        size, length = (lax.axis_size(axis), value.shape[dim])
        up = [(i, (i + 1) % size) for i in range(size)]
        last = lax.slice_in_dim(value, length - width, length, axis=dim)
        first = lax.slice_in_dim(value, 0, width, axis=dim)
        edges[dim] = (
            lax.ppermute(last, axis, up),
            lax.ppermute(first, axis, [(b, a) for a, b in up]),
        )
    done = []
    for _, dim in sides:
        low, high = edges[dim]
        around = [(width, width) if d in done else (0, 0) for d in range(value.ndim)]
        value = jnp.concatenate([jnp.pad(low, around), value, jnp.pad(high, around)], axis=dim)
        done.append(dim)
    return value


def regrid_block_list(blocks, src_ids, wgt_ids, weights):
    count = src_ids.shape[0]
    width = src_ids.shape[1]
    step = math.gcd(count, 16)

    def one_group(pair):
        src_part, wgt_part = pair
        picked = blocks[src_part]
        mats = weights[wgt_part]
        return jnp.einsum("dkij,dkj->di", mats, picked, precision=lax.Precision.HIGHEST)

    result = lax.map(
        one_group,
        (src_ids.reshape(count // step, step, width), wgt_ids.reshape(count // step, step, width)),
    )
    return result.reshape(count, blocks.shape[1])


def sea_window(sea):
    west_sea = passed_along(sea, "lon", 1)
    return jnp.concatenate([west_sea, sea], axis=1)


def ocean_local_ids(src_ids, base_row, lon_index, n_lon):
    ocean_row = src_ids // n_lon
    ocean_tile = src_ids % n_lon
    return (ocean_row - base_row) * 2 + jnp.remainder(ocean_tile - lon_index + 1, n_lon)


def flux_to_ocean(
    flux_band, a2o_src, a2o_wgt, regrid_weight_blocks, sub_index, lon_index, aband, groups, ngroups
):
    east_flux = passed_along(flux_band, "lon", -1)
    window = jnp.concatenate([flux_band, east_flux], axis=1)
    block = regrid_weight_blocks.shape[1]
    blocks = window.reshape(-1, block)
    width = a2o_src.shape[2]
    src_ids = a2o_src.reshape(-1, width)
    atm_row = src_ids // ngroups
    atm_grp = src_ids % ngroups
    local_ids = (atm_row - sub_index * aband) * (2 * groups) + jnp.remainder(
        atm_grp - lon_index * groups, ngroups
    )
    return regrid_block_list(blocks, local_ids, a2o_wgt.reshape(-1, width), regrid_weight_blocks)


def per_device(
    atm_tracer,
    courant,
    column_inverse,
    heat_exchange_factor,
    ocean_temp,
    diffusivity,
    ocean_inverse,
    land_mask,
    regrid_weight_blocks,
    a2o_src,
    a2o_wgt,
    ocean_to_atmos_source,
    ocean_to_atmos_weight,
):
    lon_index = lax.axis_index("lon")
    sub_index = lax.axis_index("sub")
    n_lon = lax.axis_size("lon")
    n_sub = lax.axis_size("sub")
    lev_dev, alat, alon_dev = atm_tracer.shape
    levels = lev_dev * n_sub
    block = regrid_weight_blocks.shape[1]
    groups = alon_dev // block
    ngroups = groups * n_lon
    olev, olat_dev, olon_dev = ocean_temp.shape
    aband = alat // n_sub
    nband = column_inverse.shape[0]
    rows_band = alat // nband
    local_bands = nband // n_sub
    width = ocean_to_atmos_source.shape[2]
    padded = with_halo(atm_tracer, (("lon", 2),), 1)
    west = padded[:, :, :-2]
    east = padded[:, :, 2:]
    advected = (
        atm_tracer
        - jnp.maximum(courant, 0.0) * (atm_tracer - west)
        - jnp.minimum(courant, 0.0) * (east - atm_tracer)
    )
    sea_mask = land_mask.astype(jnp.float32)
    sea = sea_mask * ocean_temp[0]
    band_inv = lax.dynamic_slice_in_dim(column_inverse, sub_index * local_bands, local_bands, 0)
    columns = lax.all_to_all(advected, "sub", split_axis=1, concat_axis=0, tiled=True)
    items = columns.shape[2]
    shaped = columns.reshape(levels, local_bands, rows_band * items)
    result = jnp.einsum("blm,mbc->lbc", band_inv, shaped, precision=lax.Precision.HIGHEST).reshape(
        levels, aband, items
    )
    returned = lax.all_to_all(result, "sub", split_axis=0, concat_axis=1, tiled=True)
    bottom = result[levels - 1 :]
    air_state = bottom[0]
    ocean_block_list = sea_window(sea).reshape(-1, block)
    band_src = lax.dynamic_slice_in_dim(ocean_to_atmos_source, sub_index * aband, aband, 0).reshape(
        -1, width
    )
    band_wgt = lax.dynamic_slice_in_dim(ocean_to_atmos_weight, sub_index * aband, aband, 0).reshape(
        -1, width
    )
    local_ids = ocean_local_ids(band_src, sub_index * olat_dev, lon_index, n_lon)
    sea_surface_temp_atmos = regrid_block_list(
        ocean_block_list, local_ids, band_wgt, regrid_weight_blocks
    ).reshape(aband, alon_dev)
    coef_band = lax.dynamic_slice_in_dim(heat_exchange_factor, sub_index * aband, aband, 0)
    flux_band = coef_band * (sea_surface_temp_atmos - air_state)
    flux_ocean = flux_to_ocean(
        flux_band,
        a2o_src,
        a2o_wgt,
        regrid_weight_blocks,
        sub_index,
        lon_index,
        aband,
        groups,
        ngroups,
    )
    rim = padded_2(ocean_temp, (("lon", 2), ("sub", 1)), 1)
    o_west = rim[:, 1:-1, :-2]
    o_east = rim[:, 1:-1, 2:]
    south = rim[:, :-2, 1:-1]
    north = rim[:, 2:, 1:-1]
    top_row = ocean_temp[:, olat_dev - 1, :]
    whole_top = lax.all_gather(top_row, "lon", axis=1, tiled=True)
    mirror_tile = lax.dynamic_slice_in_dim(
        whole_top, (n_lon - 1 - lon_index) * olon_dev, olon_dev, 1
    )
    folded = jnp.flip(mirror_tile, axis=1)
    south = south.at[:, 0, :].set(jnp.where(sub_index == 0, ocean_temp[:, 0, :], south[:, 0, :]))
    north = north.at[:, olat_dev - 1, :].set(
        jnp.where(sub_index == n_sub - 1, folded, north[:, olat_dev - 1, :])
    )
    lap = o_west + o_east + north + south - 4.0 * ocean_temp
    stepped = sea_mask * (ocean_temp + diffusivity * lap)
    stepped = stepped.at[0].add(sea_mask * flux_ocean)
    ocean_new = jnp.einsum(
        "lm,mc->lc",
        ocean_inverse,
        stepped.reshape(olev, olat_dev * olon_dev),
        precision=lax.Precision.HIGHEST,
    ).reshape(olev, olat_dev, olon_dev)
    return (returned, ocean_new, flux_band)


def solution(mesh):
    return jax.shard_map(
        per_device,
        mesh=mesh,
        in_specs=(
            P("sub", None, "lon"),
            P("sub", None, "lon"),
            P(),
            P(None, "lon"),
            P(None, "sub", "lon"),
            P("sub", "lon"),
            P(),
            P("sub", "lon"),
            P(),
            P("sub", "lon", None),
            P("sub", "lon", None),
            P(None, "lon", None),
            P(None, "lon", None),
        ),
        out_specs=(P("sub", None, "lon"), P(None, "sub", "lon"), P("sub", "lon")),
        check_vma=False,
    )
```

profile of v0, /device:TPU:7, one launch (start us, length us, event | category | flops | bytes accessed | tf_op | source)
XLA Modules:
  0.0 112.7 jit_solution(17873088445448974378)
XLA Ops:
  0.6 3.3 %fusion.39 = (f32[16,128,1]{2,1,0:T(8,128)}, f32[16,128,1]{2,1,0:T(8,128)}) fusion(f32[16,128,256]{2,1,0:T(8,128)} %param.21), kind=kLoop, calls=%fused_computation.96 | loop fusion | bytes 32768 | tf_op jit(solution)/shard_map/slice | solution.py:19
  3.9 1.7 %copy.76 = f32[16,128,1]{1,0,2:T(8,128)S(1)} copy(f32[16,128,1]{2,1,0:T(8,128)} %get-tuple-element.128) | data formatting | bytes 16384
  5.6 1.8 %collective-permute-start = (f32[16,128,1]{1,0,2:T(8,128)S(1)}, f32[16,128,1]{1,0,2:T(8,128)S(1)}, u32[]{:S(2)}, u32[]{:S(2)}) collective-permute-start(f32[16,128,1]{1,0,2:T(8,128)S(1)} %copy.76), channel_id=1, source_target_pairs={{0,8},{8,16},{16,24},{24,32},{32,40},{40,48},{48,56},{56,64},{64,7... | collective-permute-start | bytes 24584 | tf_op jit(solution)/shard_map/ppermute | solution.py:22
  7.4 1.6 %copy.77 = f32[16,128,1]{1,0,2:T(8,128)S(1)} copy(f32[16,128,1]{2,1,0:T(8,128)} %get-tuple-element.129) | data formatting | bytes 16384
  9.0 2.5 %copy.56 = f32[16,128,256]{2,0,1:T(8,128)} copy(f32[16,128,256]{2,1,0:T(8,128)S(1)} %copy-done.1) | data formatting | bytes 4194304 | tf_op args[0]
  11.6 1.4 %copy.53 = f32[16,128,1]{2,0,1:T(8,128)} copy(f32[16,128,1]{1,0,2:T(8,128)S(1)} %collective-permute-done) | data formatting | bytes 16384 | tf_op jit(solution)/shard_map/ppermute | solution.py:22
  13.0 1.2 %collective-permute-done.1 = f32[16,128,1]{1,0,2:T(8,128)S(1)} collective-permute-done((f32[16,128,1]{1,0,2:T(8,128)S(1)}, f32[16,128,1]{1,0,2:T(8,128)S(1)}, u32[]{:S(2)}, u32[]{:S(2)}) %collective-permute-start.1) | collective-permute-done | bytes 8224 | tf_op jit(solution)/shard_map/ppermute | solution.py:24
  14.2 1.4 %copy.60 = f32[16,128,1]{2,0,1:T(8,128)} copy(f32[16,128,1]{1,0,2:T(8,128)S(1)} %collective-permute-done.1) | data formatting | bytes 16384 | tf_op jit(solution)/shard_map/ppermute | solution.py:24
  15.6 5.3 %fusion.2 = f32[16,128,256]{2,0,1:T(8,128)} fusion(f32[16,128,256]{2,0,1:T(8,128)S(1)} %copy-done.2, f32[16,128,1]{2,0,1:T(8,128)} %copy.60, f32[16,128,1]{2,0,1:T(8,128)} %copy.53, f32[16,128,256]{2,1,0:T(8,128)} %param.22), kind=kLoop, calls=%fused_computation.13 | loop fusion | flops 5242880 | bytes 6307840 | tf_op jit(solution)/shard_map/sub | solution.py:131
  20.9 7.5 %all-to-all-start = ((f32[16,128,256]{2,0,1:T(8,128)}), f32[16,128,256]{2,0,1:T(8,128)S(1)}, u32[]{:S(2)}, u32[]{:S(2)}) async-start(f32[16,128,256]{2,0,1:T(8,128)} %fusion.2), calls=%async_computation | async-start | bytes 4194304 | tf_op jit(solution)/shard_map/all_to_all | solution.py:138
  28.5 2.4 %collective-permute-start.6 = (f32[8,128]{1,0:T(8,128)S(1)}, f32[8,128]{1,0:T(8,128)S(1)}, u32[]{:S(2)}, u32[]{:S(2)}) collective-permute-start(f32[8,128]{1,0:T(8,128)S(1)} %bitcast_multiply_fusion), channel_id=1, source_target_pairs={{0,8},{8,16},{16,24},{24,32},{32,40},{40,48},{48,56},{56,64},{64,7... | collective-permute-start | bytes 12296 | tf_op jit(solution)/shard_map/ppermute | solution.py:12
  30.9 3.9 %collective-permute-start.5 = (f32[32,1,128]{2,1,0:T(1,128)S(1)}, f32[32,1,128]{2,1,0:T(1,128)S(1)}, u32[]{:S(2)}, u32[]{:S(2)}) collective-permute-start(f32[32,1,128]{2,1,0:T(1,128)S(1)} %slice.129), channel_id=1, source_target_pairs={{0,1},{1,2},{2,3},{3,4},{4,5},{5,6},{6,7},{7,0},{8,9},{9,10},{10,1... | collective-permute-start | bytes 49160 | tf_op jit(solution)/shard_map/ppermute | solution.py:39
  36.0 18.4 %all-gather = f32[32,1,2048]{2,1,0:T(1,128)S(1)} all-gather(f32[32,1,128]{2,1,0:T(1,128)S(1)} %slice.129), channel_id=2, replica_groups=mesh['lon'=16,'sub'=8] {'lon'}, dimensions={2}, use_global_device_ids=true | all-gather | bytes 278528 | tf_op jit(solution)/shard_map/all_gather | solution.py:177
  54.8 4.3 %gather_fusion.2 = f32[32,128,128]{2,1,0:T(8,128)} fusion(f32[64,128,128]{2,1,0:T(8,128)} %param.29, s32[1024]{0:T(1024)S(1)} %pad_clamp_fusion.3), kind=kCustom, calls=%fused_computation.2 | custom fusion | bytes 4194432 | tf_op jit(solution)/shard_map/while/body/eval_jaxpr/gather | solution.py:59
  59.1 0.8 collective-permute-done.5
  59.9 1.6 %collective-permute-start.4 = (f32[32,1,128]{2,1,0:T(1,128)S(1)}, f32[32,1,128]{2,1,0:T(1,128)S(1)}, u32[]{:S(2)}, u32[]{:S(2)}) collective-permute-start(f32[32,1,128]{2,1,0:T(1,128)S(1)} %get-tuple-element.132), channel_id=1, source_target_pairs={{1,0},{2,1},{3,2},{4,3},{5,4},{6,5},{7,6},{0,7},{9,8},{10,9},{11,1... | collective-permute-start | bytes 49160 | tf_op jit(solution)/shard_map/ppermute | solution.py:40
  61.5 1.2 %copy.62 = f32[16,8,16,256]{3,2,0,1:T(8,128)S(1)} copy(f32[16,8,16,256]{3,0,2,1:T(8,128)S(1)} %bitcast.124) | data formatting | bytes 4194304 | tf_op jit(solution)/shard_map/all_to_all | solution.py:138
  62.7 1.6 %copy.78 = f32[16,8,16,256]{3,1,2,0:T(8,128)S(1)} copy(f32[16,8,16,256]{3,2,1,0:T(8,128)S(1)} %bitcast.126) | data formatting | bytes 4194304
  64.4 3.5 %fusion.17 = f32[4096,128]{1,0:T(8,128)S(1)} fusion(f32[128,4096]{1,0:T(8,128)S(1)} %bitcast.125, f32[8,128,128]{2,1,0:T(8,128)S(1)} %copy-done, s32[]{:T(128)S(6)} %select_n.123), kind=kOutput, calls=%fused_computation.40 | convolution fusion | flops 805306368 | bytes 4259844 | tf_op jit(solution)/shard_map/blm,mbc->lbc/dot_general | solution.py:141
  67.9 2.0 %copy.63 = f32[128,16,256]{2,1,0:T(8,128)} copy(f32[128,16,256]{0,2,1:T(8,128)S(1)} %bitcast.121) | data formatting | bytes 4194304 | tf_op jit(solution)/shard_map/reshape | solution.py:141
  69.9 4.5 %all-to-all-start.1 = ((f32[128,16,256]{2,1,0:T(8,128)}), f32[128,16,256]{2,1,0:T(8,128)}, u32[]{:S(2)}, u32[]{:S(2)}) async-start(f32[128,16,256]{2,1,0:T(8,128)} %copy.63), calls=%async_computation.1 | async-start | bytes 4194304 | tf_op jit(solution)/shard_map/all_to_all | solution.py:144
  74.4 22.6 %while.17 = (s32[]{:T(128)}, f32[2,16,128]{2,1,0:T(8,128)S(1)}, s32[2,16,4]{1,2,0:T(4,128)S(1)}, f32[64,128,128]{2,1,0:T(8,128)}, s32[2,16,4]{1,2,0:T(4,128)S(1)}, /*index=5*/f32[16,128]{1,0:T(8,128)S(1)}, s32[]{:T(128)}) while((s32[]{:T(128)}, f32[2,16,128]{2,1,0:T(8,128)S(1)}, s32[2,16,4]{1,2,0:T(4,128)S(1)}, f32[64,128,128]{2,1,0:T(8,128)}, ...), condition=%wide.region_1.2_spmd, body=%wide.region_0.1_spmd.sunk | while | flops 12585346 | bytes 12718165 | solution.py:62
  74.6 5.0 %gather_fusion = f32[64,128,128]{2,1,0:T(8,128)} fusion(f32[64,128,128]{2,1,0:T(8,128)} %get-tuple-element.196, s32[1024]{0:T(1024)S(1)} %pad_clamp_fusion.6), kind=kCustom, calls=%fused_computation.clone.1 | custom fusion | bytes 8388864 | tf_op jit(solution)/shard_map/while/body/eval_jaxpr/gather | solution.py:59
  80.3 5.3 %fusion.55 = f32[16,1,128,1]{2,1,3,0:T(1,128)S(1)} fusion(f32[16,4,128,128]{3,2,1,0:T(8,128)} %bitcast.120, f32[16,4,128,1]{2,3,1,0:T(1,128)S(1)} %bitcast.127), kind=kOutput, calls=%fused_computation.99.clone.1 | convolution fusion | flops 12582912 | bytes 4235264 | tf_op jit(solution)/shard_map/while/body/eval_jaxpr/dkij,dkj->di/dot_general | solution.py:60
  85.9 5.0 %gather_fusion = f32[64,128,128]{2,1,0:T(8,128)} fusion(f32[64,128,128]{2,1,0:T(8,128)} %get-tuple-element.196, s32[1024]{0:T(1024)S(1)} %pad_clamp_fusion.6), kind=kCustom, calls=%fused_computation.clone.1 | custom fusion | bytes 8388864 | tf_op jit(solution)/shard_map/while/body/eval_jaxpr/gather | solution.py:59
  91.6 5.3 %fusion.55 = f32[16,1,128,1]{2,1,3,0:T(1,128)S(1)} fusion(f32[16,4,128,128]{3,2,1,0:T(8,128)} %bitcast.120, f32[16,4,128,1]{2,3,1,0:T(1,128)S(1)} %bitcast.127), kind=kOutput, calls=%fused_computation.99.clone.1 | convolution fusion | flops 12582912 | bytes 4235264 | tf_op jit(solution)/shard_map/while/body/eval_jaxpr/dkij,dkj->di/dot_general | solution.py:60
  97.4 1.2 %slice_reduce_fusion = f32[4096]{0:T(1024)S(1)} fusion(f32[128,1,4096]{0,2,1:T(8,128)S(1)} %bitcast.122), kind=kLoop, calls=%fused_computation.9 | loop fusion | bytes 32768 | tf_op jit(solution)/shard_map/slice | solution.py:145
  98.6 0.7 subtract_multiply_fusion
  99.3 0.7 collective-permute-start.7
  100.2 4.4 %collective-permute-done.7 = f32[16,256]{1,0:T(8,128)S(1)} collective-permute-done((f32[16,256]{1,0:T(8,128)S(1)}, f32[16,256]{1,0:T(8,128)S(1)}, u32[]{:S(2)}, u32[]{:S(2)}) %collective-permute-start.7) | collective-permute-done | bytes 16416 | tf_op jit(solution)/shard_map/ppermute | solution.py:12
  105.2 3.4 %fusion.43 = f32[8,1,128,1]{2,1,3,0:T(1,128)S(1)} fusion(f32[8,4,128,128]{3,2,1,0:T(8,128)} %bitcast.123, f32[8,4,128,1]{2,3,1,0:T(1,128)S(1)} %bitcast.132), kind=kOutput, calls=%fused_computation.100 | convolution fusion | flops 6291456 | bytes 2117632 | tf_op jit(solution)/shard_map/while/body/eval_jaxpr/dkij,dkj->di/dot_general | solution.py:60
  109.6 3.2 %copy.64 = f32[16,8,16,256]{3,2,1,0:T(8,128)} copy(f32[16,8,16,256]{3,2,0,1:T(8,128)} %bitcast.16) | data formatting | bytes 4194304 | tf_op jit(solution)/shard_map/all_to_all | solution.py:144
  (89 shorter events, 5.7 us)
Async XLA Ops:
  0.6 63.8 %copy-start = (f32[8,128,128]{2,1,0:T(8,128)S(1)}, f32[8,128,128]{2,1,0:T(8,128)}, u32[]{:S(2)}) copy-start(f32[8,128,128]{2,1,0:T(8,128)} %param.23) | copy-start | bytes 1572868
  3.9 5.1 %copy-start.1 = (f32[16,128,256]{2,1,0:T(8,128)S(1)}, f32[16,128,256]{2,1,0:T(8,128)}, u32[]{:S(2)}) copy-start(f32[16,128,256]{2,1,0:T(8,128)} %param.21) | copy-start | bytes 6291460
  5.6 6.0 %collective-permute-start = (f32[16,128,1]{1,0,2:T(8,128)S(1)}, f32[16,128,1]{1,0,2:T(8,128)S(1)}, u32[]{:S(2)}, u32[]{:S(2)}) collective-permute-start(f32[16,128,1]{1,0,2:T(8,128)S(1)} %copy.76), channel_id=1, source_target_pairs={{0,8},{8,16},{16,24},{24,32},{32,40},{40,48},{48,56},{56,64},{64,7... | collective-permute-start | bytes 24584 | tf_op jit(solution)/shard_map/ppermute | solution.py:22
  9.0 5.2 %collective-permute-start.1 = (f32[16,128,1]{1,0,2:T(8,128)S(1)}, f32[16,128,1]{1,0,2:T(8,128)S(1)}, u32[]{:S(2)}, u32[]{:S(2)}) collective-permute-start(f32[16,128,1]{1,0,2:T(8,128)S(1)} %copy.77), channel_id=1, source_target_pairs={{8,0},{16,8},{24,16},{32,24},{40,32},{48,40},{56,48},{64,56},{72,6... | collective-permute-start | bytes 24584 | tf_op jit(solution)/shard_map/ppermute | solution.py:24
  11.6 4.1 %copy-start.2 = (f32[16,128,256]{2,0,1:T(8,128)S(1)}, f32[16,128,256]{2,0,1:T(8,128)}, u32[]{:S(2)}) copy-start(f32[16,128,256]{2,0,1:T(8,128)} %copy.56) | copy-start | bytes 6291460
  20.9 7.6 %copy-start.3 = (f32[32,8,128]{2,1,0:T(8,128)S(1)}, f32[32,8,128]{2,1,0:T(8,128)}, u32[]{:S(2)}) copy-start(f32[32,8,128]{2,1,0:T(8,128)} %param.25) | copy-start | bytes 393220
  20.9 7.6 %copy-start.5 = (s32[8,128]{1,0:T(8,128)S(1)}, s32[8,128]{1,0:T(8,128)}, u32[]{:S(2)}) copy-start(s32[8,128]{1,0:T(8,128)} %param.28) | copy-start | bytes 12292
  20.9 14.5 %copy-start.8 = (s32[128,2,4]{0,2,1:T(4,128)S(1)}, s32[128,2,4]{0,2,1:T(4,128)}, u32[]{:S(2)}) copy-start(s32[128,2,4]{0,2,1:T(4,128)} %param.32) | copy-start | bytes 12292
  20.9 14.5 %copy-start.9 = (s32[128,2,4]{0,2,1:T(4,128)S(1)}, s32[128,2,4]{0,2,1:T(4,128)}, u32[]{:S(2)}) copy-start(s32[128,2,4]{0,2,1:T(4,128)} %param.33) | copy-start | bytes 12292
  20.9 14.7 %copy-start.10 = (s32[8,1,4]{0,2,1:T(4,128)S(1)}, s32[8,1,4]{0,2,1:T(4,128)}, u32[]{:S(2)}) copy-start(s32[8,1,4]{0,2,1:T(4,128)} %param.30) | copy-start | bytes 388
  20.9 14.9 %copy-start.11 = (s32[8,1,4]{0,2,1:T(4,128)S(1)}, s32[8,1,4]{0,2,1:T(4,128)}, u32[]{:S(2)}) copy-start(s32[8,1,4]{0,2,1:T(4,128)} %param.31) | copy-start | bytes 388
  20.9 40.6 %all-to-all-start = ((f32[16,128,256]{2,0,1:T(8,128)}), f32[16,128,256]{2,0,1:T(8,128)S(1)}, u32[]{:S(2)}, u32[]{:S(2)}) async-start(f32[16,128,256]{2,0,1:T(8,128)} %fusion.2), calls=%async_computation | async-start | bytes 4194304 | tf_op jit(solution)/shard_map/all_to_all | solution.py:138
  28.5 30.6 %collective-permute-start.6 = (f32[8,128]{1,0:T(8,128)S(1)}, f32[8,128]{1,0:T(8,128)S(1)}, u32[]{:S(2)}, u32[]{:S(2)}) collective-permute-start(f32[8,128]{1,0:T(8,128)S(1)} %bitcast_multiply_fusion), channel_id=1, source_target_pairs={{0,8},{8,16},{16,24},{24,32},{32,40},{40,48},{48,56},{56,64},{64,7... | collective-permute-start | bytes 12296 | tf_op jit(solution)/shard_map/ppermute | solution.py:12
  30.9 29.0 %collective-permute-start.5 = (f32[32,1,128]{2,1,0:T(1,128)S(1)}, f32[32,1,128]{2,1,0:T(1,128)S(1)}, u32[]{:S(2)}, u32[]{:S(2)}) collective-permute-start(f32[32,1,128]{2,1,0:T(1,128)S(1)} %slice.129), channel_id=1, source_target_pairs={{0,1},{1,2},{2,3},{3,4},{4,5},{5,6},{6,7},{7,0},{8,9},{9,10},{10,1... | collective-permute-start | bytes 49160 | tf_op jit(solution)/shard_map/ppermute | solution.py:39
  34.9 62.1 %collective-permute-start.2 = (f32[32,8,1]{2,1,0:T(8,128)S(1)}, f32[32,8,1]{2,1,0:T(8,128)S(1)}, u32[]{:S(2)}, u32[]{:S(2)}) collective-permute-start(f32[32,8,1]{2,1,0:T(8,128)S(1)} %get-tuple-element.134), channel_id=1, source_target_pairs={{0,8},{8,16},{16,24},{24,32},{32,40},{40,48},{48,56},{56,64},{64,7... | collective-permute-start | bytes 3080 | tf_op jit(solution)/shard_map/ppermute | solution.py:39
  35.0 62.1 %collective-permute-start.3 = (f32[32,8,1]{2,1,0:T(8,128)S(1)}, f32[32,8,1]{2,1,0:T(8,128)S(1)}, u32[]{:S(2)}, u32[]{:S(2)}) collective-permute-start(f32[32,8,1]{2,1,0:T(8,128)S(1)} %get-tuple-element.135), channel_id=1, source_target_pairs={{8,0},{16,8},{24,16},{32,24},{40,32},{48,40},{56,48},{64,56},{72,6... | collective-permute-start | bytes 3080 | tf_op jit(solution)/shard_map/ppermute | solution.py:40
  59.9 37.1 %collective-permute-start.4 = (f32[32,1,128]{2,1,0:T(1,128)S(1)}, f32[32,1,128]{2,1,0:T(1,128)S(1)}, u32[]{:S(2)}, u32[]{:S(2)}) collective-permute-start(f32[32,1,128]{2,1,0:T(1,128)S(1)} %get-tuple-element.132), channel_id=1, source_target_pairs={{1,0},{2,1},{3,2},{4,3},{5,4},{6,5},{7,6},{0,7},{9,8},{10,9},{11,1... | collective-permute-start | bytes 49160 | tf_op jit(solution)/shard_map/ppermute | solution.py:40
  69.9 39.7 %all-to-all-start.1 = ((f32[128,16,256]{2,1,0:T(8,128)}), f32[128,16,256]{2,1,0:T(8,128)}, u32[]{:S(2)}, u32[]{:S(2)}) async-start(f32[128,16,256]{2,1,0:T(8,128)} %copy.63), calls=%async_computation.1 | async-start | bytes 4194304 | tf_op jit(solution)/shard_map/all_to_all | solution.py:144
  97.0 3.1 %copy-start.7 = (f32[8,128]{1,0:T(8,128)S(1)}, f32[8,128]{1,0:T(8,128)}, u32[]{:S(2)}) copy-start(f32[8,128]{1,0:T(8,128)} %param.26) | copy-start | bytes 12292
  98.5 10.1 %copy-start.6 = (f32[32,32]{1,0:T(8,128)S(1)}, f32[32,32]{1,0:T(8,128)}, u32[]{:S(2)}) copy-start(f32[32,32]{1,0:T(8,128)} %param.27) | copy-start | bytes 12292
  99.3 13.4 %copy-start.4 = (f32[16,256]{1,0:T(8,128)}, f32[16,256]{1,0:T(8,128)S(1)}, u32[]{:S(2)}) copy-start(f32[16,256]{1,0:T(8,128)S(1)} %subtract_multiply_fusion) | copy-start | bytes 49156
  99.3 5.3 %collective-permute-start.7 = (f32[16,256]{1,0:T(8,128)S(1)}, f32[16,256]{1,0:T(8,128)S(1)}, u32[]{:S(2)}, u32[]{:S(2)}) collective-permute-start(f32[16,256]{1,0:T(8,128)S(1)} %subtract_multiply_fusion), channel_id=1, source_target_pairs={{0,120},{8,0},{16,8},{24,16},{32,24},{40,32},{48,40},{56,48},{64,5... | collective-permute-start | bytes 49160 | tf_op jit(solution)/shard_map/ppermute | solution.py:12
where the time goes:
time: 114 us; the launch traced here: 113 us
  local copies, waits for them, and re-layouts  39.5 us (35%)
  starting transfers between devices  23.1 us (20%)
  blocking collectives  18.4 us (16%)
  matrix products  17.9 us (16%)
  other arithmetic  6.48 us (6%)
  waiting for transfers between devices  6.4 us (6%)
    all_gather x1, blocking collectives, per_device(): whole_top = lax.all_gather(top_row, 'lon', axis=1, tiled=True)  18.4 us
    gather x3, local copies, waits for them, and re-layouts, one_group(): mats = weights[wgt_part]  14.2 us
    dot_general x3, matrix products, one_group(): jnp.einsum('dkij,dkj->di', mats, picked, precision=lax.Precision.HIGHEST)  14.1 us
    unnamed x29, local copies, waits for them, and re-layouts  8.17 us
    all_to_all x1, starting transfers between devices, per_device(): lax.all_to_all(advected, 'sub', split_axis=1, concat_axis=0, tiled=True)  7.51 us
    sub x1, other arithmetic, per_device(): atm_tracer - jnp.maximum(courant, 0.0) * (atm_tracer - west)  5.27 us
    all_to_all x1, starting transfers between devices, per_device(): lax.all_to_all(result, 'sub', split_axis=0, concat_axis=1, tiled=True)  4.53 us
    ppermute x2, waiting for transfers between devices, passed_along(): return lax.ppermute(value, axis, pairs)  4.37 us
  transfers between devices with their start and end apart: 10, of which 3 were waited for; matrix products, arithmetic and copies ran while one was open for 44% of the time, Pallas kernels for 0%

commit v1 on v0

v1 whole, which is shorter than its diff:
```python
import functools

import jax
import jax.numpy as jnp
from jax import lax
from jax.experimental import pallas as pl
from jax.experimental.pallas import tpu as pltpu
from jax.sharding import PartitionSpec as P

F32 = jnp.float32
BF16 = jnp.bfloat16
VMEM = pl.BlockSpec(memory_space=pltpu.VMEM)
SMEM = pl.BlockSpec(memory_space=pltpu.SMEM)
ANY = pl.BlockSpec(memory_space=pl.ANY)
MIB = 1 << 20
LANES = 128


def kernel_call(body, out_shape, in_specs, out_specs, scratch=(), flops=0, moved=0, limit=16, name=None):
    return pl.pallas_call(
        body,
        out_shape=out_shape,
        in_specs=in_specs,
        out_specs=out_specs,
        scratch_shapes=list(scratch),
        compiler_params=pltpu.CompilerParams(vmem_limit_bytes=limit * MIB),
        cost_estimate=pl.CostEstimate(flops=flops, bytes_accessed=moved, transcendentals=0),
        name=name,
    )


def shape(*dims):
    return jax.ShapeDtypeStruct(dims, F32)


def split(value):
    high = value.astype(BF16)
    return high, (value - high.astype(F32)).astype(BF16)


def edges_kernel(atm, ocean, mask, east_msg, west_msg):
    levels, rows, cells = atm.shape
    lane = lax.broadcasted_iota(jnp.int32, (LANES, LANES), 1)

    def gathered(atm_col, ocean_col):
        total = jnp.zeros((LANES, LANES), F32)
        for level in range(levels):
            total = jnp.where(lane == level, atm[level, :, atm_col : atm_col + 1], total)
        for part in range(2):
            column = ocean[part * LANES : (part + 1) * LANES, ocean_col : ocean_col + 1]
            total = jnp.where(lane == levels + part, column, total)
        return total.T

    east_msg[:24, :] = gathered(cells - 1, LANES - 1)[:24, :]
    east_msg[24:, :] = mask[...].astype(F32) * ocean[:8, :]
    west_msg[...] = gathered(0, 0)[:24, :]


def advect_kernel(atm, courant, from_west, from_east, out, west_cols, east_cols):
    levels, _, cells = atm.shape
    band = out.shape[1]
    west_cols[...] = from_west[...].T
    east_cols[...] = from_east[...].T
    lane = lax.broadcasted_iota(jnp.int32, (band, cells), 1)

    @pl.loop(0, out.shape[0])
    def _(dest):
        rows = pl.ds(pl.multiple_of(dest * band, band), band)
        made = []
        for level in range(levels):
            here = atm[level, rows, :]
            speed = courant[level, rows, :]
            west = jnp.where(lane == 0, west_cols[rows, level : level + 1], pltpu.roll(here, 1, 1))
            east = jnp.where(
                lane == cells - 1, east_cols[rows, level : level + 1], pltpu.roll(here, cells - 1, 1)
            )
            made.append(
                here
                - jnp.maximum(speed, 0.0) * (here - west)
                - jnp.minimum(speed, 0.0) * (east - here)
            )
        out[dest] = jnp.swapaxes(jnp.stack(made), 0, 1)


def mat_vec(ids, first, count, source, weights):
    total = jnp.zeros(weights.shape[1:], F32)
    half = ids.shape[0] // 2
    for k in range(count):
        block = source[pl.ds(ids[first + k], 1), :]
        total = total + weights[ids[half + first + k]] * block
    return jnp.sum(total.T, axis=0, keepdims=True)


def sst_kernel(width, ids, from_west, ocean, mask, weights, sst, window, halves):
    window[:8, :] = from_west[24:32, :]
    window[8:, :] = mask[...].astype(F32) * ocean[:8, :]
    rows = sst.shape[0]

    @pl.loop(0, rows)
    def _(row):
        for g in range(2):
            halves[g, pl.ds(row, 1), :] = mat_vec(ids, (row * 2 + g) * width, width, window, weights)

    for g in range(2):
        sst[:, g * LANES : (g + 1) * LANES] = halves[g]


def solve_kernel(place, columns, inverse, factor, sst, out, flux, held):
    sub = place[0]
    groups, band, depth, cells = columns.shape
    levels = groups * depth
    high, low = split(inverse[sub])
    twice = jnp.concatenate([high, high], axis=1)

    @pl.loop(0, band)
    def _(row):
        here = columns[:, row].reshape(levels, cells)
        x_high, x_low = split(here)
        made = jnp.dot(
            twice, jnp.concatenate([x_high, x_low], axis=0), preferred_element_type=F32
        ) + jnp.dot(low, x_high, preferred_element_type=F32)
        held[row] = made

    for group in range(groups):
        out[group] = jnp.swapaxes(held[:, group * depth : (group + 1) * depth, :], 0, 1)
    rows = pl.ds(pl.multiple_of(sub * band, band), band)
    flux[...] = factor[rows, :] * (sst[...] - out[groups - 1, depth - 1])


def ocean_kernel(
    width, n_sub, place, ids, flux, from_east_flux, temp_in, diffusivity, mask_in, inverse, weights,
    from_west, from_east, even_rows, odd_rows, folded, out, window, surface,
):
    sub = place[0]
    band = flux.shape[0]
    levels, rows, cells = temp_in.shape
    for side, source in enumerate((flux, from_east_flux)):
        for g in range(2):
            at = (side * 2 + g) * band
            window[at : at + band, :] = source[:, g * LANES : (g + 1) * LANES]

    @pl.loop(0, rows)
    def _(row):
        surface[pl.ds(row, 1), :] = mat_vec(ids, row * width, width, window, weights)

    temp = temp_in[...]
    mask = mask_in[...].astype(F32)
    even = lax.rem(sub, 2) == 0
    own_south = temp[:, 0, :]
    south_row = jnp.where(even, jnp.where(sub == 0, own_south, odd_rows[...]), even_rows[...])
    north_row = jnp.where(
        even, even_rows[...], jnp.where(sub == n_sub - 1, folded[...], odd_rows[...])
    )
    south = jnp.concatenate([south_row[:, None, :], temp[:, :-1, :]], axis=1)
    north = jnp.concatenate([temp[:, 1:, :], north_row[:, None, :]], axis=1)

    def column(message):
        turned = message[16:24, :].T
        return jnp.concatenate([turned[:, 0:1], turned[:, 1:2]], axis=0)

    flat = temp.reshape(levels * rows, cells)
    lane = lax.broadcasted_iota(jnp.int32, flat.shape, 1)
    west = jnp.where(lane == 0, column(from_west), pltpu.roll(flat, 1, 1))
    east = jnp.where(lane == cells - 1, column(from_east), pltpu.roll(flat, cells - 1, 1))
    lap = (west + east).reshape(temp.shape) + north + south - 4.0 * temp
    stepped = mask[None] * (temp + diffusivity[...][None] * lap)
    heated = stepped[0] + mask * surface[...]
    turned = jnp.swapaxes(stepped, 0, 1)
    level = lax.broadcasted_iota(jnp.int32, (levels, cells), 0)
    high, low = split(inverse[...])
    made = []
    for row in range(rows):
        here = jnp.where(level == 0, heated[row : row + 1, :], turned[row])
        x_high, x_low = split(here)
        made.append(
            jnp.dot(high, x_high, preferred_element_type=F32)
            + jnp.dot(high, x_low, preferred_element_type=F32)
            + jnp.dot(low, x_high, preferred_element_type=F32)
        )
    out[...] = jnp.swapaxes(jnp.stack(made), 0, 1)


def place_kernel(parts, out, sems):
    band = parts.shape[2]
    copies = [
        pltpu.make_async_copy(parts.at[b], out.at[:, pl.ds(b * band, band), :], sems.at[b])
        for b in range(parts.shape[0])
    ]
    for copy in copies:
        copy.start()
    for copy in copies:
        copy.wait()


def pair_exchanges(n_lon, n_sub):
    first, second = [], []
    for lon in range(n_lon):
        at = lon * n_sub
        for south in range(n_sub - 1):
            pairs = first if south % 2 == 0 else second
            pairs += [(at + south, at + south + 1), (at + south + 1, at + south)]
        second.append((at + n_sub - 1, (n_lon - 1 - lon) * n_sub + n_sub - 1))
    return first, second


def per_device(
    atm_tracer,
    courant,
    column_inverse,
    heat_exchange_factor,
    ocean_temp,
    diffusivity,
    ocean_inverse,
    land_mask,
    weights,
    a2o_src,
    a2o_wgt,
    o2a_src,
    o2a_wgt,
):
    lon_index = lax.axis_index("lon")
    sub_index = lax.axis_index("sub")
    n_lon = lax.axis_size("lon")
    n_sub = lax.axis_size("sub")
    lev_dev, alat, alon_dev = atm_tracer.shape
    groups = alon_dev // LANES
    ngroups = groups * n_lon
    olev, olat_dev, olon_dev = ocean_temp.shape
    aband = alat // n_sub
    width = o2a_src.shape[2]
    ocean_flat = ocean_temp.reshape(olev * olat_dev, olon_dev)
    place = jnp.reshape(sub_index, (1,))

    east_msg, west_msg = kernel_call(
        edges_kernel, (shape(32, LANES), shape(24, LANES)), [VMEM] * 3, (VMEM, VMEM),
        flops=2 * MIB, moved=2 * MIB, name="edges",
    )(atm_tracer, ocean_flat, land_mask)
    up = [(i, (i + 1) % n_lon) for i in range(n_lon)]
    down = [(b, a) for a, b in up]
    from_west = lax.ppermute(east_msg, "lon", up)
    from_east = lax.ppermute(west_msg, "lon", down)

    advected = kernel_call(
        advect_kernel, shape(n_sub, aband, lev_dev, alon_dev), [VMEM] * 4, VMEM,
        scratch=[pltpu.VMEM((LANES, 32), F32), pltpu.VMEM((LANES, 24), F32)],
        flops=10 * MIB, moved=6 * MIB, name="advect",
    )(atm_tracer, courant, from_west, from_east)
    columns = lax.all_to_all(advected, "sub", split_axis=0, concat_axis=0, tiled=True)

    even = lax.rem(sub_index, 2) == 0
    top_row, low_row = ocean_temp[:, olat_dev - 1, :], ocean_temp[:, 0, :]
    first, second = pair_exchanges(n_lon, n_sub)
    even_rows = lax.ppermute(jnp.where(even, top_row, low_row), ("lon", "sub"), first)
    odd_rows = lax.ppermute(jnp.where(even, low_row, top_row), ("lon", "sub"), second)
    folded = jnp.flip(odd_rows, axis=1)

    band_src = lax.dynamic_slice_in_dim(o2a_src, sub_index * aband, aband, 0).reshape(-1)
    band_wgt = lax.dynamic_slice_in_dim(o2a_wgt, sub_index * aband, aband, 0).reshape(-1)
    tile = jnp.remainder(band_src % n_lon - lon_index + 1, n_lon)
    sea_ids = tile * olat_dev + band_src // n_lon - sub_index * olat_dev
    sst = kernel_call(
        functools.partial(sst_kernel, width), shape(aband, alon_dev), [SMEM] + [VMEM] * 4, VMEM,
        scratch=[pltpu.VMEM((2 * olat_dev, LANES), F32), pltpu.VMEM((groups, aband, LANES), F32)],
        flops=8 * MIB, moved=8 * MIB, name="sst",
    )(jnp.concatenate([sea_ids, band_wgt]), from_west, ocean_flat, land_mask, weights)

    solved, flux_band = kernel_call(
        solve_kernel, (shape(n_sub, lev_dev, aband, alon_dev), shape(aband, alon_dev)),
        [SMEM] + [VMEM] * 4, (VMEM, VMEM),
        scratch=[pltpu.VMEM((aband, lev_dev * n_sub, alon_dev), F32)],
        flops=400 * MIB, moved=4 * MIB, name="solve",
    )(place, columns, column_inverse, heat_exchange_factor, sst)
    parts = lax.all_to_all(solved, "sub", split_axis=0, concat_axis=0, tiled=True)

    east_flux = lax.ppermute(flux_band, "lon", down)
    src = a2o_src.reshape(-1)
    group = jnp.remainder(src % ngroups - lon_index * groups, ngroups)
    flux_ids = group * aband + src // ngroups - sub_index * aband
    ocean_new = kernel_call(
        functools.partial(ocean_kernel, width, n_sub), shape(olev, olat_dev, olon_dev),
        [SMEM] * 2 + [VMEM] * 12, VMEM,
        scratch=[pltpu.VMEM((4 * aband, LANES), F32), pltpu.VMEM((olat_dev, LANES), F32)],
        flops=8 * MIB, moved=8 * MIB, name="ocean",
    )(
        place, jnp.concatenate([flux_ids, a2o_wgt.reshape(-1)]), flux_band, east_flux, ocean_temp,
        diffusivity, land_mask, ocean_inverse, weights, from_west, from_east, even_rows, odd_rows, folded,
    )

    returned = kernel_call(
        place_kernel, shape(lev_dev, alat, alon_dev), [VMEM], ANY,
        scratch=[pltpu.SemaphoreType.DMA((n_sub,))], moved=4 * MIB, name="place",
    )(parts)
    return returned, ocean_new, flux_band


def solution(mesh):
    return jax.shard_map(
        per_device,
        mesh=mesh,
        in_specs=(
            P("sub", None, "lon"),
            P("sub", None, "lon"),
            P(),
            P(None, "lon"),
            P(None, "sub", "lon"),
            P("sub", "lon"),
            P(),
            P("sub", "lon"),
            P(),
            P("sub", "lon", None),
            P("sub", "lon", None),
            P(None, "lon", None),
            P(None, "lon", None),
        ),
        out_specs=(P("sub", None, "lon"), P(None, "sub", "lon"), P("sub", "lon")),
        check_vma=False,
    )
```

time: 114 us -> 93.8 us (0.82)
  waiting for transfers between devices: 6.4 us -> 49.8 us
  local copies, waits for them, and re-layouts: 39.5 us -> 11.1 us
  blocking collectives: 18.4 us -> 0 us
  matrix products: 17.9 us -> 0 us
  Pallas kernels: 0 us -> 14 us
  other arithmetic: 6.48 us -> 0.14 us
  starting transfers between devices: 23.1 us -> 17.1 us
    ppermute x8 -> x5, waiting for transfers between devices: 6.4 us -> 28.5 us  [the longest x1 23.3 us: per_device(): lax.ppermute(jnp.where(even, top_row, low_row), ('lon', 'sub'), first)]
    all_to_all x2, waiting for transfers between devices: 0.01 us -> 21.3 us  [the longest x1 21.3 us: per_device(): lax.all_to_all(advected, 'sub', split_axis=0, concat_axis=0, tiled=True)]
    all_gather x1 -> x0, blocking collectives: 18.4 us -> none  [per_device(): whole_top = lax.all_gather(top_row, 'lon', axis=1, tiled=True)]
    dot_general x5 -> x0, matrix products: 17.9 us -> none  [the longest x3 14.1 us: one_group(): jnp.einsum('dkij,dkj->di', mats, picked, precision=lax.Precision.HIGHEST)]
    gather x6 -> x0, local copies, waits for them, and re-layouts: 15.9 us -> none  [the longest x3 14.2 us: one_group(): mats = weights[wgt_part]]
    pallas_call x0 -> x6, Pallas kernels: none -> 14 us  [the longest x1 3.91 us: per_device(): kernel_call(solve_kernel, (shape(n_sub, lev_dev, aband, alon_dev), shape(...]
    ppermute x8 -> x5, starting transfers between devices: 11 us -> 5.8 us  [the longest x1 2.93 us: per_device(): lax.ppermute(jnp.where(even, top_row, low_row), ('lon', 'sub'), first)]
    sub x1 -> x2, other arithmetic: 5.27 us -> 0.05 us  [the longest x1 0.02 us: per_device(): flux_ids = group * aband + src // ngroups - sub_index * aband]
  transfers between devices with their start and end apart: 10 -> 7, of which waited for: 3 -> 3; matrix products, arithmetic and copies ran while one was open for 44% -> 1% of each run, Pallas kernels for 0% -> 6%
where the time goes in v1:
time: 93.8 us; the launch traced here: 93 us
  waiting for transfers between devices  49.8 us (53%)
  starting transfers between devices  17.1 us (18%)
  Pallas kernels  14 us (15%)
  local copies, waits for them, and re-layouts  11.1 us (12%)
    ppermute x1, waiting for transfers between devices, per_device(): lax.ppermute(jnp.where(even, top_row, low_row), ('lon', 'sub'), first)  23.3 us
    all_to_all x1, waiting for transfers between devices, per_device(): lax.all_to_all(advected, 'sub', split_axis=0, concat_axis=0, tiled=True)  21.3 us
    unnamed x40, local copies, waits for them, and re-layouts  10.4 us
    all_to_all x1, starting transfers between devices, per_device(): lax.all_to_all(advected, 'sub', split_axis=0, concat_axis=0, tiled=True)  7.51 us
    ppermute x1, waiting for transfers between devices, per_device(): from_east = lax.ppermute(west_msg, 'lon', down)  5.23 us
    pallas_call x1, Pallas kernels, per_device(): kernel_call(solve_kernel, (shape(n_sub, lev_dev, aband, alon_dev), shape(...  3.91 us
    all_to_all x1, starting transfers between devices, per_device(): lax.all_to_all(solved, 'sub', split_axis=0, concat_axis=0, tiled=True)  3.75 us
    ppermute x1, starting transfers between devices, per_device(): lax.ppermute(jnp.where(even, top_row, low_row), ('lon', 'sub'), first)  2.93 us
  transfers between devices with their start and end apart: 7, of which 3 were waited for; matrix products, arithmetic and copies ran while one was open for 1% of the time, Pallas kernels for 6%

profile of v1, /device:TPU:7, one launch (start us, length us, event | category | flops | bytes accessed | tf_op | source)
XLA Modules:
  0.0 93.0 jit_solution(1894456346899591760)
XLA Ops:
  0.6 1.6 %copy-done.2 = f32[16,128,256]{2,1,0:T(8,128)S(1)} copy-done((f32[16,128,256]{2,1,0:T(8,128)S(1)}, f32[16,128,256]{2,1,0:T(8,128)}, u32[]{:S(2)}) %copy-start.2) | copy-done | bytes 2097176
  2.2 0.9 copy-done.6
  3.1 0.7 copy-done.10
  3.8 0.8 edges.1
  4.6 1.8 %collective-permute-start = (f32[32,128]{1,0:T(8,128)S(1)}, f32[32,128]{1,0:T(8,128)S(1)}, u32[]{:S(2)}, u32[]{:S(2)}) collective-permute-start(f32[32,128]{1,0:T(8,128)S(1)} %get-tuple-element.7), channel_id=1, source_target_pairs={{0,8},{8,16},{16,24},{24,32},{32,40},{40,48},{48,56},{56,64},{64,7... | collective-permute-start | bytes 49160 | tf_op jit(solution)/shard_map/ppermute | solution.py:240
  6.4 5.2 %collective-permute-done.1.from_east = f32[24,128]{1,0:T(8,128)S(1)} collective-permute-done((f32[24,128]{1,0:T(8,128)S(1)}, f32[24,128]{1,0:T(8,128)S(1)}, u32[]{:S(2)}, u32[]{:S(2)}) %collective-permute-start.1) | collective-permute-done | bytes 12320 | tf_op jit(solution)/shard_map/ppermute | solution.py:241
  11.6 2.8 %advect.1 = f32[8,16,16,256]{3,2,1,0:T(8,128)S(1)} custom-call(f32[16,128,256]{2,1,0:T(8,128)S(1)} %copy-done.2, f32[16,128,256]{2,1,0:T(8,128)S(1)} %copy-done.4, f32[32,128]{1,0:T(8,128)S(1)} %collective-permute-done.from_west, f32[24,128]{1,0:T(8,128)S(1)} %collective-permute-done.1.from_east), custom_call_target="tpu_custom_call" | custom-call | flops 10485760 | bytes 6291456 | tf_op jit(solution)/shard_map/advect/pallas_call | solution.py:243
  14.4 1.3 %copy-done.3 = f32[8,16,16,256]{3,2,1,0:T(8,128)} copy-done((f32[8,16,16,256]{3,2,1,0:T(8,128)}, f32[8,16,16,256]{3,2,1,0:T(8,128)S(1)}, u32[]{:S(2)}) %copy-start.3) | copy-done | bytes 2097176
  15.7 7.5 %all-to-all-start = ((f32[8,16,16,256]{3,2,1,0:T(8,128)}), f32[8,16,16,256]{3,2,1,0:T(8,128)S(1)}, u32[]{:S(2)}, u32[]{:S(2)}) async-start(f32[8,16,16,256]{3,2,1,0:T(8,128)} %copy-done.3), calls=%async_computation | async-start | bytes 4194304 | tf_op jit(solution)/shard_map/all_to_all | solution.py:248
  23.3 0.1 constant_dynamic-slice_fusion
  23.4 0.1 copy.23
  23.5 0.1 reshape.31
  23.6 0.1 copy.22
  23.7 0.1 reshape.30
  23.9 2.2 %copy-done = f32[64,128,128]{2,1,0:T(8,128)S(1)} copy-done((f32[64,128,128]{2,1,0:T(8,128)S(1)}, f32[64,128,128]{2,1,0:T(8,128)}, u32[]{:S(2)}) %copy-start) | copy-done | bytes 4194328
  26.0 2.5 %sst.1 = f32[16,256]{1,0:T(8,128)S(1)} custom-call(s32[256]{0:T(256)S(1)} %pad_add_fusion.ids, f32[32,128]{1,0:T(8,128)S(1)} %collective-permute-done.from_west, f32[256,128]{1,0:T(8,128)S(1)} %bitcast.13, s32[8,128]{1,0:T(8,128)S(1)} %copy-done.11, f32[64,128,128]{2,1,0:T(8,128)S(1)} %copy-done), custom_call_target="tpu_custom_call" | custom-call | flops 8388608 | bytes 8388608 | tf_op jit(solution)/shard_map/sst/pallas_call | solution.py:261
  28.6 21.3 %all-to-all-done.columns = f32[8,16,16,256]{3,2,1,0:T(8,128)S(1)} async-done(((f32[8,16,16,256]{3,2,1,0:T(8,128)}), f32[8,16,16,256]{3,2,1,0:T(8,128)S(1)}, u32[]{:S(2)}, u32[]{:S(2)}) %all-to-all-start) | async-done | bytes 2097184 | tf_op jit(solution)/shard_map/all_to_all | solution.py:248
  49.9 3.9 %solve.1 = (f32[8,16,16,256]{3,2,1,0:T(8,128)S(1)}, f32[16,256]{1,0:T(8,128)}) custom-call(s32[1]{0:T(128)} %bitcast.place, f32[8,16,16,256]{3,2,1,0:T(8,128)S(1)} %all-to-all-done.columns, f32[8,128,128]{2,1,0:T(8,128)S(1)} %copy-done.8, f32[128,256]{1,0:T(8,128)S(1)} %copy-done.9, f32[16,256]{1,0:T(8,128)S(1)} %sst.1), custom_call_target="tpu_custom_call" | custom-call | flops 419430400 | bytes 4194304 | tf_op jit(solution)/shard_map/solve/pallas_call | solution.py:267
  53.8 1.3 %copy-done.5 = f32[8,16,16,256]{3,2,1,0:T(8,128)} copy-done((f32[8,16,16,256]{3,2,1,0:T(8,128)}, f32[8,16,16,256]{3,2,1,0:T(8,128)S(1)}, u32[]{:S(2)}) %copy-start.5) | copy-done | bytes 2097176
  55.1 3.7 %all-to-all-start.1 = ((f32[8,16,16,256]{3,2,1,0:T(8,128)}), f32[8,16,16,256]{3,2,1,0:T(8,128)S(1)}, u32[]{:S(2)}, u32[]{:S(2)}) async-start(f32[8,16,16,256]{3,2,1,0:T(8,128)} %copy-done.5), calls=%async_computation.1 | async-start | bytes 4194304 | tf_op jit(solution)/shard_map/all_to_all | solution.py:273
  58.9 2.9 %collective-permute-start.3 = (f32[32,128]{1,0:T(8,128)S(1)}, f32[32,128]{1,0:T(8,128)S(1)}, u32[]{:S(2)}, u32[]{:S(2)}) collective-permute-start(f32[32,128]{1,0:T(8,128)S(1)} %get-tuple-element.14), channel_id=1, source_target_pairs={{0,1},{1,0},{2,3},{3,2},{4,5},{5,4},{6,7},{7,6},{8,9},{9,8},{10,11... | collective-permute-start | bytes 49160 | tf_op jit(solution)/shard_map/ppermute | solution.py:253
  61.9 0.7 collective-permute-start.4
  62.5 0.1 copy.25
  62.6 0.1 reshape.33
  62.7 0.1 copy.24
  62.8 0.1 reshape.32
  62.9 0.4 collective-permute-start.2
  63.3 0.1 pad_add_fusion.1.ids
  63.5 23.3 %collective-permute-done.3.even_rows = f32[32,128]{1,0:T(8,128)S(1)} collective-permute-done((f32[32,128]{1,0:T(8,128)S(1)}, f32[32,128]{1,0:T(8,128)S(1)}, u32[]{:S(2)}, u32[]{:S(2)}) %collective-permute-start.3) | collective-permute-done | bytes 16416 | tf_op jit(solution)/shard_map/ppermute | solution.py:253
  86.8 2.2 %copy-done.1 = f32[64,128,128]{2,1,0:T(8,128)S(1)} copy-done((f32[64,128,128]{2,1,0:T(8,128)S(1)}, f32[64,128,128]{2,1,0:T(8,128)}, u32[]{:S(2)}) %copy-start.1) | copy-done | bytes 4194328
  89.0 2.7 %ocean.1 = f32[32,8,128]{2,1,0:T(8,128)} custom-call(s32[1]{0:T(128)} %bitcast.place, s32[64]{0:T(128)S(1)} %pad_add_fusion.1.ids, f32[16,256]{1,0:T(8,128)S(1)} %copy-done.13, f32[16,256]{1,0:T(8,128)S(1)} %collective-permute-done.2.from_east_flux, f32[32,8,128]{2,1,0:T(8,128)S(1)} %copy-done.7, f32[8,128]{1,0:T(8,128)S(1)} %copy-done.14, ...), custom_call_target="tpu_custom_call" | custom-call | flops 8388608 | bytes 8388608 | tf_op jit(solution)/shard_map/ocean/pallas_call | solution.py:279
  91.6 1.4 %place.1 = f32[16,128,256]{2,1,0:T(8,128)} custom-call(f32[8,16,16,256]{3,2,1,0:T(8,128)S(1)} %all-to-all-done.1.parts), custom_call_target="tpu_custom_call" | custom-call | bytes 4194304 | tf_op jit(solution)/shard_map/place/pallas_call | solution.py:289
  (42 shorter events, 0.2 us)
Async XLA Ops:
  0.6 1.6 %copy-start.2 = (f32[16,128,256]{2,1,0:T(8,128)S(1)}, f32[16,128,256]{2,1,0:T(8,128)}, u32[]{:S(2)}) copy-start(f32[16,128,256]{2,1,0:T(8,128)} %atm.3) | copy-start | bytes 6291460
  2.2 0.9 copy-start.6
  3.1 0.7 copy-start.10
  3.8 7.8 %copy-start.4 = (f32[16,128,256]{2,1,0:T(8,128)S(1)}, f32[16,128,256]{2,1,0:T(8,128)}, u32[]{:S(2)}) copy-start(f32[16,128,256]{2,1,0:T(8,128)} %courant.1) | copy-start | bytes 6291460
  4.6 7.0 %collective-permute-start = (f32[32,128]{1,0:T(8,128)S(1)}, f32[32,128]{1,0:T(8,128)S(1)}, u32[]{:S(2)}, u32[]{:S(2)}) collective-permute-start(f32[32,128]{1,0:T(8,128)S(1)} %get-tuple-element.7), channel_id=1, source_target_pairs={{0,8},{8,16},{16,24},{24,32},{32,40},{40,48},{48,56},{56,64},{64,7... | collective-permute-start | bytes 49160 | tf_op jit(solution)/shard_map/ppermute | solution.py:240
  6.4 5.2 %collective-permute-start.1 = (f32[24,128]{1,0:T(8,128)S(1)}, f32[24,128]{1,0:T(8,128)S(1)}, u32[]{:S(2)}, u32[]{:S(2)}) collective-permute-start(f32[24,128]{1,0:T(8,128)S(1)} %get-tuple-element.8), channel_id=1, source_target_pairs={{8,0},{16,8},{24,16},{32,24},{40,32},{48,40},{56,48},{64,56},{72,6... | collective-permute-start | bytes 36872 | tf_op jit(solution)/shard_map/ppermute | solution.py:241
  14.4 1.3 %copy-start.3 = (f32[8,16,16,256]{3,2,1,0:T(8,128)}, f32[8,16,16,256]{3,2,1,0:T(8,128)S(1)}, u32[]{:S(2)}) copy-start(f32[8,16,16,256]{3,2,1,0:T(8,128)S(1)} %advect.1) | copy-start | bytes 6291460
  15.7 7.5 %copy-start.15 = (s32[128,2,4]{0,2,1:T(4,128)S(1)}, s32[128,2,4]{0,2,1:T(4,128)}, u32[]{:S(2)}) copy-start(s32[128,2,4]{0,2,1:T(4,128)} %param.25) | copy-start | bytes 12292
  15.7 7.5 %copy-start.16 = (s32[128,2,4]{0,2,1:T(4,128)S(1)}, s32[128,2,4]{0,2,1:T(4,128)}, u32[]{:S(2)}) copy-start(s32[128,2,4]{0,2,1:T(4,128)} %param.24) | copy-start | bytes 12292
  15.7 8.1 %copy-start.7 = (f32[32,8,128]{2,1,0:T(8,128)S(1)}, f32[32,8,128]{2,1,0:T(8,128)}, u32[]{:S(2)}) copy-start(f32[32,8,128]{2,1,0:T(8,128)} %temp_in.1) | copy-start | bytes 393220
  15.7 8.1 %copy-start.11 = (s32[8,128]{1,0:T(8,128)S(1)}, s32[8,128]{1,0:T(8,128)}, u32[]{:S(2)}) copy-start(s32[8,128]{1,0:T(8,128)} %mask_in.1) | copy-start | bytes 12292
  15.7 34.1 %all-to-all-start = ((f32[8,16,16,256]{3,2,1,0:T(8,128)}), f32[8,16,16,256]{3,2,1,0:T(8,128)S(1)}, u32[]{:S(2)}, u32[]{:S(2)}) async-start(f32[8,16,16,256]{3,2,1,0:T(8,128)} %copy-done.3), calls=%async_computation | async-start | bytes 4194304 | tf_op jit(solution)/shard_map/all_to_all | solution.py:248
  23.9 2.2 %copy-start = (f32[64,128,128]{2,1,0:T(8,128)S(1)}, f32[64,128,128]{2,1,0:T(8,128)}, u32[]{:S(2)}) copy-start(f32[64,128,128]{2,1,0:T(8,128)} %weights.3) | copy-start | bytes 12582916
  26.0 23.8 %copy-start.8 = (f32[8,128,128]{2,1,0:T(8,128)S(1)}, f32[8,128,128]{2,1,0:T(8,128)}, u32[]{:S(2)}) copy-start(f32[8,128,128]{2,1,0:T(8,128)} %inverse.2) | copy-start | bytes 1572868
  26.0 23.8 %copy-start.9 = (f32[128,256]{1,0:T(8,128)S(1)}, f32[128,256]{1,0:T(8,128)}, u32[]{:S(2)}) copy-start(f32[128,256]{1,0:T(8,128)} %factor.1) | copy-start | bytes 393220
  53.8 1.3 %copy-start.5 = (f32[8,16,16,256]{3,2,1,0:T(8,128)}, f32[8,16,16,256]{3,2,1,0:T(8,128)S(1)}, u32[]{:S(2)}) copy-start(f32[8,16,16,256]{3,2,1,0:T(8,128)S(1)} %get-tuple-element.9) | copy-start | bytes 6291460
  55.1 7.4 %copy-start.17 = (s32[8,1,4]{0,2,1:T(4,128)S(1)}, s32[8,1,4]{0,2,1:T(4,128)}, u32[]{:S(2)}) copy-start(s32[8,1,4]{0,2,1:T(4,128)} %param.23) | copy-start | bytes 388
  55.1 7.6 %copy-start.18 = (s32[8,1,4]{0,2,1:T(4,128)S(1)}, s32[8,1,4]{0,2,1:T(4,128)}, u32[]{:S(2)}) copy-start(s32[8,1,4]{0,2,1:T(4,128)} %param.22) | copy-start | bytes 388
  55.1 7.8 %copy-start.13 = (f32[16,256]{1,0:T(8,128)S(1)}, f32[16,256]{1,0:T(8,128)}, u32[]{:S(2)}) copy-start(f32[16,256]{1,0:T(8,128)} %get-tuple-element.6.flux) | copy-start | bytes 49156
  55.1 31.7 %copy-start.12 = (f32[32,32]{1,0:T(8,128)S(1)}, f32[32,32]{1,0:T(8,128)}, u32[]{:S(2)}) copy-start(f32[32,32]{1,0:T(8,128)} %inverse.3) | copy-start | bytes 12292
  55.1 31.7 %copy-start.14 = (f32[8,128]{1,0:T(8,128)S(1)}, f32[8,128]{1,0:T(8,128)}, u32[]{:S(2)}) copy-start(f32[8,128]{1,0:T(8,128)} %diffusivity.1) | copy-start | bytes 12292
  55.1 36.5 %all-to-all-start.1 = ((f32[8,16,16,256]{3,2,1,0:T(8,128)}), f32[8,16,16,256]{3,2,1,0:T(8,128)S(1)}, u32[]{:S(2)}, u32[]{:S(2)}) async-start(f32[8,16,16,256]{3,2,1,0:T(8,128)} %copy-done.5), calls=%async_computation.1 | async-start | bytes 4194304 | tf_op jit(solution)/shard_map/all_to_all | solution.py:273
  58.9 27.8 %collective-permute-start.3 = (f32[32,128]{1,0:T(8,128)S(1)}, f32[32,128]{1,0:T(8,128)S(1)}, u32[]{:S(2)}, u32[]{:S(2)}) collective-permute-start(f32[32,128]{1,0:T(8,128)S(1)} %get-tuple-element.14), channel_id=1, source_target_pairs={{0,1},{1,0},{2,3},{3,2},{4,5},{5,4},{6,7},{7,6},{8,9},{9,8},{10,11... | collective-permute-start | bytes 49160 | tf_op jit(solution)/shard_map/ppermute | solution.py:253
  61.9 1.5 %collective-permute-start.4 = (f32[32,128]{1,0:T(8,128)S(1)}, f32[32,128]{1,0:T(8,128)S(1)}, u32[]{:S(2)}, u32[]{:S(2)}) collective-permute-start(f32[32,128]{1,0:T(8,128)S(1)} %get-tuple-element.13), channel_id=1, source_target_pairs={{1,2},{2,1},{3,4},{4,3},{5,6},{6,5},{7,127},{9,10},{10,9},{11,12},... | collective-permute-start | bytes 49160 | tf_op jit(solution)/shard_map/ppermute | solution.py:254
  62.9 23.9 %collective-permute-start.2 = (f32[16,256]{1,0:T(8,128)S(1)}, f32[16,256]{1,0:T(8,128)S(1)}, u32[]{:S(2)}, u32[]{:S(2)}) collective-permute-start(f32[16,256]{1,0:T(8,128)S(1)} %copy-done.13), channel_id=1, source_target_pairs={{8,0},{16,8},{24,16},{32,24},{40,32},{48,40},{56,48},{64,56},{72,6... | collective-permute-start | bytes 49160 | tf_op jit(solution)/shard_map/ppermute | solution.py:275
  86.8 2.2 %copy-start.1 = (f32[64,128,128]{2,1,0:T(8,128)S(1)}, f32[64,128,128]{2,1,0:T(8,128)}, u32[]{:S(2)}) copy-start(f32[64,128,128]{2,1,0:T(8,128)} %weights.3) | copy-start | bytes 12582916

commit v2 on v1

v2 whole, which is shorter than its diff:
```python
import functools

import jax
import jax.numpy as jnp
from jax import lax
from jax.experimental import pallas as pl
from jax.experimental.pallas import tpu as pltpu
from jax.sharding import PartitionSpec as P

F32 = jnp.float32
BF16 = jnp.bfloat16
VMEM = pl.BlockSpec(memory_space=pltpu.VMEM)
SMEM = pl.BlockSpec(memory_space=pltpu.SMEM)
ANY = pl.BlockSpec(memory_space=pl.ANY)
MIB = 1 << 20
LANES = 128
PIECES = 4
HBM = pl.BlockSpec(memory_space=pltpu.HBM)


def kernel_call(body, out_shape, in_specs, out_specs, scratch=(), flops=0, moved=0, limit=16, name=None):
    return pl.pallas_call(
        body,
        out_shape=out_shape,
        in_specs=in_specs,
        out_specs=out_specs,
        scratch_shapes=list(scratch),
        compiler_params=pltpu.CompilerParams(vmem_limit_bytes=limit * MIB),
        cost_estimate=pl.CostEstimate(flops=flops, bytes_accessed=moved, transcendentals=0),
        name=name,
    )


def shape(*dims):
    return jax.ShapeDtypeStruct(dims, F32)


def in_hbm(*dims):
    return pltpu.HBM(dims, F32)


def in_vmem(*dims):
    return pltpu.VMEM(dims, F32)


def stays(value):
    return pltpu.with_memory_space_constraint(value, pltpu.HBM)


def split(value):
    high = value.astype(BF16)
    return high, (value - high.astype(F32)).astype(BF16)


def edges_kernel(atm_in, ocean_in, mask_in, east_msg, west_msg, atm, ocean, mask, sems):
    levels, rows, cells = atm.shape
    step = levels // PIECES
    pieces = [pl.ds(piece * step, step) for piece in range(PIECES)]
    copies = [pltpu.make_async_copy(atm_in.at[p], atm.at[p], sems.at[i]) for i, p in enumerate(pieces)]
    copies.append(pltpu.make_async_copy(ocean_in, ocean, sems.at[PIECES]))
    copies.append(pltpu.make_async_copy(mask_in, mask, sems.at[PIECES + 1]))
    for copy in copies:
        copy.start()
    lane = lax.broadcasted_iota(jnp.int32, (LANES, LANES), 1)
    last = jnp.zeros((LANES, LANES), F32)
    first = jnp.zeros((LANES, LANES), F32)
    for piece in range(PIECES):
        copies[piece].wait()
        for level in range(piece * step, (piece + 1) * step):
            last = jnp.where(lane == level, atm[level, :, cells - 1 : cells], last)
            first = jnp.where(lane == level, atm[level, :, 0:1], first)
    for copy in copies[PIECES:]:
        copy.wait()
    for part in range(2):
        tile = slice(part * LANES, (part + 1) * LANES)
        last = jnp.where(lane == levels + part, ocean[tile, LANES - 1 : LANES], last)
        first = jnp.where(lane == levels + part, ocean[tile, 0:1], first)
    east_msg[:24, :] = last.T[:24, :]
    east_msg[24:, :] = mask[...].astype(F32) * ocean[:8, :]
    west_msg[...] = first.T[:24, :]


def advect_kernel(atm, courant, from_west, from_east, out, west_cols, east_cols, held, sems):
    levels, _, cells = atm.shape
    band = out.shape[1]
    west_cols[...] = from_west[...].T
    east_cols[...] = from_east[...].T
    lane = lax.broadcasted_iota(jnp.int32, (band, cells), 1)

    @pl.loop(0, out.shape[0])
    def _(dest):
        rows = pl.ds(pl.multiple_of(dest * band, band), band)
        made = []
        for level in range(levels):
            here = atm[level, rows, :]
            speed = courant[level, rows, :]
            west = jnp.where(lane == 0, west_cols[rows, level : level + 1], pltpu.roll(here, 1, 1))
            east = jnp.where(
                lane == cells - 1, east_cols[rows, level : level + 1], pltpu.roll(here, cells - 1, 1)
            )
            made.append(
                here
                - jnp.maximum(speed, 0.0) * (here - west)
                - jnp.minimum(speed, 0.0) * (east - here)
            )
        held[dest] = jnp.swapaxes(jnp.stack(made), 0, 1)
        pltpu.make_async_copy(held.at[dest], out.at[dest], sems.at[dest]).start()

    for dest in range(out.shape[0]):
        pltpu.make_async_copy(held.at[dest], out.at[dest], sems.at[dest]).wait()


def mat_vec(ids, first, count, source, weights):
    total = jnp.zeros(weights.shape[1:], F32)
    half = ids.shape[0] // 2
    for k in range(count):
        block = source[pl.ds(ids[first + k], 1), :]
        total = total + weights[ids[half + first + k]] * block
    return jnp.sum(total.T, axis=0, keepdims=True)


def sst_kernel(width, place, ids, from_west, ocean, mask, weights, sst, even_msg, odd_msg, window, halves):
    tile_rows = mask.shape[0]
    tile = ocean[...].reshape(-1, tile_rows, LANES)
    even = lax.rem(place[0], 2) == 0
    low, top = tile[:, 0, :], tile[:, tile_rows - 1, :]
    even_msg[...] = jnp.where(even, top, low)
    odd_msg[...] = jnp.where(even, low, top)
    window[:8, :] = from_west[24:32, :]
    window[8:, :] = mask[...].astype(F32) * ocean[:8, :]
    rows = sst.shape[0]

    @pl.loop(0, rows)
    def _(row):
        for g in range(2):
            halves[g, pl.ds(row, 1), :] = mat_vec(ids, (row * 2 + g) * width, width, window, weights)

    for g in range(2):
        sst[:, g * LANES : (g + 1) * LANES] = halves[g]


def solve_kernel(place, columns, inverse, factor, sst, even_rows, odd_rows, out, flux, held, turned, sems):
    sub = place[0]
    groups, band, depth, cells = columns.shape
    levels = groups * depth
    high, low = split(inverse[sub])
    twice = jnp.concatenate([high, high], axis=1)

    def solve_row(row, _):
        here = columns[:, row].reshape(levels, cells)
        x_high, x_low = split(here)
        held[row] = jnp.dot(
            twice, jnp.concatenate([x_high, x_low], axis=0), preferred_element_type=F32
        ) + jnp.dot(low, x_high, preferred_element_type=F32)
        return 0

    lax.fori_loop(0, band, solve_row, 0, unroll=4)
    copies = []
    for group in range(groups):
        turned[group] = jnp.swapaxes(held[:, group * depth : (group + 1) * depth, :], 0, 1)
        copies.append(pltpu.make_async_copy(turned.at[group], out.at[group], sems.at[group]))
        copies[-1].start()
    rows = pl.ds(pl.multiple_of(sub * band, band), band)
    flux[...] = factor[rows, :] * (sst[...] - turned[groups - 1, depth - 1])
    for copy in copies:
        copy.wait()


def ocean_kernel(
    n_sub, place, temp_in, diffusivity, mask_in, inverse,
    from_west, from_east, even_rows, odd_rows, folded, out,
):
    sub = place[0]
    levels, rows, cells = temp_in.shape
    temp = temp_in[...]
    mask = mask_in[...].astype(F32)
    even = lax.rem(sub, 2) == 0
    own_south = temp[:, 0, :]
    south_row = jnp.where(even, jnp.where(sub == 0, own_south, odd_rows[...]), even_rows[...])
    north_row = jnp.where(
        even, even_rows[...], jnp.where(sub == n_sub - 1, folded[...], odd_rows[...])
    )
    south = jnp.concatenate([south_row[:, None, :], temp[:, :-1, :]], axis=1)
    north = jnp.concatenate([temp[:, 1:, :], north_row[:, None, :]], axis=1)

    def column(message):
        side = message[16:24, :].T
        return jnp.concatenate([side[:, 0:1], side[:, 1:2]], axis=0)

    flat = temp.reshape(levels * rows, cells)
    lane = lax.broadcasted_iota(jnp.int32, flat.shape, 1)
    west = jnp.where(lane == 0, column(from_west), pltpu.roll(flat, 1, 1))
    east = jnp.where(lane == cells - 1, column(from_east), pltpu.roll(flat, cells - 1, 1))
    lap = (west + east).reshape(temp.shape) + north + south - 4.0 * temp
    stepped = mask[None] * (temp + diffusivity[...][None] * lap)
    by_row = jnp.swapaxes(stepped, 0, 1)
    high, low = split(inverse[...])
    made = []
    for row in range(rows):
        x_high, x_low = split(by_row[row])
        made.append(
            jnp.dot(high, x_high, preferred_element_type=F32)
            + jnp.dot(high, x_low, preferred_element_type=F32)
            + jnp.dot(low, x_high, preferred_element_type=F32)
        )
    out[...] = jnp.swapaxes(jnp.stack(made), 0, 1)


def last_kernel(
    width, ids, flux, from_east_flux, weights, mask, inverse, before, parts, out, ocean,
    window, picked, pick_sems, sems,
):
    entries = picked.shape[0]
    picks = [
        pltpu.make_async_copy(weights.at[ids[entries + i]], picked.at[i], pick_sems.at[i])
        for i in range(entries)
    ]
    for pick in picks:
        pick.start()
    band = parts.shape[2]
    copies = [
        pltpu.make_async_copy(parts.at[b], out.at[:, pl.ds(b * band, band), :], sems.at[b])
        for b in range(parts.shape[0])
    ]
    for copy in copies:
        copy.start()
    for side, source in enumerate((flux, from_east_flux)):
        for g in range(2):
            at = (side * 2 + g) * band
            window[at : at + band, :] = source[:, g * LANES : (g + 1) * LANES]
    levels, rows, _ = before.shape
    made = []
    for row in range(rows):
        total = jnp.zeros((LANES, LANES), F32)
        for k in range(row * width, (row + 1) * width):
            picks[k].wait()
            total = total + picked[k] * window[pl.ds(ids[k], 1), :]
        made.append(jnp.sum(total.T, axis=0, keepdims=True))
    heat = mask[...].astype(F32) * jnp.concatenate(made, axis=0)
    for level in range(levels):
        ocean[level] = before[level] + inverse[level : level + 1, 0:1] * heat
    for copy in copies:
        copy.wait()


def pair_exchanges(n_lon, n_sub):
    first, second = [], []
    for lon in range(n_lon):
        at = lon * n_sub
        for south in range(n_sub - 1):
            pairs = first if south % 2 == 0 else second
            pairs += [(at + south, at + south + 1), (at + south + 1, at + south)]
        second.append((at + n_sub - 1, (n_lon - 1 - lon) * n_sub + n_sub - 1))
    return first, second


def per_device(
    atm_tracer,
    courant,
    column_inverse,
    heat_exchange_factor,
    ocean_temp,
    diffusivity,
    ocean_inverse,
    land_mask,
    weights,
    a2o_src,
    a2o_wgt,
    o2a_src,
    o2a_wgt,
):
    lon_index = lax.axis_index("lon")
    sub_index = lax.axis_index("sub")
    n_lon = lax.axis_size("lon")
    n_sub = lax.axis_size("sub")
    lev_dev, alat, alon_dev = atm_tracer.shape
    groups = alon_dev // LANES
    ngroups = groups * n_lon
    olev, olat_dev, olon_dev = ocean_temp.shape
    aband = alat // n_sub
    width = o2a_src.shape[2]
    ocean_flat = ocean_temp.reshape(olev * olat_dev, olon_dev)
    place = jnp.reshape(sub_index, (1,))

    east_msg, west_msg, atm_here = kernel_call(
        edges_kernel, (shape(32, LANES), shape(24, LANES), in_vmem(lev_dev, alat, alon_dev)), [HBM] * 3, (VMEM,) * 3,
        scratch=[
            pltpu.VMEM(ocean_flat.shape, F32), pltpu.VMEM(land_mask.shape, land_mask.dtype),
            pltpu.SemaphoreType.DMA((PIECES + 2,)),
        ],
        flops=2 * MIB, moved=2 * MIB, name="edges",
    )(stays(atm_tracer), stays(ocean_flat), stays(land_mask))
    up = [(i, (i + 1) % n_lon) for i in range(n_lon)]
    down = [(b, a) for a, b in up]
    from_west = lax.ppermute(east_msg, "lon", up)
    from_east = lax.ppermute(west_msg, "lon", down)

    advected = kernel_call(
        advect_kernel, in_hbm(n_sub, aband, lev_dev, alon_dev), [VMEM] * 4, HBM,
        scratch=[
            pltpu.VMEM((LANES, 32), F32), pltpu.VMEM((LANES, 24), F32),
            pltpu.VMEM((n_sub, aband, lev_dev, alon_dev), F32), pltpu.SemaphoreType.DMA((n_sub,)),
        ],
        flops=10 * MIB, moved=6 * MIB, name="advect",
    )(atm_here, courant, from_west, from_east)
    columns = lax.all_to_all(advected, "sub", split_axis=0, concat_axis=0, tiled=True)

    band_src = lax.dynamic_slice_in_dim(o2a_src, sub_index * aband, aband, 0).reshape(-1)
    band_wgt = lax.dynamic_slice_in_dim(o2a_wgt, sub_index * aband, aband, 0).reshape(-1)
    tile = jnp.remainder(band_src % n_lon - lon_index + 1, n_lon)
    sea_ids = tile * olat_dev + band_src // n_lon - sub_index * olat_dev
    sst, even_msg, odd_msg = kernel_call(
        functools.partial(sst_kernel, width),
        (shape(aband, alon_dev), shape(olev, LANES), shape(olev, LANES)), [SMEM] * 2 + [VMEM] * 4, (VMEM,) * 3,
        scratch=[pltpu.VMEM((2 * olat_dev, LANES), F32), pltpu.VMEM((groups, aband, LANES), F32)],
        flops=8 * MIB, moved=8 * MIB, name="sst",
    )(place, jnp.concatenate([sea_ids, band_wgt]), from_west, ocean_flat, land_mask, weights)
    first, second = pair_exchanges(n_lon, n_sub)
    even_rows = lax.ppermute(even_msg, ("lon", "sub"), first)
    odd_rows = lax.ppermute(odd_msg, ("lon", "sub"), second)
    folded = jnp.flip(odd_rows, axis=1)

    solved, flux_band = kernel_call(
        solve_kernel, (in_hbm(n_sub, lev_dev, aband, alon_dev), shape(aband, alon_dev)),
        [SMEM] + [VMEM] * 4 + [ANY] * 2, (HBM, VMEM),
        scratch=[
            pltpu.VMEM((aband, lev_dev * n_sub, alon_dev), F32),
            pltpu.VMEM((n_sub, lev_dev, aband, alon_dev), F32), pltpu.SemaphoreType.DMA((n_sub,)),
        ],
        flops=400 * MIB, moved=4 * MIB, name="solve",
    )(place, columns, column_inverse, heat_exchange_factor, sst, even_rows, odd_rows)
    parts = lax.all_to_all(solved, "sub", split_axis=0, concat_axis=0, tiled=True)
    east_flux = lax.ppermute(flux_band, "lon", down)

    src = a2o_src.reshape(-1)
    group = jnp.remainder(src % ngroups - lon_index * groups, ngroups)
    flux_ids = group * aband + src // ngroups - sub_index * aband
    entries = src.shape[0]
    before = kernel_call(
        functools.partial(ocean_kernel, n_sub), shape(olev, olat_dev, olon_dev),
        [SMEM] + [VMEM] * 9, VMEM, flops=8 * MIB, moved=MIB, name="ocean",
    )(
        place, ocean_temp, diffusivity, land_mask, ocean_inverse,
        from_west, from_east, even_rows, odd_rows, folded,
    )
    returned, ocean_new = kernel_call(
        functools.partial(last_kernel, width), (shape(lev_dev, alat, alon_dev), shape(olev, olat_dev, olon_dev)),
        [SMEM] + [VMEM] * 2 + [HBM] + [VMEM] * 4, (HBM, VMEM),
        scratch=[
            pltpu.VMEM((4 * aband, LANES), F32), pltpu.VMEM((entries, LANES, LANES), F32),
            pltpu.SemaphoreType.DMA((entries,)), pltpu.SemaphoreType.DMA((n_sub,)),
        ],
        moved=6 * MIB, name="last",
    )(
        jnp.concatenate([flux_ids, a2o_wgt.reshape(-1)]), flux_band, east_flux, stays(weights),
        land_mask, ocean_inverse, before, parts,
    )
    return returned, ocean_new, flux_band


def solution(mesh):
    return jax.shard_map(
        per_device,
        mesh=mesh,
        in_specs=(
            P("sub", None, "lon"),
            P("sub", None, "lon"),
            P(),
            P(None, "lon"),
            P(None, "sub", "lon"),
            P("sub", "lon"),
            P(),
            P("sub", "lon"),
            P(),
            P("sub", "lon", None),
            P("sub", "lon", None),
            P(None, "lon", None),
            P(None, "lon", None),
        ),
        out_specs=(P("sub", None, "lon"), P(None, "sub", "lon"), P("sub", "lon")),
        check_vma=False,
    )
```

time: 93.8 us -> 89 us (0.949)
  local copies, waits for them, and re-layouts: 11.1 us -> 3.15 us
  Pallas kernels: 14 us -> 16.6 us
  waiting for transfers between devices: 49.8 us -> 50.9 us
    all_to_all x1, waiting for transfers between devices: 0.01 us -> 22.9 us  [per_device(): lax.all_to_all(solved, 'sub', split_axis=0, concat_axis=0, tiled=True)]
    all_to_all x1, waiting for transfers between devices: 21.3 us -> 2.08 us  [per_device(): lax.all_to_all(advected, 'sub', split_axis=0, concat_axis=0, tiled=True)]
    unnamed x40 -> x28, local copies, waits for them, and re-layouts: 10.4 us -> 2.41 us
    ppermute x2, waiting for transfers between devices: 23.3 us -> 16 us  [the longest x1 16 us: per_device(): even_rows = lax.ppermute(even_msg, ('lon', 'sub'), first)]
    ppermute x1, waiting for transfers between devices: 0.01 us -> 4.8 us  [per_device(): east_flux = lax.ppermute(flux_band, 'lon', down)]
    pallas_call x6, Pallas kernels: 14 us -> 16.6 us  [the longest x1 4.24 us: per_device(): kernel_call(functools.partial(last_kernel, width), (shape(lev_dev, alat,...]
  transfers between devices with their start and end apart: 7 -> 7, of which waited for: 3 -> 5; matrix products, arithmetic and copies ran while one was open for 1% -> 1% of each run, Pallas kernels for 6% -> 4%
where the time goes in v2:
time: 89 us; the launch traced here: 88.5 us
  waiting for transfers between devices  50.9 us (57%)
  starting transfers between devices  16.9 us (19%)
  Pallas kernels  16.6 us (19%)
  local copies, waits for them, and re-layouts  3.15 us (4%)
    all_to_all x1, waiting for transfers between devices, per_device(): lax.all_to_all(solved, 'sub', split_axis=0, concat_axis=0, tiled=True)  22.9 us
    ppermute x1, waiting for transfers between devices, per_device(): even_rows = lax.ppermute(even_msg, ('lon', 'sub'), first)  16 us
    all_to_all x1, starting transfers between devices, per_device(): lax.all_to_all(advected, 'sub', split_axis=0, concat_axis=0, tiled=True)  7.51 us
    ppermute x1, waiting for transfers between devices, per_device(): from_east = lax.ppermute(west_msg, 'lon', down)  5.23 us
    ppermute x1, waiting for transfers between devices, per_device(): east_flux = lax.ppermute(flux_band, 'lon', down)  4.8 us
    pallas_call x1, Pallas kernels, per_device(): kernel_call(functools.partial(last_kernel, width), (shape(lev_dev, alat,...  4.24 us
    all_to_all x1, starting transfers between devices, per_device(): lax.all_to_all(solved, 'sub', split_axis=0, concat_axis=0, tiled=True)  3.75 us
    pallas_call x1, Pallas kernels, per_device(): kernel_call(advect_kernel, in_hbm(n_sub, aband, lev_dev, alon_dev), [VMEM...  3.6 us
  transfers between devices with their start and end apart: 7, of which 5 were waited for; matrix products, arithmetic and copies ran while one was open for 1% of the time, Pallas kernels for 4%

profile of v2, /device:TPU:7, one launch (start us, length us, event | category | flops | bytes accessed | tf_op | source)
XLA Modules:
  0.0 88.5 jit_solution(13016958100036153927)
XLA Ops:
  0.6 2.3 %edges.1 = (f32[32,128]{1,0:T(8,128)S(1)}, f32[24,128]{1,0:T(8,128)S(1)}, f32[16,128,256]{2,1,0:T(8,128)S(1)}) custom-call(f32[16,128,256]{2,1,0:T(8,128)} %atm_in.1, f32[256,128]{1,0:T(8,128)} %bitcast.6, s32[8,128]{1,0:T(8,128)} %mask.3), custom_call_target="tpu_custom_call" | custom-call | flops 2097152 | bytes 2097152 | tf_op jit(solution)/shard_map/edges/pallas_call | solution.py:285
  2.9 1.8 %collective-permute-start = (f32[32,128]{1,0:T(8,128)S(1)}, f32[32,128]{1,0:T(8,128)S(1)}, u32[]{:S(2)}, u32[]{:S(2)}) collective-permute-start(f32[32,128]{1,0:T(8,128)S(1)} %get-tuple-element.14), channel_id=1, source_target_pairs={{0,8},{8,16},{16,24},{24,32},{32,40},{40,48},{48,56},{56,64},{64,7... | collective-permute-start | bytes 49160 | tf_op jit(solution)/shard_map/ppermute | solution.py:295
  4.8 5.2 %collective-permute-done.1.from_east = f32[24,128]{1,0:T(8,128)S(1)} collective-permute-done((f32[24,128]{1,0:T(8,128)S(1)}, f32[24,128]{1,0:T(8,128)S(1)}, u32[]{:S(2)}, u32[]{:S(2)}) %collective-permute-start.1) | collective-permute-done | bytes 12320 | tf_op jit(solution)/shard_map/ppermute | solution.py:296
  10.0 3.6 %advect.1 = f32[8,16,16,256]{3,2,1,0:T(8,128)} custom-call(f32[16,128,256]{2,1,0:T(8,128)S(1)} %get-tuple-element.13.atm, f32[16,128,256]{2,1,0:T(8,128)S(1)} %copy-done.1, f32[32,128]{1,0:T(8,128)S(1)} %collective-permute-done.from_west, f32[24,128]{1,0:T(8,128)S(1)} %collective-permute-done.1.from_east), custom_call_target="tpu_custom_call" | custom-call | flops 10485760 | bytes 6291456 | tf_op jit(solution)/shard_map/advect/pallas_call | solution.py:298
  13.6 0.0 copy-start.10
  13.6 0.0 copy-start.2
  13.7 7.5 %all-to-all-start = ((f32[8,16,16,256]{3,2,1,0:T(8,128)}), f32[8,16,16,256]{3,2,1,0:T(8,128)S(1)}, u32[]{:S(2)}, u32[]{:S(2)}) async-start(f32[8,16,16,256]{3,2,1,0:T(8,128)} %advect.1), calls=%async_computation | async-start | bytes 4194304 | tf_op jit(solution)/shard_map/all_to_all | solution.py:306
  21.2 0.1 constant_dynamic-slice_fusion
  21.3 0.1 copy.23
  21.4 0.1 reshape.29
  21.5 0.1 copy.22
  21.6 0.1 reshape.28
  21.8 2.2 %copy-done = f32[64,128,128]{2,1,0:T(8,128)S(1)} copy-done((f32[64,128,128]{2,1,0:T(8,128)S(1)}, f32[64,128,128]{2,1,0:T(8,128)}, u32[]{:S(2)}) %copy-start) | copy-done | bytes 4194328
  24.0 2.6 %sst.1 = (f32[16,256]{1,0:T(8,128)S(1)}, f32[32,128]{1,0:T(8,128)S(1)}, f32[32,128]{1,0:T(8,128)S(1)}) custom-call(s32[1]{0:T(128)} %bitcast.place, s32[256]{0:T(256)S(1)} %pad_add_fusion.ids, f32[32,128]{1,0:T(8,128)S(1)} %collective-permute-done.from_west, f32[256,128]{1,0:T(8,128)S(1)} %bitcast.7, s32[8,128]{1,0:T(8,128)S(1)} %copy-done.6, ...), custom_call_target="tpu_custom_call" | custom-call | flops 8388608 | bytes 8388608 | tf_op jit(solution)/shard_map/sst/pallas_call | solution.py:312
  26.5 3.0 %collective-permute-start.2 = (f32[32,128]{1,0:T(8,128)S(1)}, f32[32,128]{1,0:T(8,128)S(1)}, u32[]{:S(2)}, u32[]{:S(2)}) collective-permute-start(f32[32,128]{1,0:T(8,128)S(1)} %get-tuple-element.17), channel_id=1, source_target_pairs={{0,1},{1,0},{2,3},{3,2},{4,5},{5,4},{6,7},{7,6},{8,9},{9,8},{10,11... | collective-permute-start | bytes 49160 | tf_op jit(solution)/shard_map/ppermute | solution.py:319
  29.6 0.7 collective-permute-start.3
  30.2 16.0 %collective-permute-done.2.even_rows = f32[32,128]{1,0:T(8,128)S(1)} collective-permute-done((f32[32,128]{1,0:T(8,128)S(1)}, f32[32,128]{1,0:T(8,128)S(1)}, u32[]{:S(2)}, u32[]{:S(2)}) %collective-permute-start.2) | collective-permute-done | bytes 16416 | tf_op jit(solution)/shard_map/ppermute | solution.py:319
  46.2 2.1 %all-to-all-done.columns = f32[8,16,16,256]{3,2,1,0:T(8,128)S(1)} async-done(((f32[8,16,16,256]{3,2,1,0:T(8,128)}), f32[8,16,16,256]{3,2,1,0:T(8,128)S(1)}, u32[]{:S(2)}, u32[]{:S(2)}) %all-to-all-start) | async-done | bytes 2097184 | tf_op jit(solution)/shard_map/all_to_all | solution.py:306
  48.3 3.3 %solve.1 = (f32[8,16,16,256]{3,2,1,0:T(8,128)}, f32[16,256]{1,0:T(8,128)}) custom-call(s32[1]{0:T(128)} %bitcast.place, f32[8,16,16,256]{3,2,1,0:T(8,128)S(1)} %all-to-all-done.columns, f32[8,128,128]{2,1,0:T(8,128)S(1)} %copy-done.3, f32[128,256]{1,0:T(8,128)S(1)} %copy-done.4, f32[16,256]{1,0:T(8,128)S(1)} %get-tuple-element.16.sst, ...), custom_call_target="tpu_custom_call" | custom-call | flops 419430400 | bytes 4194304 | tf_op jit(solution)/shard_map/solve/pallas_call | solution.py:323
  51.6 0.0 copy-start.7
  51.6 3.7 %all-to-all-start.1 = ((f32[8,16,16,256]{3,2,1,0:T(8,128)}), f32[8,16,16,256]{3,2,1,0:T(8,128)S(1)}, u32[]{:S(2)}, u32[]{:S(2)}) async-start(f32[8,16,16,256]{3,2,1,0:T(8,128)} %get-tuple-element.20), calls=%async_computation.1 | async-start | bytes 4194304 | tf_op jit(solution)/shard_map/all_to_all | solution.py:332
  55.4 0.1 copy.20
  55.5 0.1 reshape.24
  55.6 0.1 copy.21
  55.7 0.1 reshape.25
  55.8 0.1 collective-permute-start.4
  55.9 0.1 pad_add_fusion.1.ids
  55.9 0.1 rev.4.folded
  56.0 0.6 ocean.1.before
  56.6 4.8 %collective-permute-done.4.from_east_flux = f32[16,256]{1,0:T(8,128)S(1)} collective-permute-done((f32[16,256]{1,0:T(8,128)S(1)}, f32[16,256]{1,0:T(8,128)S(1)}, u32[]{:S(2)}, u32[]{:S(2)}) %collective-permute-start.4) | collective-permute-done | bytes 16416 | tf_op jit(solution)/shard_map/ppermute | solution.py:333
  61.4 22.9 %all-to-all-done.1.parts = f32[8,16,16,256]{3,2,1,0:T(8,128)S(1)} async-done(((f32[8,16,16,256]{3,2,1,0:T(8,128)}), f32[8,16,16,256]{3,2,1,0:T(8,128)S(1)}, u32[]{:S(2)}, u32[]{:S(2)}) %all-to-all-start.1) | async-done | bytes 2097184 | tf_op jit(solution)/shard_map/all_to_all | solution.py:332
  84.3 4.2 %last.1 = (f32[16,128,256]{2,1,0:T(8,128)}, f32[32,8,128]{2,1,0:T(8,128)}) custom-call(s32[64]{0:T(128)S(1)} %pad_add_fusion.1.ids, f32[16,256]{1,0:T(8,128)S(1)} %copy-done.7, f32[16,256]{1,0:T(8,128)S(1)} %collective-permute-done.4.from_east_flux, f32[64,128,128]{2,1,0:T(8,128)} %weights.3, s32[8,128]{1,0:T(8,128)S(1)} %copy-done.6, ...), custom_call_target="tpu_custom_call" | custom-call | bytes 6291456 | tf_op jit(solution)/shard_map/last/pallas_call | solution.py:346
  (28 shorter events, 0.1 us)
Async XLA Ops:
  0.6 9.4 %copy-start.1 = (f32[16,128,256]{2,1,0:T(8,128)S(1)}, f32[16,128,256]{2,1,0:T(8,128)}, u32[]{:S(2)}) copy-start(f32[16,128,256]{2,1,0:T(8,128)} %courant.1) | copy-start | bytes 6291460
  2.9 7.1 %collective-permute-start = (f32[32,128]{1,0:T(8,128)S(1)}, f32[32,128]{1,0:T(8,128)S(1)}, u32[]{:S(2)}, u32[]{:S(2)}) collective-permute-start(f32[32,128]{1,0:T(8,128)S(1)} %get-tuple-element.14), channel_id=1, source_target_pairs={{0,8},{8,16},{16,24},{24,32},{32,40},{40,48},{48,56},{56,64},{64,7... | collective-permute-start | bytes 49160 | tf_op jit(solution)/shard_map/ppermute | solution.py:295
  4.8 5.2 %collective-permute-start.1 = (f32[24,128]{1,0:T(8,128)S(1)}, f32[24,128]{1,0:T(8,128)S(1)}, u32[]{:S(2)}, u32[]{:S(2)}) collective-permute-start(f32[24,128]{1,0:T(8,128)S(1)} %get-tuple-element.15), channel_id=1, source_target_pairs={{8,0},{16,8},{24,16},{32,24},{40,32},{48,40},{56,48},{64,56},{72,6... | collective-permute-start | bytes 36872 | tf_op jit(solution)/shard_map/ppermute | solution.py:296
  13.6 7.6 %copy-start.9 = (s32[128,2,4]{0,2,1:T(4,128)S(1)}, s32[128,2,4]{0,2,1:T(4,128)}, u32[]{:S(2)}) copy-start(s32[128,2,4]{0,2,1:T(4,128)} %param.25) | copy-start | bytes 12292
  13.6 7.6 %copy-start.10 = (s32[128,2,4]{0,2,1:T(4,128)S(1)}, s32[128,2,4]{0,2,1:T(4,128)}, u32[]{:S(2)}) copy-start(s32[128,2,4]{0,2,1:T(4,128)} %param.24) | copy-start | bytes 12292
  13.6 8.1 %copy-start.2 = (f32[32,8,128]{2,1,0:T(8,128)S(1)}, f32[32,8,128]{2,1,0:T(8,128)}, u32[]{:S(2)}) copy-start(f32[32,8,128]{2,1,0:T(8,128)} %temp_in.1) | copy-start | bytes 393220
  13.7 8.1 %copy-start.6 = (s32[8,128]{1,0:T(8,128)S(1)}, s32[8,128]{1,0:T(8,128)}, u32[]{:S(2)}) copy-start(s32[8,128]{1,0:T(8,128)} %mask.3) | copy-start | bytes 12292
  13.7 34.6 %all-to-all-start = ((f32[8,16,16,256]{3,2,1,0:T(8,128)}), f32[8,16,16,256]{3,2,1,0:T(8,128)S(1)}, u32[]{:S(2)}, u32[]{:S(2)}) async-start(f32[8,16,16,256]{3,2,1,0:T(8,128)} %advect.1), calls=%async_computation | async-start | bytes 4194304 | tf_op jit(solution)/shard_map/all_to_all | solution.py:306
  21.8 2.2 %copy-start = (f32[64,128,128]{2,1,0:T(8,128)S(1)}, f32[64,128,128]{2,1,0:T(8,128)}, u32[]{:S(2)}) copy-start(f32[64,128,128]{2,1,0:T(8,128)} %weights.3) | copy-start | bytes 12582916
  24.0 24.3 %copy-start.3 = (f32[8,128,128]{2,1,0:T(8,128)S(1)}, f32[8,128,128]{2,1,0:T(8,128)}, u32[]{:S(2)}) copy-start(f32[8,128,128]{2,1,0:T(8,128)} %inverse.3) | copy-start | bytes 1572868
  24.0 24.3 %copy-start.4 = (f32[128,256]{1,0:T(8,128)S(1)}, f32[128,256]{1,0:T(8,128)}, u32[]{:S(2)}) copy-start(f32[128,256]{1,0:T(8,128)} %factor.1) | copy-start | bytes 393220
  26.5 19.7 %collective-permute-start.2 = (f32[32,128]{1,0:T(8,128)S(1)}, f32[32,128]{1,0:T(8,128)S(1)}, u32[]{:S(2)}, u32[]{:S(2)}) collective-permute-start(f32[32,128]{1,0:T(8,128)S(1)} %get-tuple-element.17), channel_id=1, source_target_pairs={{0,1},{1,0},{2,3},{3,2},{4,5},{5,4},{6,7},{7,6},{8,9},{9,8},{10,11... | collective-permute-start | bytes 49160 | tf_op jit(solution)/shard_map/ppermute | solution.py:319
  29.6 16.6 %collective-permute-start.3 = (f32[32,128]{1,0:T(8,128)S(1)}, f32[32,128]{1,0:T(8,128)S(1)}, u32[]{:S(2)}, u32[]{:S(2)}) collective-permute-start(f32[32,128]{1,0:T(8,128)S(1)} %get-tuple-element.18), channel_id=1, source_target_pairs={{1,2},{2,1},{3,4},{4,3},{5,6},{6,5},{7,127},{9,10},{10,9},{11,12},... | collective-permute-start | bytes 49160 | tf_op jit(solution)/shard_map/ppermute | solution.py:320
  51.6 3.8 %copy-start.11 = (s32[8,1,4]{0,2,1:T(4,128)S(1)}, s32[8,1,4]{0,2,1:T(4,128)}, u32[]{:S(2)}) copy-start(s32[8,1,4]{0,2,1:T(4,128)} %param.22) | copy-start | bytes 388
  51.6 4.0 %copy-start.12 = (s32[8,1,4]{0,2,1:T(4,128)S(1)}, s32[8,1,4]{0,2,1:T(4,128)}, u32[]{:S(2)}) copy-start(s32[8,1,4]{0,2,1:T(4,128)} %param.23) | copy-start | bytes 388
  51.6 4.2 %copy-start.7 = (f32[16,256]{1,0:T(8,128)S(1)}, f32[16,256]{1,0:T(8,128)}, u32[]{:S(2)}) copy-start(f32[16,256]{1,0:T(8,128)} %get-tuple-element.12.flux) | copy-start | bytes 49156
  51.6 4.4 %copy-start.5 = (f32[32,32]{1,0:T(8,128)S(1)}, f32[32,32]{1,0:T(8,128)}, u32[]{:S(2)}) copy-start(f32[32,32]{1,0:T(8,128)} %inverse.5) | copy-start | bytes 12292
  51.6 4.4 %copy-start.8 = (f32[8,128]{1,0:T(8,128)S(1)}, f32[8,128]{1,0:T(8,128)}, u32[]{:S(2)}) copy-start(f32[8,128]{1,0:T(8,128)} %diffusivity.1) | copy-start | bytes 12292
  51.6 32.6 %all-to-all-start.1 = ((f32[8,16,16,256]{3,2,1,0:T(8,128)}), f32[8,16,16,256]{3,2,1,0:T(8,128)S(1)}, u32[]{:S(2)}, u32[]{:S(2)}) async-start(f32[8,16,16,256]{3,2,1,0:T(8,128)} %get-tuple-element.20), calls=%async_computation.1 | async-start | bytes 4194304 | tf_op jit(solution)/shard_map/all_to_all | solution.py:332
  55.8 5.6 %collective-permute-start.4 = (f32[16,256]{1,0:T(8,128)S(1)}, f32[16,256]{1,0:T(8,128)S(1)}, u32[]{:S(2)}, u32[]{:S(2)}) collective-permute-start(f32[16,256]{1,0:T(8,128)S(1)} %copy-done.7), channel_id=1, source_target_pairs={{8,0},{16,8},{24,16},{32,24},{40,32},{48,40},{56,48},{64,56},{72,6... | collective-permute-start | bytes 49160 | tf_op jit(solution)/shard_map/ppermute | solution.py:333

commit v3 on v2

--- a/solution.py
+++ b/solution.py
@@ -167,10 +167,22 @@
 
 
 def ocean_kernel(
-    n_sub, place, temp_in, diffusivity, mask_in, inverse,
-    from_west, from_east, even_rows, odd_rows, folded, out,
+    width, n_sub, place, ids, flux, from_east_flux, weights, temp_in, diffusivity, mask_in, inverse,
+    from_west, from_east, even_rows, odd_rows, folded, out, window, picked, sems,
 ):
     sub = place[0]
+    band = flux.shape[0]
+    entries = picked.shape[0]
+    picks = [
+        pltpu.make_async_copy(weights.at[ids[entries + i]], picked.at[i], sems.at[i])
+        for i in range(entries)
+    ]
+    for pick in picks:
+        pick.start()
+    for side, source in enumerate((flux, from_east_flux)):
+        for g in range(2):
+            at = (side * 2 + g) * band
+            window[at : at + band, :] = source[:, g * LANES : (g + 1) * LANES]
     levels, rows, cells = temp_in.shape
     temp = temp_in[...]
     mask = mask_in[...].astype(F32)
@@ -194,10 +206,16 @@
     lap = (west + east).reshape(temp.shape) + north + south - 4.0 * temp
     stepped = mask[None] * (temp + diffusivity[...][None] * lap)
     by_row = jnp.swapaxes(stepped, 0, 1)
+    level = lax.broadcasted_iota(jnp.int32, (levels, cells), 0)
     high, low = split(inverse[...])
     made = []
     for row in range(rows):
-        x_high, x_low = split(by_row[row])
+        total = jnp.zeros((LANES, LANES), F32)
+        for k in range(row * width, (row + 1) * width):
+            picks[k].wait()
+            total = total + picked[k] * window[pl.ds(ids[k], 1), :]
+        heat = mask[row : row + 1, :] * jnp.sum(total.T, axis=0, keepdims=True)
+        x_high, x_low = split(by_row[row] + jnp.where(level == 0, heat, 0.0))
         made.append(
             jnp.dot(high, x_high, preferred_element_type=F32)
             + jnp.dot(high, x_low, preferred_element_type=F32)
@@ -206,17 +224,7 @@
     out[...] = jnp.swapaxes(jnp.stack(made), 0, 1)
 
 
-def last_kernel(
-    width, ids, flux, from_east_flux, weights, mask, inverse, before, parts, out, ocean,
-    window, picked, pick_sems, sems,
-):
-    entries = picked.shape[0]
-    picks = [
-        pltpu.make_async_copy(weights.at[ids[entries + i]], picked.at[i], pick_sems.at[i])
-        for i in range(entries)
-    ]
-    for pick in picks:
-        pick.start()
+def place_kernel(parts, out, sems):
     band = parts.shape[2]
     copies = [
         pltpu.make_async_copy(parts.at[b], out.at[:, pl.ds(b * band, band), :], sems.at[b])
@@ -224,21 +232,6 @@
     ]
     for copy in copies:
         copy.start()
-    for side, source in enumerate((flux, from_east_flux)):
-        for g in range(2):
-            at = (side * 2 + g) * band
-            window[at : at + band, :] = source[:, g * LANES : (g + 1) * LANES]
-    levels, rows, _ = before.shape
-    made = []
-    for row in range(rows):
-        total = jnp.zeros((LANES, LANES), F32)
-        for k in range(row * width, (row + 1) * width):
-            picks[k].wait()
-            total = total + picked[k] * window[pl.ds(ids[k], 1), :]
-        made.append(jnp.sum(total.T, axis=0, keepdims=True))
-    heat = mask[...].astype(F32) * jnp.concatenate(made, axis=0)
-    for level in range(levels):
-        ocean[level] = before[level] + inverse[level : level + 1, 0:1] * heat
     for copy in copies:
         copy.wait()
 
@@ -336,25 +329,22 @@
     group = jnp.remainder(src % ngroups - lon_index * groups, ngroups)
     flux_ids = group * aband + src // ngroups - sub_index * aband
     entries = src.shape[0]
-    before = kernel_call(
-        functools.partial(ocean_kernel, n_sub), shape(olev, olat_dev, olon_dev),
-        [SMEM] + [VMEM] * 9, VMEM, flops=8 * MIB, moved=MIB, name="ocean",
-    )(
-        place, ocean_temp, diffusivity, land_mask, ocean_inverse,
-        from_west, from_east, even_rows, odd_rows, folded,
-    )
-    returned, ocean_new = kernel_call(
-        functools.partial(last_kernel, width), (shape(lev_dev, alat, alon_dev), shape(olev, olat_dev, olon_dev)),
-        [SMEM] + [VMEM] * 2 + [HBM] + [VMEM] * 4, (HBM, VMEM),
+    ocean_new = kernel_call(
+        functools.partial(ocean_kernel, width, n_sub), shape(olev, olat_dev, olon_dev),
+        [SMEM] * 2 + [VMEM] * 2 + [HBM] + [VMEM] * 9, VMEM,
         scratch=[
             pltpu.VMEM((4 * aband, LANES), F32), pltpu.VMEM((entries, LANES, LANES), F32),
-            pltpu.SemaphoreType.DMA((entries,)), pltpu.SemaphoreType.DMA((n_sub,)),
+            pltpu.SemaphoreType.DMA((entries,)),
         ],
-        moved=6 * MIB, name="last",
+        flops=8 * MIB, moved=4 * MIB, name="ocean",
     )(
-        jnp.concatenate([flux_ids, a2o_wgt.reshape(-1)]), flux_band, east_flux, stays(weights),
-        land_mask, ocean_inverse, before, parts,
+        place, jnp.concatenate([flux_ids, a2o_wgt.reshape(-1)]), flux_band, east_flux, stays(weights),
+        ocean_temp, diffusivity, land_mask, ocean_inverse, from_west, from_east, even_rows, odd_rows, folded,
     )
+    returned = kernel_call(
+        place_kernel, shape(lev_dev, alat, alon_dev), [VMEM], HBM,
+        scratch=[pltpu.SemaphoreType.DMA((n_sub,))], moved=4 * MIB, name="place",
+    )(parts)
     return returned, ocean_new, flux_band
 
 

time: 89 us -> 86 us (0.966)
  waiting for transfers between devices: 50.9 us -> 46.6 us
  Pallas kernels: 16.6 us -> 18 us
    all_to_all x1, waiting for transfers between devices: 22.9 us -> 17.9 us  [per_device(): lax.all_to_all(solved, 'sub', split_axis=0, concat_axis=0, tiled=True)]
    pallas_call x2, Pallas kernels: 4.84 us -> 6.27 us  [the longest x1 4.9 us: per_device(): kernel_call(functools.partial(ocean_kernel, width, n_sub), shape(olev, ol...]
  transfers between devices with their start and end apart: 7 -> 7, of which waited for: 5 -> 5; matrix products, arithmetic and copies ran while one was open for 1% -> 1% of each run, Pallas kernels for 4% -> 9%
where the time goes in v3:
time: 86 us; the launch traced here: 85.6 us
  waiting for transfers between devices  46.6 us (54%)
  Pallas kernels  18 us (21%)
  starting transfers between devices  16.9 us (20%)
  local copies, waits for them, and re-layouts  3.15 us (4%)
    all_to_all x1, waiting for transfers between devices, per_device(): lax.all_to_all(solved, 'sub', split_axis=0, concat_axis=0, tiled=True)  17.9 us
    ppermute x1, waiting for transfers between devices, per_device(): even_rows = lax.ppermute(even_msg, ('lon', 'sub'), first)  16 us
    all_to_all x1, starting transfers between devices, per_device(): lax.all_to_all(advected, 'sub', split_axis=0, concat_axis=0, tiled=True)  7.51 us
    ppermute x1, waiting for transfers between devices, per_device(): east_flux = lax.ppermute(flux_band, 'lon', down)  5.41 us
    ppermute x1, waiting for transfers between devices, per_device(): from_east = lax.ppermute(west_msg, 'lon', down)  5.23 us
    pallas_call x1, Pallas kernels, per_device(): kernel_call(functools.partial(ocean_kernel, width, n_sub), shape(olev, ol...  4.9 us
    all_to_all x1, starting transfers between devices, per_device(): lax.all_to_all(solved, 'sub', split_axis=0, concat_axis=0, tiled=True)  3.75 us
    pallas_call x1, Pallas kernels, per_device(): kernel_call(advect_kernel, in_hbm(n_sub, aband, lev_dev, alon_dev), [VMEM...  3.58 us
  transfers between devices with their start and end apart: 7, of which 5 were waited for; matrix products, arithmetic and copies ran while one was open for 1% of the time, Pallas kernels for 9%

profile of v3, /device:TPU:7, one launch (start us, length us, event | category | flops | bytes accessed | tf_op | source)
XLA Modules:
  0.0 85.6 jit_solution(1565135540868209781)
XLA Ops:
  0.6 2.3 %edges.1 = (f32[32,128]{1,0:T(8,128)S(1)}, f32[24,128]{1,0:T(8,128)S(1)}, f32[16,128,256]{2,1,0:T(8,128)S(1)}) custom-call(f32[16,128,256]{2,1,0:T(8,128)} %atm_in.1, f32[256,128]{1,0:T(8,128)} %bitcast.6, s32[8,128]{1,0:T(8,128)} %mask_in.3), custom_call_target="tpu_custom_call" | custom-call | flops 2097152 | bytes 2097152 | tf_op jit(solution)/shard_map/edges/pallas_call | solution.py:278
  2.9 1.8 %collective-permute-start = (f32[32,128]{1,0:T(8,128)S(1)}, f32[32,128]{1,0:T(8,128)S(1)}, u32[]{:S(2)}, u32[]{:S(2)}) collective-permute-start(f32[32,128]{1,0:T(8,128)S(1)} %get-tuple-element.12), channel_id=1, source_target_pairs={{0,8},{8,16},{16,24},{24,32},{32,40},{40,48},{48,56},{56,64},{64,7... | collective-permute-start | bytes 49160 | tf_op jit(solution)/shard_map/ppermute | solution.py:288
  4.8 5.2 %collective-permute-done.1.from_east = f32[24,128]{1,0:T(8,128)S(1)} collective-permute-done((f32[24,128]{1,0:T(8,128)S(1)}, f32[24,128]{1,0:T(8,128)S(1)}, u32[]{:S(2)}, u32[]{:S(2)}) %collective-permute-start.1) | collective-permute-done | bytes 12320 | tf_op jit(solution)/shard_map/ppermute | solution.py:289
  10.0 3.6 %advect.1 = f32[8,16,16,256]{3,2,1,0:T(8,128)} custom-call(f32[16,128,256]{2,1,0:T(8,128)S(1)} %get-tuple-element.11.atm, f32[16,128,256]{2,1,0:T(8,128)S(1)} %copy-done.1, f32[32,128]{1,0:T(8,128)S(1)} %collective-permute-done.from_west, f32[24,128]{1,0:T(8,128)S(1)} %collective-permute-done.1.from_east), custom_call_target="tpu_custom_call" | custom-call | flops 10485760 | bytes 6291456 | tf_op jit(solution)/shard_map/advect/pallas_call | solution.py:291
  13.6 0.0 copy-start.9
  13.6 0.0 copy-start.5
  13.7 7.5 %all-to-all-start = ((f32[8,16,16,256]{3,2,1,0:T(8,128)}), f32[8,16,16,256]{3,2,1,0:T(8,128)S(1)}, u32[]{:S(2)}, u32[]{:S(2)}) async-start(f32[8,16,16,256]{3,2,1,0:T(8,128)} %advect.1), calls=%async_computation | async-start | bytes 4194304 | tf_op jit(solution)/shard_map/all_to_all | solution.py:299
  21.2 0.1 constant_dynamic-slice_fusion
  21.3 0.1 copy.21
  21.4 0.1 reshape.27
  21.5 0.1 copy.20
  21.6 0.1 reshape.26
  21.8 2.2 %copy-done = f32[64,128,128]{2,1,0:T(8,128)S(1)} copy-done((f32[64,128,128]{2,1,0:T(8,128)S(1)}, f32[64,128,128]{2,1,0:T(8,128)}, u32[]{:S(2)}) %copy-start) | copy-done | bytes 4194328
  23.9 2.6 %sst.1 = (f32[16,256]{1,0:T(8,128)S(1)}, f32[32,128]{1,0:T(8,128)S(1)}, f32[32,128]{1,0:T(8,128)S(1)}) custom-call(s32[1]{0:T(128)} %bitcast.place, s32[256]{0:T(256)S(1)} %pad_add_fusion.ids, f32[32,128]{1,0:T(8,128)S(1)} %collective-permute-done.from_west, f32[256,128]{1,0:T(8,128)S(1)} %bitcast.7, s32[8,128]{1,0:T(8,128)S(1)} %copy-done.5, ...), custom_call_target="tpu_custom_call" | custom-call | flops 8388608 | bytes 8388608 | tf_op jit(solution)/shard_map/sst/pallas_call | solution.py:305
  26.5 3.0 %collective-permute-start.2 = (f32[32,128]{1,0:T(8,128)S(1)}, f32[32,128]{1,0:T(8,128)S(1)}, u32[]{:S(2)}, u32[]{:S(2)}) collective-permute-start(f32[32,128]{1,0:T(8,128)S(1)} %get-tuple-element.15), channel_id=1, source_target_pairs={{0,1},{1,0},{2,3},{3,2},{4,5},{5,4},{6,7},{7,6},{8,9},{9,8},{10,11... | collective-permute-start | bytes 49160 | tf_op jit(solution)/shard_map/ppermute | solution.py:312
  29.6 0.7 collective-permute-start.3
  30.2 16.0 %collective-permute-done.2.even_rows = f32[32,128]{1,0:T(8,128)S(1)} collective-permute-done((f32[32,128]{1,0:T(8,128)S(1)}, f32[32,128]{1,0:T(8,128)S(1)}, u32[]{:S(2)}, u32[]{:S(2)}) %collective-permute-start.2) | collective-permute-done | bytes 16416 | tf_op jit(solution)/shard_map/ppermute | solution.py:312
  46.2 2.1 %all-to-all-done.columns = f32[8,16,16,256]{3,2,1,0:T(8,128)S(1)} async-done(((f32[8,16,16,256]{3,2,1,0:T(8,128)}), f32[8,16,16,256]{3,2,1,0:T(8,128)S(1)}, u32[]{:S(2)}, u32[]{:S(2)}) %all-to-all-start) | async-done | bytes 2097184 | tf_op jit(solution)/shard_map/all_to_all | solution.py:299
  48.3 3.3 %solve.1 = (f32[8,16,16,256]{3,2,1,0:T(8,128)}, f32[16,256]{1,0:T(8,128)}) custom-call(s32[1]{0:T(128)} %bitcast.place, f32[8,16,16,256]{3,2,1,0:T(8,128)S(1)} %all-to-all-done.columns, f32[8,128,128]{2,1,0:T(8,128)S(1)} %copy-done.3, f32[128,256]{1,0:T(8,128)S(1)} %copy-done.4, f32[16,256]{1,0:T(8,128)S(1)} %get-tuple-element.14.sst, ...), custom_call_target="tpu_custom_call" | custom-call | flops 419430400 | bytes 4194304 | tf_op jit(solution)/shard_map/solve/pallas_call | solution.py:316
  51.6 0.0 copy-start.7
  51.6 3.7 %all-to-all-start.1 = ((f32[8,16,16,256]{3,2,1,0:T(8,128)}), f32[8,16,16,256]{3,2,1,0:T(8,128)S(1)}, u32[]{:S(2)}, u32[]{:S(2)}) async-start(f32[8,16,16,256]{3,2,1,0:T(8,128)} %get-tuple-element.17), calls=%async_computation.1 | async-start | bytes 4194304 | tf_op jit(solution)/shard_map/all_to_all | solution.py:325
  55.4 0.1 copy.22
  55.5 0.1 reshape.28
  55.6 0.1 copy.23
  55.6 0.1 reshape.29
  55.8 0.1 collective-permute-start.4
  55.8 0.1 pad_add_fusion.1.ids
  55.9 0.1 rev.4.folded
  56.0 5.4 %collective-permute-done.4.from_east_flux = f32[16,256]{1,0:T(8,128)S(1)} collective-permute-done((f32[16,256]{1,0:T(8,128)S(1)}, f32[16,256]{1,0:T(8,128)S(1)}, u32[]{:S(2)}, u32[]{:S(2)}) %collective-permute-start.4) | collective-permute-done | bytes 16416 | tf_op jit(solution)/shard_map/ppermute | solution.py:326
  61.4 4.9 %ocean.1 = f32[32,8,128]{2,1,0:T(8,128)} custom-call(s32[1]{0:T(128)} %bitcast.place, s32[64]{0:T(128)S(1)} %pad_add_fusion.1.ids, f32[16,256]{1,0:T(8,128)S(1)} %copy-done.7, f32[16,256]{1,0:T(8,128)S(1)} %collective-permute-done.4.from_east_flux, f32[64,128,128]{2,1,0:T(8,128)} %weights.3, f32[32,8,128]{2,1,0:T(8,128)S(1)} %copy-done.2, ...), custom_call_target="tpu_custom_call" | custom-call | flops 8388608 | bytes 4194304 | tf_op jit(solution)/shard_map/ocean/pallas_call | solution.py:332
  66.3 17.9 %all-to-all-done.1.parts = f32[8,16,16,256]{3,2,1,0:T(8,128)S(1)} async-done(((f32[8,16,16,256]{3,2,1,0:T(8,128)}), f32[8,16,16,256]{3,2,1,0:T(8,128)S(1)}, u32[]{:S(2)}, u32[]{:S(2)}) %all-to-all-start.1) | async-done | bytes 2097184 | tf_op jit(solution)/shard_map/all_to_all | solution.py:325
  84.2 1.4 %place.1 = f32[16,128,256]{2,1,0:T(8,128)} custom-call(f32[8,16,16,256]{3,2,1,0:T(8,128)S(1)} %all-to-all-done.1.parts), custom_call_target="tpu_custom_call" | custom-call | bytes 4194304 | tf_op jit(solution)/shard_map/place/pallas_call | solution.py:344
  (28 shorter events, 0.1 us)
Async XLA Ops:
  0.6 9.4 %copy-start.1 = (f32[16,128,256]{2,1,0:T(8,128)S(1)}, f32[16,128,256]{2,1,0:T(8,128)}, u32[]{:S(2)}) copy-start(f32[16,128,256]{2,1,0:T(8,128)} %courant.1) | copy-start | bytes 6291460
  2.9 7.1 %collective-permute-start = (f32[32,128]{1,0:T(8,128)S(1)}, f32[32,128]{1,0:T(8,128)S(1)}, u32[]{:S(2)}, u32[]{:S(2)}) collective-permute-start(f32[32,128]{1,0:T(8,128)S(1)} %get-tuple-element.12), channel_id=1, source_target_pairs={{0,8},{8,16},{16,24},{24,32},{32,40},{40,48},{48,56},{56,64},{64,7... | collective-permute-start | bytes 49160 | tf_op jit(solution)/shard_map/ppermute | solution.py:288
  4.8 5.2 %collective-permute-start.1 = (f32[24,128]{1,0:T(8,128)S(1)}, f32[24,128]{1,0:T(8,128)S(1)}, u32[]{:S(2)}, u32[]{:S(2)}) collective-permute-start(f32[24,128]{1,0:T(8,128)S(1)} %get-tuple-element.13), channel_id=1, source_target_pairs={{8,0},{16,8},{24,16},{32,24},{40,32},{48,40},{56,48},{64,56},{72,6... | collective-permute-start | bytes 36872 | tf_op jit(solution)/shard_map/ppermute | solution.py:289
  13.6 7.6 %copy-start.9 = (s32[128,2,4]{0,2,1:T(4,128)S(1)}, s32[128,2,4]{0,2,1:T(4,128)}, u32[]{:S(2)}) copy-start(s32[128,2,4]{0,2,1:T(4,128)} %param.25) | copy-start | bytes 12292
  13.6 7.6 %copy-start.10 = (s32[128,2,4]{0,2,1:T(4,128)S(1)}, s32[128,2,4]{0,2,1:T(4,128)}, u32[]{:S(2)}) copy-start(s32[128,2,4]{0,2,1:T(4,128)} %param.24) | copy-start | bytes 12292
  13.6 8.1 %copy-start.2 = (f32[32,8,128]{2,1,0:T(8,128)S(1)}, f32[32,8,128]{2,1,0:T(8,128)}, u32[]{:S(2)}) copy-start(f32[32,8,128]{2,1,0:T(8,128)} %temp_in.1) | copy-start | bytes 393220
  13.6 8.1 %copy-start.5 = (s32[8,128]{1,0:T(8,128)S(1)}, s32[8,128]{1,0:T(8,128)}, u32[]{:S(2)}) copy-start(s32[8,128]{1,0:T(8,128)} %mask_in.3) | copy-start | bytes 12292
  13.7 34.6 %all-to-all-start = ((f32[8,16,16,256]{3,2,1,0:T(8,128)}), f32[8,16,16,256]{3,2,1,0:T(8,128)S(1)}, u32[]{:S(2)}, u32[]{:S(2)}) async-start(f32[8,16,16,256]{3,2,1,0:T(8,128)} %advect.1), calls=%async_computation | async-start | bytes 4194304 | tf_op jit(solution)/shard_map/all_to_all | solution.py:299
  21.7 2.2 %copy-start = (f32[64,128,128]{2,1,0:T(8,128)S(1)}, f32[64,128,128]{2,1,0:T(8,128)}, u32[]{:S(2)}) copy-start(f32[64,128,128]{2,1,0:T(8,128)} %weights.3) | copy-start | bytes 12582916
  23.9 24.3 %copy-start.3 = (f32[8,128,128]{2,1,0:T(8,128)S(1)}, f32[8,128,128]{2,1,0:T(8,128)}, u32[]{:S(2)}) copy-start(f32[8,128,128]{2,1,0:T(8,128)} %inverse.2) | copy-start | bytes 1572868
  23.9 24.3 %copy-start.4 = (f32[128,256]{1,0:T(8,128)S(1)}, f32[128,256]{1,0:T(8,128)}, u32[]{:S(2)}) copy-start(f32[128,256]{1,0:T(8,128)} %factor.1) | copy-start | bytes 393220
  26.5 19.7 %collective-permute-start.2 = (f32[32,128]{1,0:T(8,128)S(1)}, f32[32,128]{1,0:T(8,128)S(1)}, u32[]{:S(2)}, u32[]{:S(2)}) collective-permute-start(f32[32,128]{1,0:T(8,128)S(1)} %get-tuple-element.15), channel_id=1, source_target_pairs={{0,1},{1,0},{2,3},{3,2},{4,5},{5,4},{6,7},{7,6},{8,9},{9,8},{10,11... | collective-permute-start | bytes 49160 | tf_op jit(solution)/shard_map/ppermute | solution.py:312
  29.6 16.6 %collective-permute-start.3 = (f32[32,128]{1,0:T(8,128)S(1)}, f32[32,128]{1,0:T(8,128)S(1)}, u32[]{:S(2)}, u32[]{:S(2)}) collective-permute-start(f32[32,128]{1,0:T(8,128)S(1)} %get-tuple-element.16), channel_id=1, source_target_pairs={{1,2},{2,1},{3,4},{4,3},{5,6},{6,5},{7,127},{9,10},{10,9},{11,12},... | collective-permute-start | bytes 49160 | tf_op jit(solution)/shard_map/ppermute | solution.py:313
  51.6 3.8 %copy-start.11 = (s32[8,1,4]{0,2,1:T(4,128)S(1)}, s32[8,1,4]{0,2,1:T(4,128)}, u32[]{:S(2)}) copy-start(s32[8,1,4]{0,2,1:T(4,128)} %param.22) | copy-start | bytes 388
  51.6 4.0 %copy-start.12 = (s32[8,1,4]{0,2,1:T(4,128)S(1)}, s32[8,1,4]{0,2,1:T(4,128)}, u32[]{:S(2)}) copy-start(s32[8,1,4]{0,2,1:T(4,128)} %param.23) | copy-start | bytes 388
  51.6 4.2 %copy-start.7 = (f32[16,256]{1,0:T(8,128)S(1)}, f32[16,256]{1,0:T(8,128)}, u32[]{:S(2)}) copy-start(f32[16,256]{1,0:T(8,128)} %get-tuple-element.10.flux) | copy-start | bytes 49156
  51.6 9.8 %copy-start.6 = (f32[32,32]{1,0:T(8,128)S(1)}, f32[32,32]{1,0:T(8,128)}, u32[]{:S(2)}) copy-start(f32[32,32]{1,0:T(8,128)} %inverse.3) | copy-start | bytes 12292
  51.6 9.8 %copy-start.8 = (f32[8,128]{1,0:T(8,128)S(1)}, f32[8,128]{1,0:T(8,128)}, u32[]{:S(2)}) copy-start(f32[8,128]{1,0:T(8,128)} %diffusivity.1) | copy-start | bytes 12292
  51.6 32.6 %all-to-all-start.1 = ((f32[8,16,16,256]{3,2,1,0:T(8,128)}), f32[8,16,16,256]{3,2,1,0:T(8,128)S(1)}, u32[]{:S(2)}, u32[]{:S(2)}) async-start(f32[8,16,16,256]{3,2,1,0:T(8,128)} %get-tuple-element.17), calls=%async_computation.1 | async-start | bytes 4194304 | tf_op jit(solution)/shard_map/all_to_all | solution.py:325
  55.8 5.6 %collective-permute-start.4 = (f32[16,256]{1,0:T(8,128)S(1)}, f32[16,256]{1,0:T(8,128)S(1)}, u32[]{:S(2)}, u32[]{:S(2)}) collective-permute-start(f32[16,256]{1,0:T(8,128)S(1)} %copy-done.7), channel_id=1, source_target_pairs={{8,0},{16,8},{24,16},{32,24},{40,32},{48,40},{56,48},{64,56},{72,6... | collective-permute-start | bytes 49160 | tf_op jit(solution)/shard_map/ppermute | solution.py:326

commit v4 on v3

--- a/solution.py
+++ b/solution.py
@@ -14,7 +14,7 @@
 ANY = pl.BlockSpec(memory_space=pl.ANY)
 MIB = 1 << 20
 LANES = 128
-PIECES = 4
+PIECES = 8
 HBM = pl.BlockSpec(memory_space=pltpu.HBM)
 
 
@@ -80,11 +80,9 @@
     west_msg[...] = first.T[:24, :]
 
 
-def advect_kernel(atm, courant, from_west, from_east, out, west_cols, east_cols, held, sems):
+def base_kernel(atm, courant, out, west_speed, east_speed):
     levels, _, cells = atm.shape
     band = out.shape[1]
-    west_cols[...] = from_west[...].T
-    east_cols[...] = from_east[...].T
     lane = lax.broadcasted_iota(jnp.int32, (band, cells), 1)
 
     @pl.loop(0, out.shape[0])
@@ -94,20 +92,44 @@
         for level in range(levels):
             here = atm[level, rows, :]
             speed = courant[level, rows, :]
-            west = jnp.where(lane == 0, west_cols[rows, level : level + 1], pltpu.roll(here, 1, 1))
-            east = jnp.where(
-                lane == cells - 1, east_cols[rows, level : level + 1], pltpu.roll(here, cells - 1, 1)
-            )
+            west = jnp.where(lane == 0, 0.0, pltpu.roll(here, 1, 1))
+            east = jnp.where(lane == cells - 1, 0.0, pltpu.roll(here, cells - 1, 1))
             made.append(
                 here
                 - jnp.maximum(speed, 0.0) * (here - west)
                 - jnp.minimum(speed, 0.0) * (east - here)
             )
-        held[dest] = jnp.swapaxes(jnp.stack(made), 0, 1)
-        pltpu.make_async_copy(held.at[dest], out.at[dest], sems.at[dest]).start()
-
-    for dest in range(out.shape[0]):
-        pltpu.make_async_copy(held.at[dest], out.at[dest], sems.at[dest]).wait()
+        out[dest] = jnp.swapaxes(jnp.stack(made), 0, 1)
+
+    at = lax.broadcasted_iota(jnp.int32, (LANES, LANES), 1)
+    first = jnp.zeros((LANES, LANES), F32)
+    last = jnp.zeros((LANES, LANES), F32)
+    for level in range(levels):
+        first = jnp.where(at == level, courant[level, :, 0:1], first)
+        last = jnp.where(at == level, courant[level, :, cells - 1 : cells], last)
+    west_speed[...] = jnp.maximum(first.T[:levels, :], 0.0)
+    east_speed[...] = jnp.minimum(last.T[:levels, :], 0.0)
+
+
+def inflow_kernel(base, west_speed, east_speed, from_west, from_east, out, held, sems):
+    dests, band, levels, cells = base.shape
+    west = west_speed[...] * from_west[:levels, :]
+    east = -east_speed[...] * from_east[:levels, :]
+    lane = lax.broadcasted_iota(jnp.int32, (levels, LANES), 1)
+    copies = []
+    for dest in range(dests):
+        for row in range(band):
+            at = dest * band + row
+            held[dest, row, :, :LANES] = base[dest, row, :, :LANES] + jnp.where(
+                lane == 0, west[:, at : at + 1], 0.0
+            )
+            held[dest, row, :, cells - LANES :] = base[dest, row, :, cells - LANES :] + jnp.where(
+                lane == LANES - 1, east[:, at : at + 1], 0.0
+            )
+        copies.append(pltpu.make_async_copy(held.at[dest], out.at[dest], sems.at[dest]))
+        copies[-1].start()
+    for copy in copies:
+        copy.wait()
 
 
 def mat_vec(ids, first, count, source, weights):
@@ -143,25 +165,28 @@
     sub = place[0]
     groups, band, depth, cells = columns.shape
     levels = groups * depth
+    parts, step = out.shape[1], out.shape[3]
     high, low = split(inverse[sub])
     twice = jnp.concatenate([high, high], axis=1)
-
-    def solve_row(row, _):
-        here = columns[:, row].reshape(levels, cells)
-        x_high, x_low = split(here)
-        held[row] = jnp.dot(
-            twice, jnp.concatenate([x_high, x_low], axis=0), preferred_element_type=F32
-        ) + jnp.dot(low, x_high, preferred_element_type=F32)
-        return 0
-
-    lax.fori_loop(0, band, solve_row, 0, unroll=4)
     copies = []
-    for group in range(groups):
-        turned[group] = jnp.swapaxes(held[:, group * depth : (group + 1) * depth, :], 0, 1)
-        copies.append(pltpu.make_async_copy(turned.at[group], out.at[group], sems.at[group]))
-        copies[-1].start()
+    for part in range(parts):
+        for row in range(part * step, (part + 1) * step):
+            x_high, x_low = split(columns[:, row].reshape(levels, cells))
+            held[row] = jnp.dot(
+                twice, jnp.concatenate([x_high, x_low], axis=0), preferred_element_type=F32
+            ) + jnp.dot(low, x_high, preferred_element_type=F32)
+        for group in range(groups):
+            turned[group, part] = jnp.swapaxes(
+                held[part * step : (part + 1) * step, group * depth : (group + 1) * depth, :], 0, 1
+            )
+            copies.append(
+                pltpu.make_async_copy(
+                    turned.at[group, part], out.at[group, part], sems.at[group * parts + part]
+                )
+            )
+            copies[-1].start()
     rows = pl.ds(pl.multiple_of(sub * band, band), band)
-    flux[...] = factor[rows, :] * (sst[...] - turned[groups - 1, depth - 1])
+    flux[...] = factor[rows, :] * (sst[...] - held[:, levels - 1, :])
     for copy in copies:
         copy.wait()
 
@@ -225,13 +250,14 @@
 
 
 def place_kernel(parts, out, sems):
-    band = parts.shape[2]
-    copies = [
-        pltpu.make_async_copy(parts.at[b], out.at[:, pl.ds(b * band, band), :], sems.at[b])
-        for b in range(parts.shape[0])
-    ]
-    for copy in copies:
-        copy.start()
+    bands, pieces, _, step, _ = parts.shape
+    copies = []
+    for band in range(bands):
+        for piece in range(pieces):
+            at = band * pieces + piece
+            rows = pl.ds(at * step, step)
+            copies.append(pltpu.make_async_copy(parts.at[band, piece], out.at[:, rows, :], sems.at[at]))
+            copies[-1].start()
     for copy in copies:
         copy.wait()
 
@@ -288,14 +314,16 @@
     from_west = lax.ppermute(east_msg, "lon", up)
     from_east = lax.ppermute(west_msg, "lon", down)
 
+    base, west_speed, east_speed = kernel_call(
+        base_kernel,
+        (in_vmem(n_sub, aband, lev_dev, alon_dev), shape(lev_dev, LANES), shape(lev_dev, LANES)),
+        [VMEM] * 2, (VMEM,) * 3, flops=10 * MIB, moved=6 * MIB, name="base",
+    )(atm_here, courant)
     advected = kernel_call(
-        advect_kernel, in_hbm(n_sub, aband, lev_dev, alon_dev), [VMEM] * 4, HBM,
-        scratch=[
-            pltpu.VMEM((LANES, 32), F32), pltpu.VMEM((LANES, 24), F32),
-            pltpu.VMEM((n_sub, aband, lev_dev, alon_dev), F32), pltpu.SemaphoreType.DMA((n_sub,)),
-        ],
-        flops=10 * MIB, moved=6 * MIB, name="advect",
-    )(atm_here, courant, from_west, from_east)
+        inflow_kernel, in_hbm(n_sub, aband, lev_dev, alon_dev), [VMEM] * 5, HBM,
+        scratch=[pltpu.VMEM((n_sub, aband, lev_dev, alon_dev), F32), pltpu.SemaphoreType.DMA((n_sub,))],
+        flops=2 * MIB, moved=4 * MIB, name="inflow",
+    )(base, west_speed, east_speed, from_west, from_east)
     columns = lax.all_to_all(advected, "sub", split_axis=0, concat_axis=0, tiled=True)
 
     band_src = lax.dynamic_slice_in_dim(o2a_src, sub_index * aband, aband, 0).reshape(-1)
@@ -313,12 +341,14 @@
     odd_rows = lax.ppermute(odd_msg, ("lon", "sub"), second)
     folded = jnp.flip(odd_rows, axis=1)
 
+    step = 8
+    halves = aband // step
     solved, flux_band = kernel_call(
-        solve_kernel, (in_hbm(n_sub, lev_dev, aband, alon_dev), shape(aband, alon_dev)),
+        solve_kernel, (in_hbm(n_sub, halves, lev_dev, step, alon_dev), shape(aband, alon_dev)),
         [SMEM] + [VMEM] * 4 + [ANY] * 2, (HBM, VMEM),
         scratch=[
             pltpu.VMEM((aband, lev_dev * n_sub, alon_dev), F32),
-            pltpu.VMEM((n_sub, lev_dev, aband, alon_dev), F32), pltpu.SemaphoreType.DMA((n_sub,)),
+            pltpu.VMEM((n_sub, halves, lev_dev, step, alon_dev), F32), pltpu.SemaphoreType.DMA((n_sub * halves,)),
         ],
         flops=400 * MIB, moved=4 * MIB, name="solve",
     )(place, columns, column_inverse, heat_exchange_factor, sst, even_rows, odd_rows)
@@ -343,7 +373,7 @@
     )
     returned = kernel_call(
         place_kernel, shape(lev_dev, alat, alon_dev), [VMEM], HBM,
-        scratch=[pltpu.SemaphoreType.DMA((n_sub,))], moved=4 * MIB, name="place",
+        scratch=[pltpu.SemaphoreType.DMA((n_sub * halves,))], moved=4 * MIB, name="place",
     )(parts)
     return returned, ocean_new, flux_band
 

time: 86 us -> 85 us (0.988)
  waiting for transfers between devices: 46.6 us -> 45.4 us
    ppermute x1, waiting for transfers between devices: 5.23 us -> 2.64 us  [per_device(): from_east = lax.ppermute(west_msg, 'lon', down)]
    ppermute x1, waiting for transfers between devices: 16 us -> 18.3 us  [per_device(): even_rows = lax.ppermute(even_msg, ('lon', 'sub'), first)]
    all_to_all x1, waiting for transfers between devices: 2.08 us -> 0.93 us  [per_device(): lax.all_to_all(advected, 'sub', split_axis=0, concat_axis=0, tiled=True)]
    pallas_call x2 -> x3, Pallas kernels: 6.86 us -> 6.82 us  [the longest x1 2.65 us: per_device(): kernel_call(solve_kernel, (in_hbm(n_sub, halves, lev_dev, step, alon_dev)...]
  transfers between devices with their start and end apart: 7 -> 7, of which waited for: 5 -> 5; matrix products, arithmetic and copies ran while one was open for 1% -> 1% of each run, Pallas kernels for 9% -> 12%
where the time goes in v4:
time: 85 us; the launch traced here: 84.6 us
  waiting for transfers between devices  45.4 us (53%)
  Pallas kernels  18.2 us (21%)
  starting transfers between devices  16.9 us (20%)
  local copies, waits for them, and re-layouts  3.15 us (4%)
  between operations  0.85 us (1%)
    ppermute x1, waiting for transfers between devices, per_device(): even_rows = lax.ppermute(even_msg, ('lon', 'sub'), first)  18.3 us
    all_to_all x1, waiting for transfers between devices, per_device(): lax.all_to_all(solved, 'sub', split_axis=0, concat_axis=0, tiled=True)  18.1 us
    all_to_all x1, starting transfers between devices, per_device(): lax.all_to_all(advected, 'sub', split_axis=0, concat_axis=0, tiled=True)  7.51 us
    ppermute x1, waiting for transfers between devices, per_device(): east_flux = lax.ppermute(flux_band, 'lon', down)  5.41 us
    pallas_call x1, Pallas kernels, per_device(): kernel_call(functools.partial(ocean_kernel, width, n_sub), shape(olev, ol...  4.9 us
    all_to_all x1, starting transfers between devices, per_device(): lax.all_to_all(solved, 'sub', split_axis=0, concat_axis=0, tiled=True)  3.75 us
    ppermute x1, starting transfers between devices, per_device(): even_rows = lax.ppermute(even_msg, ('lon', 'sub'), first)  3.04 us
    pallas_call x1, Pallas kernels, per_device(): kernel_call(solve_kernel, (in_hbm(n_sub, halves, lev_dev, step, alon_dev)...  2.65 us
  transfers between devices with their start and end apart: 7, of which 5 were waited for; matrix products, arithmetic and copies ran while one was open for 1% of the time, Pallas kernels for 12%

profile of v4, /device:TPU:7, one launch (start us, length us, event | category | flops | bytes accessed | tf_op | source)
XLA Modules:
  0.0 84.6 jit_solution(4775235433297747965)
XLA Ops:
  0.6 2.5 %edges.1 = (f32[32,128]{1,0:T(8,128)S(1)}, f32[24,128]{1,0:T(8,128)S(1)}, f32[16,128,256]{2,1,0:T(8,128)S(1)}) custom-call(f32[16,128,256]{2,1,0:T(8,128)} %atm_in.1, f32[256,128]{1,0:T(8,128)} %bitcast.6, s32[8,128]{1,0:T(8,128)} %mask_in.3), custom_call_target="tpu_custom_call" | custom-call | flops 2097152 | bytes 2097152 | tf_op jit(solution)/shard_map/edges/pallas_call | solution.py:304
  3.1 1.8 %collective-permute-start = (f32[32,128]{1,0:T(8,128)S(1)}, f32[32,128]{1,0:T(8,128)S(1)}, u32[]{:S(2)}, u32[]{:S(2)}) collective-permute-start(f32[32,128]{1,0:T(8,128)S(1)} %get-tuple-element.18), channel_id=1, source_target_pairs={{0,8},{8,16},{16,24},{24,32},{32,40},{40,48},{48,56},{56,64},{64,7... | collective-permute-start | bytes 49160 | tf_op jit(solution)/shard_map/ppermute | solution.py:314
  5.0 2.6 %base.1 = (f32[8,16,16,256]{3,2,1,0:T(8,128)S(1)}, f32[16,128]{1,0:T(8,128)S(1)}, f32[16,128]{1,0:T(8,128)S(1)}) custom-call(f32[16,128,256]{2,1,0:T(8,128)S(1)} %get-tuple-element.14.atm, f32[16,128,256]{2,1,0:T(8,128)S(1)} %copy-done.1), custom_call_target="tpu_custom_call" | custom-call | flops 10485760 | bytes 6291456 | tf_op jit(solution)/shard_map/base/pallas_call | solution.py:317
  7.6 2.6 %collective-permute-done.1.from_east = f32[24,128]{1,0:T(8,128)S(1)} collective-permute-done((f32[24,128]{1,0:T(8,128)S(1)}, f32[24,128]{1,0:T(8,128)S(1)}, u32[]{:S(2)}, u32[]{:S(2)}) %collective-permute-start.1) | collective-permute-done | bytes 12320 | tf_op jit(solution)/shard_map/ppermute | solution.py:315
  10.2 1.6 %inflow.1 = f32[8,16,16,256]{3,2,1,0:T(8,128)} custom-call(f32[8,16,16,256]{3,2,1,0:T(8,128)S(1)} %get-tuple-element.15.base, f32[16,128]{1,0:T(8,128)S(1)} %get-tuple-element.16.west_speed, f32[16,128]{1,0:T(8,128)S(1)} %get-tuple-element.17.east_speed, f32[32,128]{1,0:T(8,128)S(1)} %collective-permute-done.from_west, ...), custom_call_target="tpu_custom_call" | custom-call | flops 2097152 | bytes 4194304 | tf_op jit(solution)/shard_map/inflow/pallas_call | solution.py:322
  11.8 0.0 copy-start.9
  11.9 7.5 %all-to-all-start = ((f32[8,16,16,256]{3,2,1,0:T(8,128)}), f32[8,16,16,256]{3,2,1,0:T(8,128)S(1)}, u32[]{:S(2)}, u32[]{:S(2)}) async-start(f32[8,16,16,256]{3,2,1,0:T(8,128)} %inflow.1), calls=%async_computation | async-start | bytes 4194304 | tf_op jit(solution)/shard_map/all_to_all | solution.py:327
  19.4 0.1 constant_dynamic-slice_fusion
  19.5 0.1 copy.21
  19.6 0.1 reshape.27
  19.7 0.1 copy.20
  19.8 0.1 reshape.26
  20.0 2.2 %copy-done = f32[64,128,128]{2,1,0:T(8,128)S(1)} copy-done((f32[64,128,128]{2,1,0:T(8,128)S(1)}, f32[64,128,128]{2,1,0:T(8,128)}, u32[]{:S(2)}) %copy-start) | copy-done | bytes 4194328
  22.1 2.6 %sst.1 = (f32[16,256]{1,0:T(8,128)S(1)}, f32[32,128]{1,0:T(8,128)S(1)}, f32[32,128]{1,0:T(8,128)S(1)}) custom-call(s32[1]{0:T(128)} %bitcast.place, s32[256]{0:T(256)S(1)} %pad_add_fusion.ids, f32[32,128]{1,0:T(8,128)S(1)} %collective-permute-done.from_west, f32[256,128]{1,0:T(8,128)S(1)} %bitcast.7, s32[8,128]{1,0:T(8,128)S(1)} %copy-done.5, ...), custom_call_target="tpu_custom_call" | custom-call | flops 8388608 | bytes 8388608 | tf_op jit(solution)/shard_map/sst/pallas_call | solution.py:333
  24.7 3.0 %collective-permute-start.2 = (f32[32,128]{1,0:T(8,128)S(1)}, f32[32,128]{1,0:T(8,128)S(1)}, u32[]{:S(2)}, u32[]{:S(2)}) collective-permute-start(f32[32,128]{1,0:T(8,128)S(1)} %get-tuple-element.21), channel_id=1, source_target_pairs={{0,1},{1,0},{2,3},{3,2},{4,5},{5,4},{6,7},{7,6},{8,9},{9,8},{10,11... | collective-permute-start | bytes 49160 | tf_op jit(solution)/shard_map/ppermute | solution.py:340
  27.8 0.7 collective-permute-start.3
  28.4 18.3 %collective-permute-done.2.even_rows = f32[32,128]{1,0:T(8,128)S(1)} collective-permute-done((f32[32,128]{1,0:T(8,128)S(1)}, f32[32,128]{1,0:T(8,128)S(1)}, u32[]{:S(2)}, u32[]{:S(2)}) %collective-permute-start.2) | collective-permute-done | bytes 16416 | tf_op jit(solution)/shard_map/ppermute | solution.py:340
  46.7 0.9 %all-to-all-done.columns = f32[8,16,16,256]{3,2,1,0:T(8,128)S(1)} async-done(((f32[8,16,16,256]{3,2,1,0:T(8,128)}), f32[8,16,16,256]{3,2,1,0:T(8,128)S(1)}, u32[]{:S(2)}, u32[]{:S(2)}) %all-to-all-start) | async-done | bytes 2097184 | tf_op jit(solution)/shard_map/all_to_all | solution.py:327
  47.7 2.7 %solve.1 = (f32[8,2,16,8,256]{4,3,2,1,0:T(8,128)}, f32[16,256]{1,0:T(8,128)}) custom-call(s32[1]{0:T(128)} %bitcast.place, f32[8,16,16,256]{3,2,1,0:T(8,128)S(1)} %all-to-all-done.columns, f32[8,128,128]{2,1,0:T(8,128)S(1)} %copy-done.3, f32[128,256]{1,0:T(8,128)S(1)} %copy-done.4, f32[16,256]{1,0:T(8,128)S(1)} %get-tuple-element.20.sst, ...), custom_call_target="tpu_custom_call" | custom-call | flops 419430400 | bytes 4194304 | tf_op jit(solution)/shard_map/solve/pallas_call | solution.py:346
  50.4 0.0 copy-start.7
  50.4 3.7 %all-to-all-start.1 = ((f32[8,2,16,8,256]{4,3,2,1,0:T(8,128)}), f32[8,2,16,8,256]{4,3,2,1,0:T(8,128)S(1)}, u32[]{:S(2)}, u32[]{:S(2)}) async-start(f32[8,2,16,8,256]{4,3,2,1,0:T(8,128)} %get-tuple-element.23), calls=%async_computation.1 | async-start | bytes 4194304 | tf_op jit(solution)/shard_map/all_to_all | solution.py:355
  54.2 0.1 copy.22
  54.2 0.1 reshape.28
  54.3 0.1 copy.23
  54.4 0.1 reshape.29
  54.5 0.1 collective-permute-start.4
  54.6 0.1 pad_add_fusion.1.ids
  54.7 0.1 rev.4.folded
  54.8 5.4 %collective-permute-done.4.from_east_flux = f32[16,256]{1,0:T(8,128)S(1)} collective-permute-done((f32[16,256]{1,0:T(8,128)S(1)}, f32[16,256]{1,0:T(8,128)S(1)}, u32[]{:S(2)}, u32[]{:S(2)}) %collective-permute-start.4) | collective-permute-done | bytes 16416 | tf_op jit(solution)/shard_map/ppermute | solution.py:356
  60.2 4.9 %ocean.1 = f32[32,8,128]{2,1,0:T(8,128)} custom-call(s32[1]{0:T(128)} %bitcast.place, s32[64]{0:T(128)S(1)} %pad_add_fusion.1.ids, f32[16,256]{1,0:T(8,128)S(1)} %copy-done.7, f32[16,256]{1,0:T(8,128)S(1)} %collective-permute-done.4.from_east_flux, f32[64,128,128]{2,1,0:T(8,128)} %weights.3, f32[32,8,128]{2,1,0:T(8,128)S(1)} %copy-done.2, ...), custom_call_target="tpu_custom_call" | custom-call | flops 8388608 | bytes 4194304 | tf_op jit(solution)/shard_map/ocean/pallas_call | solution.py:362
  65.1 18.1 %all-to-all-done.1.parts = f32[8,2,16,8,256]{4,3,2,1,0:T(8,128)S(1)} async-done(((f32[8,2,16,8,256]{4,3,2,1,0:T(8,128)}), f32[8,2,16,8,256]{4,3,2,1,0:T(8,128)S(1)}, u32[]{:S(2)}, u32[]{:S(2)}) %all-to-all-start.1) | async-done | bytes 2097184 | tf_op jit(solution)/shard_map/all_to_all | solution.py:355
  83.2 1.4 %place.1 = f32[16,128,256]{2,1,0:T(8,128)} custom-call(f32[8,2,16,8,256]{4,3,2,1,0:T(8,128)S(1)} %all-to-all-done.1.parts), custom_call_target="tpu_custom_call" | custom-call | bytes 4194304 | tf_op jit(solution)/shard_map/place/pallas_call | solution.py:374
  (29 shorter events, 0.1 us)
Async XLA Ops:
  0.6 4.4 %copy-start.1 = (f32[16,128,256]{2,1,0:T(8,128)S(1)}, f32[16,128,256]{2,1,0:T(8,128)}, u32[]{:S(2)}) copy-start(f32[16,128,256]{2,1,0:T(8,128)} %courant.1) | copy-start | bytes 6291460
  3.1 7.1 %collective-permute-start = (f32[32,128]{1,0:T(8,128)S(1)}, f32[32,128]{1,0:T(8,128)S(1)}, u32[]{:S(2)}, u32[]{:S(2)}) collective-permute-start(f32[32,128]{1,0:T(8,128)S(1)} %get-tuple-element.18), channel_id=1, source_target_pairs={{0,8},{8,16},{16,24},{24,32},{32,40},{40,48},{48,56},{56,64},{64,7... | collective-permute-start | bytes 49160 | tf_op jit(solution)/shard_map/ppermute | solution.py:314
  5.0 5.2 %collective-permute-start.1 = (f32[24,128]{1,0:T(8,128)S(1)}, f32[24,128]{1,0:T(8,128)S(1)}, u32[]{:S(2)}, u32[]{:S(2)}) collective-permute-start(f32[24,128]{1,0:T(8,128)S(1)} %get-tuple-element.19), channel_id=1, source_target_pairs={{8,0},{16,8},{24,16},{32,24},{40,32},{48,40},{56,48},{64,56},{72,6... | collective-permute-start | bytes 36872 | tf_op jit(solution)/shard_map/ppermute | solution.py:315
  11.8 7.6 %copy-start.9 = (s32[128,2,4]{0,2,1:T(4,128)S(1)}, s32[128,2,4]{0,2,1:T(4,128)}, u32[]{:S(2)}) copy-start(s32[128,2,4]{0,2,1:T(4,128)} %param.25) | copy-start | bytes 12292
  11.8 7.6 %copy-start.10 = (s32[128,2,4]{0,2,1:T(4,128)S(1)}, s32[128,2,4]{0,2,1:T(4,128)}, u32[]{:S(2)}) copy-start(s32[128,2,4]{0,2,1:T(4,128)} %param.24) | copy-start | bytes 12292
  11.8 8.1 %copy-start.2 = (f32[32,8,128]{2,1,0:T(8,128)S(1)}, f32[32,8,128]{2,1,0:T(8,128)}, u32[]{:S(2)}) copy-start(f32[32,8,128]{2,1,0:T(8,128)} %temp_in.1) | copy-start | bytes 393220
  11.8 8.1 %copy-start.5 = (s32[8,128]{1,0:T(8,128)S(1)}, s32[8,128]{1,0:T(8,128)}, u32[]{:S(2)}) copy-start(s32[8,128]{1,0:T(8,128)} %mask_in.3) | copy-start | bytes 12292
  11.9 35.8 %all-to-all-start = ((f32[8,16,16,256]{3,2,1,0:T(8,128)}), f32[8,16,16,256]{3,2,1,0:T(8,128)S(1)}, u32[]{:S(2)}, u32[]{:S(2)}) async-start(f32[8,16,16,256]{3,2,1,0:T(8,128)} %inflow.1), calls=%async_computation | async-start | bytes 4194304 | tf_op jit(solution)/shard_map/all_to_all | solution.py:327
  20.0 2.2 %copy-start = (f32[64,128,128]{2,1,0:T(8,128)S(1)}, f32[64,128,128]{2,1,0:T(8,128)}, u32[]{:S(2)}) copy-start(f32[64,128,128]{2,1,0:T(8,128)} %weights.3) | copy-start | bytes 12582916
  22.1 25.5 %copy-start.3 = (f32[8,128,128]{2,1,0:T(8,128)S(1)}, f32[8,128,128]{2,1,0:T(8,128)}, u32[]{:S(2)}) copy-start(f32[8,128,128]{2,1,0:T(8,128)} %inverse.2) | copy-start | bytes 1572868
  22.1 25.5 %copy-start.4 = (f32[128,256]{1,0:T(8,128)S(1)}, f32[128,256]{1,0:T(8,128)}, u32[]{:S(2)}) copy-start(f32[128,256]{1,0:T(8,128)} %factor.1) | copy-start | bytes 393220
  24.7 22.0 %collective-permute-start.2 = (f32[32,128]{1,0:T(8,128)S(1)}, f32[32,128]{1,0:T(8,128)S(1)}, u32[]{:S(2)}, u32[]{:S(2)}) collective-permute-start(f32[32,128]{1,0:T(8,128)S(1)} %get-tuple-element.21), channel_id=1, source_target_pairs={{0,1},{1,0},{2,3},{3,2},{4,5},{5,4},{6,7},{7,6},{8,9},{9,8},{10,11... | collective-permute-start | bytes 49160 | tf_op jit(solution)/shard_map/ppermute | solution.py:340
  27.8 19.0 %collective-permute-start.3 = (f32[32,128]{1,0:T(8,128)S(1)}, f32[32,128]{1,0:T(8,128)S(1)}, u32[]{:S(2)}, u32[]{:S(2)}) collective-permute-start(f32[32,128]{1,0:T(8,128)S(1)} %get-tuple-element.22), channel_id=1, source_target_pairs={{1,2},{2,1},{3,4},{4,3},{5,6},{6,5},{7,127},{9,10},{10,9},{11,12},... | collective-permute-start | bytes 49160 | tf_op jit(solution)/shard_map/ppermute | solution.py:341
  50.3 3.8 %copy-start.11 = (s32[8,1,4]{0,2,1:T(4,128)S(1)}, s32[8,1,4]{0,2,1:T(4,128)}, u32[]{:S(2)}) copy-start(s32[8,1,4]{0,2,1:T(4,128)} %param.22) | copy-start | bytes 388
  50.3 4.0 %copy-start.12 = (s32[8,1,4]{0,2,1:T(4,128)S(1)}, s32[8,1,4]{0,2,1:T(4,128)}, u32[]{:S(2)}) copy-start(s32[8,1,4]{0,2,1:T(4,128)} %param.23) | copy-start | bytes 388
  50.4 4.2 %copy-start.7 = (f32[16,256]{1,0:T(8,128)S(1)}, f32[16,256]{1,0:T(8,128)}, u32[]{:S(2)}) copy-start(f32[16,256]{1,0:T(8,128)} %get-tuple-element.13.flux) | copy-start | bytes 49156
  50.4 9.8 %copy-start.6 = (f32[32,32]{1,0:T(8,128)S(1)}, f32[32,32]{1,0:T(8,128)}, u32[]{:S(2)}) copy-start(f32[32,32]{1,0:T(8,128)} %inverse.3) | copy-start | bytes 12292
  50.4 9.8 %copy-start.8 = (f32[8,128]{1,0:T(8,128)S(1)}, f32[8,128]{1,0:T(8,128)}, u32[]{:S(2)}) copy-start(f32[8,128]{1,0:T(8,128)} %diffusivity.1) | copy-start | bytes 12292
  50.4 32.8 %all-to-all-start.1 = ((f32[8,2,16,8,256]{4,3,2,1,0:T(8,128)}), f32[8,2,16,8,256]{4,3,2,1,0:T(8,128)S(1)}, u32[]{:S(2)}, u32[]{:S(2)}) async-start(f32[8,2,16,8,256]{4,3,2,1,0:T(8,128)} %get-tuple-element.23), calls=%async_computation.1 | async-start | bytes 4194304 | tf_op jit(solution)/shard_map/all_to_all | solution.py:355
  54.5 5.6 %collective-permute-start.4 = (f32[16,256]{1,0:T(8,128)S(1)}, f32[16,256]{1,0:T(8,128)S(1)}, u32[]{:S(2)}, u32[]{:S(2)}) collective-permute-start(f32[16,256]{1,0:T(8,128)S(1)} %copy-done.7), channel_id=1, source_target_pairs={{8,0},{16,8},{24,16},{32,24},{40,32},{48,40},{56,48},{64,56},{72,6... | collective-permute-start | bytes 49160 | tf_op jit(solution)/shard_map/ppermute | solution.py:356

commit v5 on v4

--- a/solution.py
+++ b/solution.py
@@ -14,7 +14,7 @@
 ANY = pl.BlockSpec(memory_space=pl.ANY)
 MIB = 1 << 20
 LANES = 128
-PIECES = 8
+PIECES = 4
 HBM = pl.BlockSpec(memory_space=pltpu.HBM)
 
 
@@ -52,7 +52,7 @@
     return high, (value - high.astype(F32)).astype(BF16)
 
 
-def edges_kernel(atm_in, ocean_in, mask_in, east_msg, west_msg, atm, ocean, mask, sems):
+def edges_kernel(place, atm_in, ocean_in, mask_in, east_msg, west_msg, even_msg, odd_msg, atm, ocean, mask, sems):
     levels, rows, cells = atm.shape
     step = levels // PIECES
     pieces = [pl.ds(piece * step, step) for piece in range(PIECES)]
@@ -64,20 +64,35 @@
     lane = lax.broadcasted_iota(jnp.int32, (LANES, LANES), 1)
     last = jnp.zeros((LANES, LANES), F32)
     first = jnp.zeros((LANES, LANES), F32)
+
+    def gather(at, low, high, first, last):
+        turned = pltpu.roll(jnp.where(lane == LANES - 1, high, low), at, 1)
+        return (
+            jnp.where(lane == at, turned, first),
+            jnp.where(lane == (at + LANES - 1) % LANES, turned, last),
+        )
+
     for piece in range(PIECES):
         copies[piece].wait()
         for level in range(piece * step, (piece + 1) * step):
-            last = jnp.where(lane == level, atm[level, :, cells - 1 : cells], last)
-            first = jnp.where(lane == level, atm[level, :, 0:1], first)
+            first, last = gather(
+                level, atm[level, :, :LANES], atm[level, :, cells - LANES :], first, last
+            )
     for copy in copies[PIECES:]:
         copy.wait()
     for part in range(2):
-        tile = slice(part * LANES, (part + 1) * LANES)
-        last = jnp.where(lane == levels + part, ocean[tile, LANES - 1 : LANES], last)
-        first = jnp.where(lane == levels + part, ocean[tile, 0:1], first)
+        tile = ocean[part * LANES : (part + 1) * LANES, :]
+        first, last = gather(levels + part, tile, tile, first, last)
+    last = pltpu.roll(last, 1, 1)
     east_msg[:24, :] = last.T[:24, :]
     east_msg[24:, :] = mask[...].astype(F32) * ocean[:8, :]
     west_msg[...] = first.T[:24, :]
+    tile_rows = mask.shape[0]
+    tile = ocean[...].reshape(-1, tile_rows, LANES)
+    even = lax.rem(place[0], 2) == 0
+    low, top = tile[:, 0, :], tile[:, tile_rows - 1, :]
+    even_msg[...] = jnp.where(even, top, low)
+    odd_msg[...] = jnp.where(even, low, top)
 
 
 def base_kernel(atm, courant, out, west_speed, east_speed):
@@ -141,13 +156,7 @@
     return jnp.sum(total.T, axis=0, keepdims=True)
 
 
-def sst_kernel(width, place, ids, from_west, ocean, mask, weights, sst, even_msg, odd_msg, window, halves):
-    tile_rows = mask.shape[0]
-    tile = ocean[...].reshape(-1, tile_rows, LANES)
-    even = lax.rem(place[0], 2) == 0
-    low, top = tile[:, 0, :], tile[:, tile_rows - 1, :]
-    even_msg[...] = jnp.where(even, top, low)
-    odd_msg[...] = jnp.where(even, low, top)
+def sst_kernel(width, ids, from_west, ocean, mask, weights, sst, window, halves):
     window[:8, :] = from_west[24:32, :]
     window[8:, :] = mask[...].astype(F32) * ocean[:8, :]
     rows = sst.shape[0]
@@ -161,20 +170,20 @@
         sst[:, g * LANES : (g + 1) * LANES] = halves[g]
 
 
-def solve_kernel(place, columns, inverse, factor, sst, even_rows, odd_rows, out, flux, held, turned, sems):
+def solve_kernel(place, columns, inverse, factor, sst, out, flux, held, turned, sems):
     sub = place[0]
     groups, band, depth, cells = columns.shape
     levels = groups * depth
     parts, step = out.shape[1], out.shape[3]
     high, low = split(inverse[sub])
-    twice = jnp.concatenate([high, high], axis=1)
+    thrice = jnp.concatenate([high, high, low], axis=1)
     copies = []
     for part in range(parts):
         for row in range(part * step, (part + 1) * step):
             x_high, x_low = split(columns[:, row].reshape(levels, cells))
             held[row] = jnp.dot(
-                twice, jnp.concatenate([x_high, x_low], axis=0), preferred_element_type=F32
-            ) + jnp.dot(low, x_high, preferred_element_type=F32)
+                thrice, jnp.concatenate([x_high, x_low, x_high], axis=0), preferred_element_type=F32
+            )
         for group in range(groups):
             turned[group, part] = jnp.swapaxes(
                 held[part * step : (part + 1) * step, group * depth : (group + 1) * depth, :], 0, 1
@@ -301,18 +310,24 @@
     ocean_flat = ocean_temp.reshape(olev * olat_dev, olon_dev)
     place = jnp.reshape(sub_index, (1,))
 
-    east_msg, west_msg, atm_here = kernel_call(
-        edges_kernel, (shape(32, LANES), shape(24, LANES), in_vmem(lev_dev, alat, alon_dev)), [HBM] * 3, (VMEM,) * 3,
+    east_msg, west_msg, even_msg, odd_msg, atm_here = kernel_call(
+        edges_kernel,
+        (shape(32, LANES), shape(24, LANES), shape(olev, LANES), shape(olev, LANES), in_vmem(lev_dev, alat, alon_dev)),
+        [SMEM] + [HBM] * 3, (VMEM,) * 5,
         scratch=[
             pltpu.VMEM(ocean_flat.shape, F32), pltpu.VMEM(land_mask.shape, land_mask.dtype),
             pltpu.SemaphoreType.DMA((PIECES + 2,)),
         ],
         flops=2 * MIB, moved=2 * MIB, name="edges",
-    )(stays(atm_tracer), stays(ocean_flat), stays(land_mask))
+    )(place, stays(atm_tracer), stays(ocean_flat), stays(land_mask))
     up = [(i, (i + 1) % n_lon) for i in range(n_lon)]
     down = [(b, a) for a, b in up]
     from_west = lax.ppermute(east_msg, "lon", up)
     from_east = lax.ppermute(west_msg, "lon", down)
+
+    first, second = pair_exchanges(n_lon, n_sub)
+    even_rows = lax.ppermute(even_msg, ("lon", "sub"), first)
+    odd_rows = lax.ppermute(odd_msg, ("lon", "sub"), second)
 
     base, west_speed, east_speed = kernel_call(
         base_kernel,
@@ -330,28 +345,24 @@
     band_wgt = lax.dynamic_slice_in_dim(o2a_wgt, sub_index * aband, aband, 0).reshape(-1)
     tile = jnp.remainder(band_src % n_lon - lon_index + 1, n_lon)
     sea_ids = tile * olat_dev + band_src // n_lon - sub_index * olat_dev
-    sst, even_msg, odd_msg = kernel_call(
-        functools.partial(sst_kernel, width),
-        (shape(aband, alon_dev), shape(olev, LANES), shape(olev, LANES)), [SMEM] * 2 + [VMEM] * 4, (VMEM,) * 3,
+    sst = kernel_call(
+        functools.partial(sst_kernel, width), shape(aband, alon_dev), [SMEM] + [VMEM] * 4, VMEM,
         scratch=[pltpu.VMEM((2 * olat_dev, LANES), F32), pltpu.VMEM((groups, aband, LANES), F32)],
         flops=8 * MIB, moved=8 * MIB, name="sst",
-    )(place, jnp.concatenate([sea_ids, band_wgt]), from_west, ocean_flat, land_mask, weights)
-    first, second = pair_exchanges(n_lon, n_sub)
-    even_rows = lax.ppermute(even_msg, ("lon", "sub"), first)
-    odd_rows = lax.ppermute(odd_msg, ("lon", "sub"), second)
-    folded = jnp.flip(odd_rows, axis=1)
-
+    )(jnp.concatenate([sea_ids, band_wgt]), from_west, ocean_flat, land_mask, weights)
     step = 8
     halves = aband // step
     solved, flux_band = kernel_call(
         solve_kernel, (in_hbm(n_sub, halves, lev_dev, step, alon_dev), shape(aband, alon_dev)),
-        [SMEM] + [VMEM] * 4 + [ANY] * 2, (HBM, VMEM),
+        [SMEM] + [VMEM] * 4, (HBM, VMEM),
         scratch=[
             pltpu.VMEM((aband, lev_dev * n_sub, alon_dev), F32),
             pltpu.VMEM((n_sub, halves, lev_dev, step, alon_dev), F32), pltpu.SemaphoreType.DMA((n_sub * halves,)),
         ],
         flops=400 * MIB, moved=4 * MIB, name="solve",
-    )(place, columns, column_inverse, heat_exchange_factor, sst, even_rows, odd_rows)
+    )(place, columns, column_inverse, heat_exchange_factor, sst)
+    solved, even_rows, odd_rows = lax.optimization_barrier((solved, even_rows, odd_rows))
+    folded = jnp.flip(odd_rows, axis=1)
     parts = lax.all_to_all(solved, "sub", split_axis=0, concat_axis=0, tiled=True)
     east_flux = lax.ppermute(flux_band, "lon", down)
 

time: 85 us -> 84.6 us (level)
    all_to_all x1, waiting for transfers between devices: 0.93 us -> 19.4 us  [per_device(): lax.all_to_all(advected, 'sub', split_axis=0, concat_axis=0, tiled=True)]
    ppermute x1, waiting for transfers between devices: 18.3 us -> 0.01 us  [per_device(): even_rows = lax.ppermute(even_msg, ('lon', 'sub'), first)]
  transfers between devices with their start and end apart: 7 -> 7, of which waited for: 5 -> 4; matrix products, arithmetic and copies ran while one was open for 1% -> 1% of each run, Pallas kernels for 12% -> 15%
where the time goes in v5:
time: 84.6 us; the launch traced here: 84.2 us
  waiting for transfers between devices  45.6 us (54%)
  Pallas kernels  17.7 us (21%)
  starting transfers between devices  16.8 us (20%)
  local copies, waits for them, and re-layouts  3.15 us (4%)
  between operations  0.88 us (1%)
    all_to_all x1, waiting for transfers between devices, per_device(): lax.all_to_all(advected, 'sub', split_axis=0, concat_axis=0, tiled=True)  19.4 us
    all_to_all x1, waiting for transfers between devices, per_device(): lax.all_to_all(solved, 'sub', split_axis=0, concat_axis=0, tiled=True)  18.1 us
    all_to_all x1, starting transfers between devices, per_device(): lax.all_to_all(advected, 'sub', split_axis=0, concat_axis=0, tiled=True)  7.51 us
    ppermute x1, waiting for transfers between devices, per_device(): east_flux = lax.ppermute(flux_band, 'lon', down)  5.41 us
    pallas_call x1, Pallas kernels, per_device(): kernel_call(functools.partial(ocean_kernel, width, n_sub), shape(olev, ol...  4.9 us
    all_to_all x1, starting transfers between devices, per_device(): lax.all_to_all(solved, 'sub', split_axis=0, concat_axis=0, tiled=True)  3.75 us
    ppermute x1, starting transfers between devices, per_device(): even_rows = lax.ppermute(even_msg, ('lon', 'sub'), first)  2.97 us
    ppermute x1, waiting for transfers between devices, per_device(): from_east = lax.ppermute(west_msg, 'lon', down)  2.64 us
  transfers between devices with their start and end apart: 7, of which 4 were waited for; matrix products, arithmetic and copies ran while one was open for 1% of the time, Pallas kernels for 15%

profile of v5, /device:TPU:7, one launch (start us, length us, event | category | flops | bytes accessed | tf_op | source)
XLA Modules:
  0.0 84.2 jit_solution(10128709464172287008)
XLA Ops:
  0.6 2.1 %edges.1 = (f32[32,128]{1,0:T(8,128)S(1)}, f32[24,128]{1,0:T(8,128)S(1)}, f32[32,128]{1,0:T(8,128)S(1)}, f32[32,128]{1,0:T(8,128)S(1)}, f32[16,128,256]{2,1,0:T(8,128)S(1)}) custom-call(s32[1]{0:T(128)} %bitcast.place, f32[16,128,256]{2,1,0:T(8,128)} %atm_in.1, f32[256,128]{1,0:T(8,128)} %bitcast.6, s32[8,128]{1,0:T(8,128)} %mask_in.3), custom_call_target="tpu_custom_call" | custom-call | flops 2097152 | bytes 2097152 | tf_op jit(solution)/shard_map/edges/pallas_call | solution.py:313
  2.7 1.8 %collective-permute-start = (f32[32,128]{1,0:T(8,128)S(1)}, f32[32,128]{1,0:T(8,128)S(1)}, u32[]{:S(2)}, u32[]{:S(2)}) collective-permute-start(f32[32,128]{1,0:T(8,128)S(1)} %get-tuple-element.20), channel_id=1, source_target_pairs={{0,8},{8,16},{16,24},{24,32},{32,40},{40,48},{48,56},{56,64},{64,7... | collective-permute-start | bytes 49160 | tf_op jit(solution)/shard_map/ppermute | solution.py:325
  4.6 2.6 %base.1 = (f32[8,16,16,256]{3,2,1,0:T(8,128)S(1)}, f32[16,128]{1,0:T(8,128)S(1)}, f32[16,128]{1,0:T(8,128)S(1)}) custom-call(f32[16,128,256]{2,1,0:T(8,128)S(1)} %get-tuple-element.16.atm, f32[16,128,256]{2,1,0:T(8,128)S(1)} %copy-done.1), custom_call_target="tpu_custom_call" | custom-call | flops 10485760 | bytes 6291456 | tf_op jit(solution)/shard_map/base/pallas_call | solution.py:332
  7.2 2.6 %collective-permute-done.1.from_east = f32[24,128]{1,0:T(8,128)S(1)} collective-permute-done((f32[24,128]{1,0:T(8,128)S(1)}, f32[24,128]{1,0:T(8,128)S(1)}, u32[]{:S(2)}, u32[]{:S(2)}) %collective-permute-start.1) | collective-permute-done | bytes 12320 | tf_op jit(solution)/shard_map/ppermute | solution.py:326
  9.8 1.6 %inflow.1 = f32[8,16,16,256]{3,2,1,0:T(8,128)} custom-call(f32[8,16,16,256]{3,2,1,0:T(8,128)S(1)} %get-tuple-element.17.base, f32[16,128]{1,0:T(8,128)S(1)} %get-tuple-element.18.west_speed, f32[16,128]{1,0:T(8,128)S(1)} %get-tuple-element.19.east_speed, f32[32,128]{1,0:T(8,128)S(1)} %collective-permute-done.from_west, ...), custom_call_target="tpu_custom_call" | custom-call | flops 2097152 | bytes 4194304 | tf_op jit(solution)/shard_map/inflow/pallas_call | solution.py:337
  11.4 0.0 copy-start.9
  11.4 0.0 copy-start.5
  11.4 7.5 %all-to-all-start = ((f32[8,16,16,256]{3,2,1,0:T(8,128)}), f32[8,16,16,256]{3,2,1,0:T(8,128)S(1)}, u32[]{:S(2)}, u32[]{:S(2)}) async-start(f32[8,16,16,256]{3,2,1,0:T(8,128)} %inflow.1), calls=%async_computation | async-start | bytes 4194304 | tf_op jit(solution)/shard_map/all_to_all | solution.py:342
  18.9 3.0 %collective-permute-start.2 = (f32[32,128]{1,0:T(8,128)S(1)}, f32[32,128]{1,0:T(8,128)S(1)}, u32[]{:S(2)}, u32[]{:S(2)}) collective-permute-start(f32[32,128]{1,0:T(8,128)S(1)} %get-tuple-element.23), channel_id=1, source_target_pairs={{0,1},{1,0},{2,3},{3,2},{4,5},{5,4},{6,7},{7,6},{8,9},{9,8},{10,11... | collective-permute-start | bytes 49160 | tf_op jit(solution)/shard_map/ppermute | solution.py:329
  21.9 0.7 collective-permute-start.3
  22.6 0.1 constant_dynamic-slice_fusion
  22.7 0.1 copy.21
  22.8 0.1 reshape.27
  22.9 0.1 copy.20
  23.0 0.1 reshape.26
  23.2 2.2 %copy-done = f32[64,128,128]{2,1,0:T(8,128)S(1)} copy-done((f32[64,128,128]{2,1,0:T(8,128)S(1)}, f32[64,128,128]{2,1,0:T(8,128)}, u32[]{:S(2)}) %copy-start) | copy-done | bytes 4194328
  25.4 2.5 %sst.1 = f32[16,256]{1,0:T(8,128)S(1)} custom-call(s32[256]{0:T(256)S(1)} %pad_add_fusion.ids, f32[32,128]{1,0:T(8,128)S(1)} %collective-permute-done.from_west, f32[256,128]{1,0:T(8,128)S(1)} %bitcast.7, s32[8,128]{1,0:T(8,128)S(1)} %copy-done.5, f32[64,128,128]{2,1,0:T(8,128)S(1)} %copy-done), custom_call_target="tpu_custom_call" | custom-call | flops 8388608 | bytes 8388608 | tf_op jit(solution)/shard_map/sst/pallas_call | solution.py:348
  27.9 19.4 %all-to-all-done.columns = f32[8,16,16,256]{3,2,1,0:T(8,128)S(1)} async-done(((f32[8,16,16,256]{3,2,1,0:T(8,128)}), f32[8,16,16,256]{3,2,1,0:T(8,128)S(1)}, u32[]{:S(2)}, u32[]{:S(2)}) %all-to-all-start) | async-done | bytes 2097184 | tf_op jit(solution)/shard_map/all_to_all | solution.py:342
  47.3 2.6 %solve.1 = (f32[8,2,16,8,256]{4,3,2,1,0:T(8,128)}, f32[16,256]{1,0:T(8,128)}) custom-call(s32[1]{0:T(128)} %bitcast.place, f32[8,16,16,256]{3,2,1,0:T(8,128)S(1)} %all-to-all-done.columns, f32[8,128,128]{2,1,0:T(8,128)S(1)} %copy-done.3, f32[128,256]{1,0:T(8,128)S(1)} %copy-done.4, f32[16,256]{1,0:T(8,128)S(1)} %sst.1), custom_call_target="tpu_custom_call" | custom-call | flops 419430400 | bytes 4194304 | tf_op jit(solution)/shard_map/solve/pallas_call | solution.py:355
  50.0 0.0 copy-start.7
  50.0 3.7 %all-to-all-start.1 = ((f32[8,2,16,8,256]{4,3,2,1,0:T(8,128)}), f32[8,2,16,8,256]{4,3,2,1,0:T(8,128)S(1)}, u32[]{:S(2)}, u32[]{:S(2)}) async-start(f32[8,2,16,8,256]{4,3,2,1,0:T(8,128)} %get-tuple-element.25), calls=%async_computation.1 | async-start | bytes 4194304 | tf_op jit(solution)/shard_map/all_to_all | solution.py:366
  53.8 0.1 copy.23
  53.8 0.1 reshape.29
  53.9 0.1 copy.22
  54.0 0.1 reshape.28
  54.1 0.1 collective-permute-start.4
  54.2 0.1 pad_add_fusion.1.ids
  54.3 0.1 rev.4.folded
  54.4 5.4 %collective-permute-done.4.from_east_flux = f32[16,256]{1,0:T(8,128)S(1)} collective-permute-done((f32[16,256]{1,0:T(8,128)S(1)}, f32[16,256]{1,0:T(8,128)S(1)}, u32[]{:S(2)}, u32[]{:S(2)}) %collective-permute-start.4) | collective-permute-done | bytes 16416 | tf_op jit(solution)/shard_map/ppermute | solution.py:367
  59.8 4.9 %ocean.1 = f32[32,8,128]{2,1,0:T(8,128)} custom-call(s32[1]{0:T(128)} %bitcast.place, s32[64]{0:T(128)S(1)} %pad_add_fusion.1.ids, f32[16,256]{1,0:T(8,128)S(1)} %copy-done.7, f32[16,256]{1,0:T(8,128)S(1)} %collective-permute-done.4.from_east_flux, f32[64,128,128]{2,1,0:T(8,128)} %weights.3, f32[32,8,128]{2,1,0:T(8,128)S(1)} %copy-done.2, ...), custom_call_target="tpu_custom_call" | custom-call | flops 8388608 | bytes 4194304 | tf_op jit(solution)/shard_map/ocean/pallas_call | solution.py:373
  64.7 18.1 %all-to-all-done.1.parts = f32[8,2,16,8,256]{4,3,2,1,0:T(8,128)S(1)} async-done(((f32[8,2,16,8,256]{4,3,2,1,0:T(8,128)}), f32[8,2,16,8,256]{4,3,2,1,0:T(8,128)S(1)}, u32[]{:S(2)}, u32[]{:S(2)}) %all-to-all-start.1) | async-done | bytes 2097184 | tf_op jit(solution)/shard_map/all_to_all | solution.py:366
  82.8 1.4 %place.1 = f32[16,128,256]{2,1,0:T(8,128)} custom-call(f32[8,2,16,8,256]{4,3,2,1,0:T(8,128)S(1)} %all-to-all-done.1.parts), custom_call_target="tpu_custom_call" | custom-call | bytes 4194304 | tf_op jit(solution)/shard_map/place/pallas_call | solution.py:385
  (29 shorter events, 0.1 us)
Async XLA Ops:
  0.6 3.9 %copy-start.1 = (f32[16,128,256]{2,1,0:T(8,128)S(1)}, f32[16,128,256]{2,1,0:T(8,128)}, u32[]{:S(2)}) copy-start(f32[16,128,256]{2,1,0:T(8,128)} %courant.1) | copy-start | bytes 6291460
  2.7 7.1 %collective-permute-start = (f32[32,128]{1,0:T(8,128)S(1)}, f32[32,128]{1,0:T(8,128)S(1)}, u32[]{:S(2)}, u32[]{:S(2)}) collective-permute-start(f32[32,128]{1,0:T(8,128)S(1)} %get-tuple-element.20), channel_id=1, source_target_pairs={{0,8},{8,16},{16,24},{24,32},{32,40},{40,48},{48,56},{56,64},{64,7... | collective-permute-start | bytes 49160 | tf_op jit(solution)/shard_map/ppermute | solution.py:325
  4.6 5.2 %collective-permute-start.1 = (f32[24,128]{1,0:T(8,128)S(1)}, f32[24,128]{1,0:T(8,128)S(1)}, u32[]{:S(2)}, u32[]{:S(2)}) collective-permute-start(f32[24,128]{1,0:T(8,128)S(1)} %get-tuple-element.21), channel_id=1, source_target_pairs={{8,0},{16,8},{24,16},{32,24},{40,32},{48,40},{56,48},{64,56},{72,6... | collective-permute-start | bytes 36872 | tf_op jit(solution)/shard_map/ppermute | solution.py:326
  11.4 11.2 %copy-start.9 = (s32[128,2,4]{0,2,1:T(4,128)S(1)}, s32[128,2,4]{0,2,1:T(4,128)}, u32[]{:S(2)}) copy-start(s32[128,2,4]{0,2,1:T(4,128)} %param.25) | copy-start | bytes 12292
  11.4 11.2 %copy-start.10 = (s32[128,2,4]{0,2,1:T(4,128)S(1)}, s32[128,2,4]{0,2,1:T(4,128)}, u32[]{:S(2)}) copy-start(s32[128,2,4]{0,2,1:T(4,128)} %param.24) | copy-start | bytes 12292
  11.4 11.7 %copy-start.2 = (f32[32,8,128]{2,1,0:T(8,128)S(1)}, f32[32,8,128]{2,1,0:T(8,128)}, u32[]{:S(2)}) copy-start(f32[32,8,128]{2,1,0:T(8,128)} %temp_in.1) | copy-start | bytes 393220
  11.4 11.7 %copy-start.5 = (s32[8,128]{1,0:T(8,128)S(1)}, s32[8,128]{1,0:T(8,128)}, u32[]{:S(2)}) copy-start(s32[8,128]{1,0:T(8,128)} %mask_in.3) | copy-start | bytes 12292
  11.4 35.8 %all-to-all-start = ((f32[8,16,16,256]{3,2,1,0:T(8,128)}), f32[8,16,16,256]{3,2,1,0:T(8,128)S(1)}, u32[]{:S(2)}, u32[]{:S(2)}) async-start(f32[8,16,16,256]{3,2,1,0:T(8,128)} %inflow.1), calls=%async_computation | async-start | bytes 4194304 | tf_op jit(solution)/shard_map/all_to_all | solution.py:342
  18.9 31.0 %collective-permute-start.2 = (f32[32,128]{1,0:T(8,128)S(1)}, f32[32,128]{1,0:T(8,128)S(1)}, u32[]{:S(2)}, u32[]{:S(2)}) collective-permute-start(f32[32,128]{1,0:T(8,128)S(1)} %get-tuple-element.23), channel_id=1, source_target_pairs={{0,1},{1,0},{2,3},{3,2},{4,5},{5,4},{6,7},{7,6},{8,9},{9,8},{10,11... | collective-permute-start | bytes 49160 | tf_op jit(solution)/shard_map/ppermute | solution.py:329
  21.9 28.0 %collective-permute-start.3 = (f32[32,128]{1,0:T(8,128)S(1)}, f32[32,128]{1,0:T(8,128)S(1)}, u32[]{:S(2)}, u32[]{:S(2)}) collective-permute-start(f32[32,128]{1,0:T(8,128)S(1)} %get-tuple-element.24), channel_id=1, source_target_pairs={{1,2},{2,1},{3,4},{4,3},{5,6},{6,5},{7,127},{9,10},{10,9},{11,12},... | collective-permute-start | bytes 49160 | tf_op jit(solution)/shard_map/ppermute | solution.py:330
  23.2 2.2 %copy-start = (f32[64,128,128]{2,1,0:T(8,128)S(1)}, f32[64,128,128]{2,1,0:T(8,128)}, u32[]{:S(2)}) copy-start(f32[64,128,128]{2,1,0:T(8,128)} %weights.3) | copy-start | bytes 12582916
  25.4 21.9 %copy-start.3 = (f32[8,128,128]{2,1,0:T(8,128)S(1)}, f32[8,128,128]{2,1,0:T(8,128)}, u32[]{:S(2)}) copy-start(f32[8,128,128]{2,1,0:T(8,128)} %inverse.2) | copy-start | bytes 1572868
  25.4 21.9 %copy-start.4 = (f32[128,256]{1,0:T(8,128)S(1)}, f32[128,256]{1,0:T(8,128)}, u32[]{:S(2)}) copy-start(f32[128,256]{1,0:T(8,128)} %factor.1) | copy-start | bytes 393220
  49.9 3.8 %copy-start.11 = (s32[8,1,4]{0,2,1:T(4,128)S(1)}, s32[8,1,4]{0,2,1:T(4,128)}, u32[]{:S(2)}) copy-start(s32[8,1,4]{0,2,1:T(4,128)} %param.23) | copy-start | bytes 388
  49.9 4.0 %copy-start.12 = (s32[8,1,4]{0,2,1:T(4,128)S(1)}, s32[8,1,4]{0,2,1:T(4,128)}, u32[]{:S(2)}) copy-start(s32[8,1,4]{0,2,1:T(4,128)} %param.22) | copy-start | bytes 388
  50.0 4.2 %copy-start.7 = (f32[16,256]{1,0:T(8,128)S(1)}, f32[16,256]{1,0:T(8,128)}, u32[]{:S(2)}) copy-start(f32[16,256]{1,0:T(8,128)} %get-tuple-element.15.flux) | copy-start | bytes 49156
  50.0 9.8 %copy-start.6 = (f32[32,32]{1,0:T(8,128)S(1)}, f32[32,32]{1,0:T(8,128)}, u32[]{:S(2)}) copy-start(f32[32,32]{1,0:T(8,128)} %inverse.3) | copy-start | bytes 12292
  50.0 9.8 %copy-start.8 = (f32[8,128]{1,0:T(8,128)S(1)}, f32[8,128]{1,0:T(8,128)}, u32[]{:S(2)}) copy-start(f32[8,128]{1,0:T(8,128)} %diffusivity.1) | copy-start | bytes 12292
  50.0 32.8 %all-to-all-start.1 = ((f32[8,2,16,8,256]{4,3,2,1,0:T(8,128)}), f32[8,2,16,8,256]{4,3,2,1,0:T(8,128)S(1)}, u32[]{:S(2)}, u32[]{:S(2)}) async-start(f32[8,2,16,8,256]{4,3,2,1,0:T(8,128)} %get-tuple-element.25), calls=%async_computation.1 | async-start | bytes 4194304 | tf_op jit(solution)/shard_map/all_to_all | solution.py:366
  54.1 5.6 %collective-permute-start.4 = (f32[16,256]{1,0:T(8,128)S(1)}, f32[16,256]{1,0:T(8,128)S(1)}, u32[]{:S(2)}, u32[]{:S(2)}) collective-permute-start(f32[16,256]{1,0:T(8,128)S(1)} %copy-done.7), channel_id=1, source_target_pairs={{8,0},{16,8},{24,16},{32,24},{40,32},{48,40},{56,48},{64,56},{72,6... | collective-permute-start | bytes 49160 | tf_op jit(solution)/shard_map/ppermute | solution.py:367

commit v6 on v5

--- a/solution.py
+++ b/solution.py
@@ -50,6 +50,14 @@
 def split(value):
     high = value.astype(BF16)
     return high, (value - high.astype(F32)).astype(BF16)
+
+
+def gather(lane, at, low, high, first, last):
+    turned = pltpu.roll(jnp.where(lane == LANES - 1, high, low), at, 1)
+    return (
+        jnp.where(lane == at, turned, first),
+        jnp.where(lane == (at + LANES - 1) % LANES, turned, last),
+    )
 
 
 def edges_kernel(place, atm_in, ocean_in, mask_in, east_msg, west_msg, even_msg, odd_msg, atm, ocean, mask, sems):
@@ -65,24 +73,17 @@
     last = jnp.zeros((LANES, LANES), F32)
     first = jnp.zeros((LANES, LANES), F32)
 
-    def gather(at, low, high, first, last):
-        turned = pltpu.roll(jnp.where(lane == LANES - 1, high, low), at, 1)
-        return (
-            jnp.where(lane == at, turned, first),
-            jnp.where(lane == (at + LANES - 1) % LANES, turned, last),
-        )
-
     for piece in range(PIECES):
         copies[piece].wait()
         for level in range(piece * step, (piece + 1) * step):
             first, last = gather(
-                level, atm[level, :, :LANES], atm[level, :, cells - LANES :], first, last
+                lane, level, atm[level, :, :LANES], atm[level, :, cells - LANES :], first, last
             )
     for copy in copies[PIECES:]:
         copy.wait()
     for part in range(2):
         tile = ocean[part * LANES : (part + 1) * LANES, :]
-        first, last = gather(levels + part, tile, tile, first, last)
+        first, last = gather(lane, levels + part, tile, tile, first, last)
     last = pltpu.roll(last, 1, 1)
     east_msg[:24, :] = last.T[:24, :]
     east_msg[24:, :] = mask[...].astype(F32) * ocean[:8, :]
@@ -120,8 +121,8 @@
     first = jnp.zeros((LANES, LANES), F32)
     last = jnp.zeros((LANES, LANES), F32)
     for level in range(levels):
-        first = jnp.where(at == level, courant[level, :, 0:1], first)
-        last = jnp.where(at == level, courant[level, :, cells - 1 : cells], last)
+        first, last = gather(at, level, courant[level, :, :LANES], courant[level, :, cells - LANES :], first, last)
+    last = pltpu.roll(last, 1, 1)
     west_speed[...] = jnp.maximum(first.T[:levels, :], 0.0)
     east_speed[...] = jnp.minimum(last.T[:levels, :], 0.0)
 

time: 84.6 us -> 84.1 us (level)
  no operation moved by 1% of the time
where the time goes in v6:
time: 84.1 us; the launch traced here: 83.7 us
  waiting for transfers between devices  45.3 us (54%)
  Pallas kernels  17.5 us (21%)
  starting transfers between devices  16.8 us (20%)
  local copies, waits for them, and re-layouts  3.15 us (4%)
  between operations  0.88 us (1%)
    all_to_all x1, waiting for transfers between devices, per_device(): lax.all_to_all(advected, 'sub', split_axis=0, concat_axis=0, tiled=True)  19.1 us
    all_to_all x1, waiting for transfers between devices, per_device(): lax.all_to_all(solved, 'sub', split_axis=0, concat_axis=0, tiled=True)  17.9 us
    all_to_all x1, starting transfers between devices, per_device(): lax.all_to_all(advected, 'sub', split_axis=0, concat_axis=0, tiled=True)  7.51 us
    ppermute x1, waiting for transfers between devices, per_device(): east_flux = lax.ppermute(flux_band, 'lon', down)  5.41 us
    pallas_call x1, Pallas kernels, per_device(): kernel_call(functools.partial(ocean_kernel, width, n_sub), shape(olev, ol...  4.9 us
    all_to_all x1, starting transfers between devices, per_device(): lax.all_to_all(solved, 'sub', split_axis=0, concat_axis=0, tiled=True)  3.75 us
    ppermute x1, starting transfers between devices, per_device(): even_rows = lax.ppermute(even_msg, ('lon', 'sub'), first)  2.97 us
    ppermute x1, waiting for transfers between devices, per_device(): from_east = lax.ppermute(west_msg, 'lon', down)  2.91 us
  transfers between devices with their start and end apart: 7, of which 4 were waited for; matrix products, arithmetic and copies ran while one was open for 1% of the time, Pallas kernels for 15%

profile of v6, /device:TPU:7, one launch (start us, length us, event | category | flops | bytes accessed | tf_op | source)
XLA Modules:
  0.0 83.7 jit_solution(4173275383350251886)
XLA Ops:
  0.6 2.1 %edges.1 = (f32[32,128]{1,0:T(8,128)S(1)}, f32[24,128]{1,0:T(8,128)S(1)}, f32[32,128]{1,0:T(8,128)S(1)}, f32[32,128]{1,0:T(8,128)S(1)}, f32[16,128,256]{2,1,0:T(8,128)S(1)}) custom-call(s32[1]{0:T(128)} %bitcast.place, f32[16,128,256]{2,1,0:T(8,128)} %atm_in.1, f32[256,128]{1,0:T(8,128)} %bitcast.6, s32[8,128]{1,0:T(8,128)} %mask_in.3), custom_call_target="tpu_custom_call" | custom-call | flops 2097152 | bytes 2097152 | tf_op jit(solution)/shard_map/edges/pallas_call | solution.py:314
  2.7 1.8 %collective-permute-start = (f32[32,128]{1,0:T(8,128)S(1)}, f32[32,128]{1,0:T(8,128)S(1)}, u32[]{:S(2)}, u32[]{:S(2)}) collective-permute-start(f32[32,128]{1,0:T(8,128)S(1)} %get-tuple-element.20), channel_id=1, source_target_pairs={{0,8},{8,16},{16,24},{24,32},{32,40},{40,48},{48,56},{56,64},{64,7... | collective-permute-start | bytes 49160 | tf_op jit(solution)/shard_map/ppermute | solution.py:326
  4.6 2.3 %base.1 = (f32[8,16,16,256]{3,2,1,0:T(8,128)S(1)}, f32[16,128]{1,0:T(8,128)S(1)}, f32[16,128]{1,0:T(8,128)S(1)}) custom-call(f32[16,128,256]{2,1,0:T(8,128)S(1)} %get-tuple-element.16.atm, f32[16,128,256]{2,1,0:T(8,128)S(1)} %copy-done.1), custom_call_target="tpu_custom_call" | custom-call | flops 10485760 | bytes 6291456 | tf_op jit(solution)/shard_map/base/pallas_call | solution.py:333
  6.9 2.9 %collective-permute-done.1.from_east = f32[24,128]{1,0:T(8,128)S(1)} collective-permute-done((f32[24,128]{1,0:T(8,128)S(1)}, f32[24,128]{1,0:T(8,128)S(1)}, u32[]{:S(2)}, u32[]{:S(2)}) %collective-permute-start.1) | collective-permute-done | bytes 12320 | tf_op jit(solution)/shard_map/ppermute | solution.py:327
  9.8 1.6 %inflow.1 = f32[8,16,16,256]{3,2,1,0:T(8,128)} custom-call(f32[8,16,16,256]{3,2,1,0:T(8,128)S(1)} %get-tuple-element.17.base, f32[16,128]{1,0:T(8,128)S(1)} %get-tuple-element.18.west_speed, f32[16,128]{1,0:T(8,128)S(1)} %get-tuple-element.19.east_speed, f32[32,128]{1,0:T(8,128)S(1)} %collective-permute-done.from_west, ...), custom_call_target="tpu_custom_call" | custom-call | flops 2097152 | bytes 4194304 | tf_op jit(solution)/shard_map/inflow/pallas_call | solution.py:338
  11.4 0.0 copy-start.9
  11.4 0.0 copy-start.5
  11.4 7.5 %all-to-all-start = ((f32[8,16,16,256]{3,2,1,0:T(8,128)}), f32[8,16,16,256]{3,2,1,0:T(8,128)S(1)}, u32[]{:S(2)}, u32[]{:S(2)}) async-start(f32[8,16,16,256]{3,2,1,0:T(8,128)} %inflow.1), calls=%async_computation | async-start | bytes 4194304 | tf_op jit(solution)/shard_map/all_to_all | solution.py:343
  18.9 3.0 %collective-permute-start.2 = (f32[32,128]{1,0:T(8,128)S(1)}, f32[32,128]{1,0:T(8,128)S(1)}, u32[]{:S(2)}, u32[]{:S(2)}) collective-permute-start(f32[32,128]{1,0:T(8,128)S(1)} %get-tuple-element.23), channel_id=1, source_target_pairs={{0,1},{1,0},{2,3},{3,2},{4,5},{5,4},{6,7},{7,6},{8,9},{9,8},{10,11... | collective-permute-start | bytes 49160 | tf_op jit(solution)/shard_map/ppermute | solution.py:330
  21.9 0.7 collective-permute-start.3
  22.6 0.1 constant_dynamic-slice_fusion
  22.7 0.1 copy.21
  22.8 0.1 reshape.27
  22.9 0.1 copy.20
  23.0 0.1 reshape.26
  23.2 2.2 %copy-done = f32[64,128,128]{2,1,0:T(8,128)S(1)} copy-done((f32[64,128,128]{2,1,0:T(8,128)S(1)}, f32[64,128,128]{2,1,0:T(8,128)}, u32[]{:S(2)}) %copy-start) | copy-done | bytes 4194328
  25.4 2.5 %sst.1 = f32[16,256]{1,0:T(8,128)S(1)} custom-call(s32[256]{0:T(256)S(1)} %pad_add_fusion.ids, f32[32,128]{1,0:T(8,128)S(1)} %collective-permute-done.from_west, f32[256,128]{1,0:T(8,128)S(1)} %bitcast.7, s32[8,128]{1,0:T(8,128)S(1)} %copy-done.5, f32[64,128,128]{2,1,0:T(8,128)S(1)} %copy-done), custom_call_target="tpu_custom_call" | custom-call | flops 8388608 | bytes 8388608 | tf_op jit(solution)/shard_map/sst/pallas_call | solution.py:349
  27.9 19.1 %all-to-all-done.columns = f32[8,16,16,256]{3,2,1,0:T(8,128)S(1)} async-done(((f32[8,16,16,256]{3,2,1,0:T(8,128)}), f32[8,16,16,256]{3,2,1,0:T(8,128)S(1)}, u32[]{:S(2)}, u32[]{:S(2)}) %all-to-all-start) | async-done | bytes 2097184 | tf_op jit(solution)/shard_map/all_to_all | solution.py:343
  47.0 2.6 %solve.1 = (f32[8,2,16,8,256]{4,3,2,1,0:T(8,128)}, f32[16,256]{1,0:T(8,128)}) custom-call(s32[1]{0:T(128)} %bitcast.place, f32[8,16,16,256]{3,2,1,0:T(8,128)S(1)} %all-to-all-done.columns, f32[8,128,128]{2,1,0:T(8,128)S(1)} %copy-done.3, f32[128,256]{1,0:T(8,128)S(1)} %copy-done.4, f32[16,256]{1,0:T(8,128)S(1)} %sst.1), custom_call_target="tpu_custom_call" | custom-call | flops 419430400 | bytes 4194304 | tf_op jit(solution)/shard_map/solve/pallas_call | solution.py:356
  49.7 0.0 copy-start.7
  49.7 3.7 %all-to-all-start.1 = ((f32[8,2,16,8,256]{4,3,2,1,0:T(8,128)}), f32[8,2,16,8,256]{4,3,2,1,0:T(8,128)S(1)}, u32[]{:S(2)}, u32[]{:S(2)}) async-start(f32[8,2,16,8,256]{4,3,2,1,0:T(8,128)} %get-tuple-element.25), calls=%async_computation.1 | async-start | bytes 4194304 | tf_op jit(solution)/shard_map/all_to_all | solution.py:367
  53.5 0.1 copy.23
  53.6 0.1 reshape.29
  53.6 0.1 copy.22
  53.7 0.1 reshape.28
  53.8 0.1 collective-permute-start.4
  53.9 0.1 pad_add_fusion.1.ids
  54.0 0.1 rev.4.folded
  54.1 5.4 %collective-permute-done.4.from_east_flux = f32[16,256]{1,0:T(8,128)S(1)} collective-permute-done((f32[16,256]{1,0:T(8,128)S(1)}, f32[16,256]{1,0:T(8,128)S(1)}, u32[]{:S(2)}, u32[]{:S(2)}) %collective-permute-start.4) | collective-permute-done | bytes 16416 | tf_op jit(solution)/shard_map/ppermute | solution.py:368
  59.5 4.9 %ocean.1 = f32[32,8,128]{2,1,0:T(8,128)} custom-call(s32[1]{0:T(128)} %bitcast.place, s32[64]{0:T(128)S(1)} %pad_add_fusion.1.ids, f32[16,256]{1,0:T(8,128)S(1)} %copy-done.7, f32[16,256]{1,0:T(8,128)S(1)} %collective-permute-done.4.from_east_flux, f32[64,128,128]{2,1,0:T(8,128)} %weights.3, f32[32,8,128]{2,1,0:T(8,128)S(1)} %copy-done.2, ...), custom_call_target="tpu_custom_call" | custom-call | flops 8388608 | bytes 4194304 | tf_op jit(solution)/shard_map/ocean/pallas_call | solution.py:374
  64.4 17.9 %all-to-all-done.1.parts = f32[8,2,16,8,256]{4,3,2,1,0:T(8,128)S(1)} async-done(((f32[8,2,16,8,256]{4,3,2,1,0:T(8,128)}), f32[8,2,16,8,256]{4,3,2,1,0:T(8,128)S(1)}, u32[]{:S(2)}, u32[]{:S(2)}) %all-to-all-start.1) | async-done | bytes 2097184 | tf_op jit(solution)/shard_map/all_to_all | solution.py:367
  82.3 1.4 %place.1 = f32[16,128,256]{2,1,0:T(8,128)} custom-call(f32[8,2,16,8,256]{4,3,2,1,0:T(8,128)S(1)} %all-to-all-done.1.parts), custom_call_target="tpu_custom_call" | custom-call | bytes 4194304 | tf_op jit(solution)/shard_map/place/pallas_call | solution.py:386
  (29 shorter events, 0.1 us)
Async XLA Ops:
  0.6 3.9 %copy-start.1 = (f32[16,128,256]{2,1,0:T(8,128)S(1)}, f32[16,128,256]{2,1,0:T(8,128)}, u32[]{:S(2)}) copy-start(f32[16,128,256]{2,1,0:T(8,128)} %courant.1) | copy-start | bytes 6291460
  2.7 7.1 %collective-permute-start = (f32[32,128]{1,0:T(8,128)S(1)}, f32[32,128]{1,0:T(8,128)S(1)}, u32[]{:S(2)}, u32[]{:S(2)}) collective-permute-start(f32[32,128]{1,0:T(8,128)S(1)} %get-tuple-element.20), channel_id=1, source_target_pairs={{0,8},{8,16},{16,24},{24,32},{32,40},{40,48},{48,56},{56,64},{64,7... | collective-permute-start | bytes 49160 | tf_op jit(solution)/shard_map/ppermute | solution.py:326
  4.6 5.2 %collective-permute-start.1 = (f32[24,128]{1,0:T(8,128)S(1)}, f32[24,128]{1,0:T(8,128)S(1)}, u32[]{:S(2)}, u32[]{:S(2)}) collective-permute-start(f32[24,128]{1,0:T(8,128)S(1)} %get-tuple-element.21), channel_id=1, source_target_pairs={{8,0},{16,8},{24,16},{32,24},{40,32},{48,40},{56,48},{64,56},{72,6... | collective-permute-start | bytes 36872 | tf_op jit(solution)/shard_map/ppermute | solution.py:327
  11.4 11.2 %copy-start.9 = (s32[128,2,4]{0,2,1:T(4,128)S(1)}, s32[128,2,4]{0,2,1:T(4,128)}, u32[]{:S(2)}) copy-start(s32[128,2,4]{0,2,1:T(4,128)} %param.25) | copy-start | bytes 12292
  11.4 11.2 %copy-start.10 = (s32[128,2,4]{0,2,1:T(4,128)S(1)}, s32[128,2,4]{0,2,1:T(4,128)}, u32[]{:S(2)}) copy-start(s32[128,2,4]{0,2,1:T(4,128)} %param.24) | copy-start | bytes 12292
  11.4 11.7 %copy-start.2 = (f32[32,8,128]{2,1,0:T(8,128)S(1)}, f32[32,8,128]{2,1,0:T(8,128)}, u32[]{:S(2)}) copy-start(f32[32,8,128]{2,1,0:T(8,128)} %temp_in.1) | copy-start | bytes 393220
  11.4 11.7 %copy-start.5 = (s32[8,128]{1,0:T(8,128)S(1)}, s32[8,128]{1,0:T(8,128)}, u32[]{:S(2)}) copy-start(s32[8,128]{1,0:T(8,128)} %mask_in.3) | copy-start | bytes 12292
  11.4 35.6 %all-to-all-start = ((f32[8,16,16,256]{3,2,1,0:T(8,128)}), f32[8,16,16,256]{3,2,1,0:T(8,128)S(1)}, u32[]{:S(2)}, u32[]{:S(2)}) async-start(f32[8,16,16,256]{3,2,1,0:T(8,128)} %inflow.1), calls=%async_computation | async-start | bytes 4194304 | tf_op jit(solution)/shard_map/all_to_all | solution.py:343
  18.9 30.7 %collective-permute-start.2 = (f32[32,128]{1,0:T(8,128)S(1)}, f32[32,128]{1,0:T(8,128)S(1)}, u32[]{:S(2)}, u32[]{:S(2)}) collective-permute-start(f32[32,128]{1,0:T(8,128)S(1)} %get-tuple-element.23), channel_id=1, source_target_pairs={{0,1},{1,0},{2,3},{3,2},{4,5},{5,4},{6,7},{7,6},{8,9},{9,8},{10,11... | collective-permute-start | bytes 49160 | tf_op jit(solution)/shard_map/ppermute | solution.py:330
  21.9 27.7 %collective-permute-start.3 = (f32[32,128]{1,0:T(8,128)S(1)}, f32[32,128]{1,0:T(8,128)S(1)}, u32[]{:S(2)}, u32[]{:S(2)}) collective-permute-start(f32[32,128]{1,0:T(8,128)S(1)} %get-tuple-element.24), channel_id=1, source_target_pairs={{1,2},{2,1},{3,4},{4,3},{5,6},{6,5},{7,127},{9,10},{10,9},{11,12},... | collective-permute-start | bytes 49160 | tf_op jit(solution)/shard_map/ppermute | solution.py:331
  23.2 2.2 %copy-start = (f32[64,128,128]{2,1,0:T(8,128)S(1)}, f32[64,128,128]{2,1,0:T(8,128)}, u32[]{:S(2)}) copy-start(f32[64,128,128]{2,1,0:T(8,128)} %weights.3) | copy-start | bytes 12582916
  25.4 21.7 %copy-start.3 = (f32[8,128,128]{2,1,0:T(8,128)S(1)}, f32[8,128,128]{2,1,0:T(8,128)}, u32[]{:S(2)}) copy-start(f32[8,128,128]{2,1,0:T(8,128)} %inverse.2) | copy-start | bytes 1572868
  25.4 21.7 %copy-start.4 = (f32[128,256]{1,0:T(8,128)S(1)}, f32[128,256]{1,0:T(8,128)}, u32[]{:S(2)}) copy-start(f32[128,256]{1,0:T(8,128)} %factor.1) | copy-start | bytes 393220
  49.6 3.8 %copy-start.11 = (s32[8,1,4]{0,2,1:T(4,128)S(1)}, s32[8,1,4]{0,2,1:T(4,128)}, u32[]{:S(2)}) copy-start(s32[8,1,4]{0,2,1:T(4,128)} %param.23) | copy-start | bytes 388
  49.7 4.0 %copy-start.12 = (s32[8,1,4]{0,2,1:T(4,128)S(1)}, s32[8,1,4]{0,2,1:T(4,128)}, u32[]{:S(2)}) copy-start(s32[8,1,4]{0,2,1:T(4,128)} %param.22) | copy-start | bytes 388
  49.7 4.2 %copy-start.7 = (f32[16,256]{1,0:T(8,128)S(1)}, f32[16,256]{1,0:T(8,128)}, u32[]{:S(2)}) copy-start(f32[16,256]{1,0:T(8,128)} %get-tuple-element.15.flux) | copy-start | bytes 49156
  49.7 9.8 %copy-start.6 = (f32[32,32]{1,0:T(8,128)S(1)}, f32[32,32]{1,0:T(8,128)}, u32[]{:S(2)}) copy-start(f32[32,32]{1,0:T(8,128)} %inverse.3) | copy-start | bytes 12292
  49.7 9.8 %copy-start.8 = (f32[8,128]{1,0:T(8,128)S(1)}, f32[8,128]{1,0:T(8,128)}, u32[]{:S(2)}) copy-start(f32[8,128]{1,0:T(8,128)} %diffusivity.1) | copy-start | bytes 12292
  49.7 32.6 %all-to-all-start.1 = ((f32[8,2,16,8,256]{4,3,2,1,0:T(8,128)}), f32[8,2,16,8,256]{4,3,2,1,0:T(8,128)S(1)}, u32[]{:S(2)}, u32[]{:S(2)}) async-start(f32[8,2,16,8,256]{4,3,2,1,0:T(8,128)} %get-tuple-element.25), calls=%async_computation.1 | async-start | bytes 4194304 | tf_op jit(solution)/shard_map/all_to_all | solution.py:367
  53.8 5.6 %collective-permute-start.4 = (f32[16,256]{1,0:T(8,128)S(1)}, f32[16,256]{1,0:T(8,128)S(1)}, u32[]{:S(2)}, u32[]{:S(2)}) collective-permute-start(f32[16,256]{1,0:T(8,128)S(1)} %copy-done.7), channel_id=1, source_target_pairs={{8,0},{16,8},{24,16},{32,24},{40,32},{48,40},{56,48},{64,56},{72,6... | collective-permute-start | bytes 49160 | tf_op jit(solution)/shard_map/ppermute | solution.py:368

commit v7 on v6

--- a/solution.py
+++ b/solution.py
@@ -101,7 +101,7 @@
     band = out.shape[1]
     lane = lax.broadcasted_iota(jnp.int32, (band, cells), 1)
 
-    @pl.loop(0, out.shape[0])
+    @pl.loop(0, out.shape[0], unroll=2)
     def _(dest):
         rows = pl.ds(pl.multiple_of(dest * band, band), band)
         made = []

time: 84.1 us -> 83.7 us (level)
  transfers between devices with their start and end apart: 7 -> 7, of which waited for: 4 -> 4; matrix products, arithmetic and copies ran while one was open for 1% -> 1% of each run, Pallas kernels for 15% -> 14%
where the time goes in v7:
time: 83.7 us; the launch traced here: 83.3 us
  waiting for transfers between devices  45.3 us (54%)
  Pallas kernels  17.1 us (20%)
  starting transfers between devices  16.8 us (20%)
  local copies, waits for them, and re-layouts  3.15 us (4%)
  between operations  0.88 us (1%)
    all_to_all x1, waiting for transfers between devices, per_device(): lax.all_to_all(advected, 'sub', split_axis=0, concat_axis=0, tiled=True)  18.7 us
    all_to_all x1, waiting for transfers between devices, per_device(): lax.all_to_all(solved, 'sub', split_axis=0, concat_axis=0, tiled=True)  17.9 us
    all_to_all x1, starting transfers between devices, per_device(): lax.all_to_all(advected, 'sub', split_axis=0, concat_axis=0, tiled=True)  7.51 us
    ppermute x1, waiting for transfers between devices, per_device(): east_flux = lax.ppermute(flux_band, 'lon', down)  5.41 us
    pallas_call x1, Pallas kernels, per_device(): kernel_call(functools.partial(ocean_kernel, width, n_sub), shape(olev, ol...  4.9 us
    all_to_all x1, starting transfers between devices, per_device(): lax.all_to_all(solved, 'sub', split_axis=0, concat_axis=0, tiled=True)  3.75 us
    ppermute x1, waiting for transfers between devices, per_device(): from_east = lax.ppermute(west_msg, 'lon', down)  3.27 us
    ppermute x1, starting transfers between devices, per_device(): even_rows = lax.ppermute(even_msg, ('lon', 'sub'), first)  2.97 us
  transfers between devices with their start and end apart: 7, of which 4 were waited for; matrix products, arithmetic and copies ran while one was open for 1% of the time, Pallas kernels for 14%

profile of v7, /device:TPU:7, one launch (start us, length us, event | category | flops | bytes accessed | tf_op | source)
XLA Modules:
  0.0 83.3 jit_solution(15542720397920991590)
XLA Ops:
  0.6 2.1 %edges.1 = (f32[32,128]{1,0:T(8,128)S(1)}, f32[24,128]{1,0:T(8,128)S(1)}, f32[32,128]{1,0:T(8,128)S(1)}, f32[32,128]{1,0:T(8,128)S(1)}, f32[16,128,256]{2,1,0:T(8,128)S(1)}) custom-call(s32[1]{0:T(128)} %bitcast.place, f32[16,128,256]{2,1,0:T(8,128)} %atm_in.1, f32[256,128]{1,0:T(8,128)} %bitcast.6, s32[8,128]{1,0:T(8,128)} %mask_in.3), custom_call_target="tpu_custom_call" | custom-call | flops 2097152 | bytes 2097152 | tf_op jit(solution)/shard_map/edges/pallas_call | solution.py:314
  2.7 1.8 %collective-permute-start = (f32[32,128]{1,0:T(8,128)S(1)}, f32[32,128]{1,0:T(8,128)S(1)}, u32[]{:S(2)}, u32[]{:S(2)}) collective-permute-start(f32[32,128]{1,0:T(8,128)S(1)} %get-tuple-element.20), channel_id=1, source_target_pairs={{0,8},{8,16},{16,24},{24,32},{32,40},{40,48},{48,56},{56,64},{64,7... | collective-permute-start | bytes 49160 | tf_op jit(solution)/shard_map/ppermute | solution.py:326
  4.6 1.9 %base.1 = (f32[8,16,16,256]{3,2,1,0:T(8,128)S(1)}, f32[16,128]{1,0:T(8,128)S(1)}, f32[16,128]{1,0:T(8,128)S(1)}) custom-call(f32[16,128,256]{2,1,0:T(8,128)S(1)} %get-tuple-element.16.atm, f32[16,128,256]{2,1,0:T(8,128)S(1)} %copy-done.1), custom_call_target="tpu_custom_call" | custom-call | flops 10485760 | bytes 6291456 | tf_op jit(solution)/shard_map/base/pallas_call | solution.py:333
  6.5 3.3 %collective-permute-done.1.from_east = f32[24,128]{1,0:T(8,128)S(1)} collective-permute-done((f32[24,128]{1,0:T(8,128)S(1)}, f32[24,128]{1,0:T(8,128)S(1)}, u32[]{:S(2)}, u32[]{:S(2)}) %collective-permute-start.1) | collective-permute-done | bytes 12320 | tf_op jit(solution)/shard_map/ppermute | solution.py:327
  9.8 1.6 %inflow.1 = f32[8,16,16,256]{3,2,1,0:T(8,128)} custom-call(f32[8,16,16,256]{3,2,1,0:T(8,128)S(1)} %get-tuple-element.17.base, f32[16,128]{1,0:T(8,128)S(1)} %get-tuple-element.18.west_speed, f32[16,128]{1,0:T(8,128)S(1)} %get-tuple-element.19.east_speed, f32[32,128]{1,0:T(8,128)S(1)} %collective-permute-done.from_west, ...), custom_call_target="tpu_custom_call" | custom-call | flops 2097152 | bytes 4194304 | tf_op jit(solution)/shard_map/inflow/pallas_call | solution.py:338
  11.4 0.0 copy-start.9
  11.4 0.0 copy-start.5
  11.4 7.5 %all-to-all-start = ((f32[8,16,16,256]{3,2,1,0:T(8,128)}), f32[8,16,16,256]{3,2,1,0:T(8,128)S(1)}, u32[]{:S(2)}, u32[]{:S(2)}) async-start(f32[8,16,16,256]{3,2,1,0:T(8,128)} %inflow.1), calls=%async_computation | async-start | bytes 4194304 | tf_op jit(solution)/shard_map/all_to_all | solution.py:343
  18.9 3.0 %collective-permute-start.2 = (f32[32,128]{1,0:T(8,128)S(1)}, f32[32,128]{1,0:T(8,128)S(1)}, u32[]{:S(2)}, u32[]{:S(2)}) collective-permute-start(f32[32,128]{1,0:T(8,128)S(1)} %get-tuple-element.23), channel_id=1, source_target_pairs={{0,1},{1,0},{2,3},{3,2},{4,5},{5,4},{6,7},{7,6},{8,9},{9,8},{10,11... | collective-permute-start | bytes 49160 | tf_op jit(solution)/shard_map/ppermute | solution.py:330
  21.9 0.7 collective-permute-start.3
  22.6 0.1 constant_dynamic-slice_fusion
  22.7 0.1 copy.21
  22.8 0.1 reshape.27
  22.9 0.1 copy.20
  23.0 0.1 reshape.26
  23.2 2.2 %copy-done = f32[64,128,128]{2,1,0:T(8,128)S(1)} copy-done((f32[64,128,128]{2,1,0:T(8,128)S(1)}, f32[64,128,128]{2,1,0:T(8,128)}, u32[]{:S(2)}) %copy-start) | copy-done | bytes 4194328
  25.4 2.5 %sst.1 = f32[16,256]{1,0:T(8,128)S(1)} custom-call(s32[256]{0:T(256)S(1)} %pad_add_fusion.ids, f32[32,128]{1,0:T(8,128)S(1)} %collective-permute-done.from_west, f32[256,128]{1,0:T(8,128)S(1)} %bitcast.7, s32[8,128]{1,0:T(8,128)S(1)} %copy-done.5, f32[64,128,128]{2,1,0:T(8,128)S(1)} %copy-done), custom_call_target="tpu_custom_call" | custom-call | flops 8388608 | bytes 8388608 | tf_op jit(solution)/shard_map/sst/pallas_call | solution.py:349
  27.9 18.7 %all-to-all-done.columns = f32[8,16,16,256]{3,2,1,0:T(8,128)S(1)} async-done(((f32[8,16,16,256]{3,2,1,0:T(8,128)}), f32[8,16,16,256]{3,2,1,0:T(8,128)S(1)}, u32[]{:S(2)}, u32[]{:S(2)}) %all-to-all-start) | async-done | bytes 2097184 | tf_op jit(solution)/shard_map/all_to_all | solution.py:343
  46.6 2.6 %solve.1 = (f32[8,2,16,8,256]{4,3,2,1,0:T(8,128)}, f32[16,256]{1,0:T(8,128)}) custom-call(s32[1]{0:T(128)} %bitcast.place, f32[8,16,16,256]{3,2,1,0:T(8,128)S(1)} %all-to-all-done.columns, f32[8,128,128]{2,1,0:T(8,128)S(1)} %copy-done.3, f32[128,256]{1,0:T(8,128)S(1)} %copy-done.4, f32[16,256]{1,0:T(8,128)S(1)} %sst.1), custom_call_target="tpu_custom_call" | custom-call | flops 419430400 | bytes 4194304 | tf_op jit(solution)/shard_map/solve/pallas_call | solution.py:356
  49.3 0.0 copy-start.7
  49.3 3.7 %all-to-all-start.1 = ((f32[8,2,16,8,256]{4,3,2,1,0:T(8,128)}), f32[8,2,16,8,256]{4,3,2,1,0:T(8,128)S(1)}, u32[]{:S(2)}, u32[]{:S(2)}) async-start(f32[8,2,16,8,256]{4,3,2,1,0:T(8,128)} %get-tuple-element.25), calls=%async_computation.1 | async-start | bytes 4194304 | tf_op jit(solution)/shard_map/all_to_all | solution.py:367
  53.1 0.1 copy.23
  53.2 0.1 reshape.29
  53.3 0.1 copy.22
  53.4 0.1 reshape.28
  53.5 0.1 collective-permute-start.4
  53.6 0.1 pad_add_fusion.1.ids
  53.6 0.1 rev.4.folded
  53.7 5.4 %collective-permute-done.4.from_east_flux = f32[16,256]{1,0:T(8,128)S(1)} collective-permute-done((f32[16,256]{1,0:T(8,128)S(1)}, f32[16,256]{1,0:T(8,128)S(1)}, u32[]{:S(2)}, u32[]{:S(2)}) %collective-permute-start.4) | collective-permute-done | bytes 16416 | tf_op jit(solution)/shard_map/ppermute | solution.py:368
  59.1 4.9 %ocean.1 = f32[32,8,128]{2,1,0:T(8,128)} custom-call(s32[1]{0:T(128)} %bitcast.place, s32[64]{0:T(128)S(1)} %pad_add_fusion.1.ids, f32[16,256]{1,0:T(8,128)S(1)} %copy-done.7, f32[16,256]{1,0:T(8,128)S(1)} %collective-permute-done.4.from_east_flux, f32[64,128,128]{2,1,0:T(8,128)} %weights.3, f32[32,8,128]{2,1,0:T(8,128)S(1)} %copy-done.2, ...), custom_call_target="tpu_custom_call" | custom-call | flops 8388608 | bytes 4194304 | tf_op jit(solution)/shard_map/ocean/pallas_call | solution.py:374
  64.0 17.9 %all-to-all-done.1.parts = f32[8,2,16,8,256]{4,3,2,1,0:T(8,128)S(1)} async-done(((f32[8,2,16,8,256]{4,3,2,1,0:T(8,128)}), f32[8,2,16,8,256]{4,3,2,1,0:T(8,128)S(1)}, u32[]{:S(2)}, u32[]{:S(2)}) %all-to-all-start.1) | async-done | bytes 2097184 | tf_op jit(solution)/shard_map/all_to_all | solution.py:367
  81.9 1.4 %place.1 = f32[16,128,256]{2,1,0:T(8,128)} custom-call(f32[8,2,16,8,256]{4,3,2,1,0:T(8,128)S(1)} %all-to-all-done.1.parts), custom_call_target="tpu_custom_call" | custom-call | bytes 4194304 | tf_op jit(solution)/shard_map/place/pallas_call | solution.py:386
  (29 shorter events, 0.1 us)
Async XLA Ops:
  0.6 3.9 %copy-start.1 = (f32[16,128,256]{2,1,0:T(8,128)S(1)}, f32[16,128,256]{2,1,0:T(8,128)}, u32[]{:S(2)}) copy-start(f32[16,128,256]{2,1,0:T(8,128)} %courant.1) | copy-start | bytes 6291460
  2.7 7.1 %collective-permute-start = (f32[32,128]{1,0:T(8,128)S(1)}, f32[32,128]{1,0:T(8,128)S(1)}, u32[]{:S(2)}, u32[]{:S(2)}) collective-permute-start(f32[32,128]{1,0:T(8,128)S(1)} %get-tuple-element.20), channel_id=1, source_target_pairs={{0,8},{8,16},{16,24},{24,32},{32,40},{40,48},{48,56},{56,64},{64,7... | collective-permute-start | bytes 49160 | tf_op jit(solution)/shard_map/ppermute | solution.py:326
  4.6 5.2 %collective-permute-start.1 = (f32[24,128]{1,0:T(8,128)S(1)}, f32[24,128]{1,0:T(8,128)S(1)}, u32[]{:S(2)}, u32[]{:S(2)}) collective-permute-start(f32[24,128]{1,0:T(8,128)S(1)} %get-tuple-element.21), channel_id=1, source_target_pairs={{8,0},{16,8},{24,16},{32,24},{40,32},{48,40},{56,48},{64,56},{72,6... | collective-permute-start | bytes 36872 | tf_op jit(solution)/shard_map/ppermute | solution.py:327
  11.4 11.2 %copy-start.9 = (s32[128,2,4]{0,2,1:T(4,128)S(1)}, s32[128,2,4]{0,2,1:T(4,128)}, u32[]{:S(2)}) copy-start(s32[128,2,4]{0,2,1:T(4,128)} %param.25) | copy-start | bytes 12292
  11.4 11.2 %copy-start.10 = (s32[128,2,4]{0,2,1:T(4,128)S(1)}, s32[128,2,4]{0,2,1:T(4,128)}, u32[]{:S(2)}) copy-start(s32[128,2,4]{0,2,1:T(4,128)} %param.24) | copy-start | bytes 12292
  11.4 11.7 %copy-start.2 = (f32[32,8,128]{2,1,0:T(8,128)S(1)}, f32[32,8,128]{2,1,0:T(8,128)}, u32[]{:S(2)}) copy-start(f32[32,8,128]{2,1,0:T(8,128)} %temp_in.1) | copy-start | bytes 393220
  11.4 11.7 %copy-start.5 = (s32[8,128]{1,0:T(8,128)S(1)}, s32[8,128]{1,0:T(8,128)}, u32[]{:S(2)}) copy-start(s32[8,128]{1,0:T(8,128)} %mask_in.3) | copy-start | bytes 12292
  11.4 35.2 %all-to-all-start = ((f32[8,16,16,256]{3,2,1,0:T(8,128)}), f32[8,16,16,256]{3,2,1,0:T(8,128)S(1)}, u32[]{:S(2)}, u32[]{:S(2)}) async-start(f32[8,16,16,256]{3,2,1,0:T(8,128)} %inflow.1), calls=%async_computation | async-start | bytes 4194304 | tf_op jit(solution)/shard_map/all_to_all | solution.py:343
  18.9 30.3 %collective-permute-start.2 = (f32[32,128]{1,0:T(8,128)S(1)}, f32[32,128]{1,0:T(8,128)S(1)}, u32[]{:S(2)}, u32[]{:S(2)}) collective-permute-start(f32[32,128]{1,0:T(8,128)S(1)} %get-tuple-element.23), channel_id=1, source_target_pairs={{0,1},{1,0},{2,3},{3,2},{4,5},{5,4},{6,7},{7,6},{8,9},{9,8},{10,11... | collective-permute-start | bytes 49160 | tf_op jit(solution)/shard_map/ppermute | solution.py:330
  21.9 27.4 %collective-permute-start.3 = (f32[32,128]{1,0:T(8,128)S(1)}, f32[32,128]{1,0:T(8,128)S(1)}, u32[]{:S(2)}, u32[]{:S(2)}) collective-permute-start(f32[32,128]{1,0:T(8,128)S(1)} %get-tuple-element.24), channel_id=1, source_target_pairs={{1,2},{2,1},{3,4},{4,3},{5,6},{6,5},{7,127},{9,10},{10,9},{11,12},... | collective-permute-start | bytes 49160 | tf_op jit(solution)/shard_map/ppermute | solution.py:331
  23.2 2.2 %copy-start = (f32[64,128,128]{2,1,0:T(8,128)S(1)}, f32[64,128,128]{2,1,0:T(8,128)}, u32[]{:S(2)}) copy-start(f32[64,128,128]{2,1,0:T(8,128)} %weights.3) | copy-start | bytes 12582916
  25.4 21.3 %copy-start.3 = (f32[8,128,128]{2,1,0:T(8,128)S(1)}, f32[8,128,128]{2,1,0:T(8,128)}, u32[]{:S(2)}) copy-start(f32[8,128,128]{2,1,0:T(8,128)} %inverse.2) | copy-start | bytes 1572868
  25.4 21.3 %copy-start.4 = (f32[128,256]{1,0:T(8,128)S(1)}, f32[128,256]{1,0:T(8,128)}, u32[]{:S(2)}) copy-start(f32[128,256]{1,0:T(8,128)} %factor.1) | copy-start | bytes 393220
  49.3 3.8 %copy-start.11 = (s32[8,1,4]{0,2,1:T(4,128)S(1)}, s32[8,1,4]{0,2,1:T(4,128)}, u32[]{:S(2)}) copy-start(s32[8,1,4]{0,2,1:T(4,128)} %param.23) | copy-start | bytes 388
  49.3 4.0 %copy-start.12 = (s32[8,1,4]{0,2,1:T(4,128)S(1)}, s32[8,1,4]{0,2,1:T(4,128)}, u32[]{:S(2)}) copy-start(s32[8,1,4]{0,2,1:T(4,128)} %param.22) | copy-start | bytes 388
  49.3 4.2 %copy-start.7 = (f32[16,256]{1,0:T(8,128)S(1)}, f32[16,256]{1,0:T(8,128)}, u32[]{:S(2)}) copy-start(f32[16,256]{1,0:T(8,128)} %get-tuple-element.15.flux) | copy-start | bytes 49156
  49.3 9.8 %copy-start.6 = (f32[32,32]{1,0:T(8,128)S(1)}, f32[32,32]{1,0:T(8,128)}, u32[]{:S(2)}) copy-start(f32[32,32]{1,0:T(8,128)} %inverse.3) | copy-start | bytes 12292
  49.3 9.8 %copy-start.8 = (f32[8,128]{1,0:T(8,128)S(1)}, f32[8,128]{1,0:T(8,128)}, u32[]{:S(2)}) copy-start(f32[8,128]{1,0:T(8,128)} %diffusivity.1) | copy-start | bytes 12292
  49.3 32.6 %all-to-all-start.1 = ((f32[8,2,16,8,256]{4,3,2,1,0:T(8,128)}), f32[8,2,16,8,256]{4,3,2,1,0:T(8,128)S(1)}, u32[]{:S(2)}, u32[]{:S(2)}) async-start(f32[8,2,16,8,256]{4,3,2,1,0:T(8,128)} %get-tuple-element.25), calls=%async_computation.1 | async-start | bytes 4194304 | tf_op jit(solution)/shard_map/all_to_all | solution.py:367
  53.5 5.6 %collective-permute-start.4 = (f32[16,256]{1,0:T(8,128)S(1)}, f32[16,256]{1,0:T(8,128)S(1)}, u32[]{:S(2)}, u32[]{:S(2)}) collective-permute-start(f32[16,256]{1,0:T(8,128)S(1)} %copy-done.7), channel_id=1, source_target_pairs={{8,0},{16,8},{24,16},{32,24},{40,32},{48,40},{56,48},{64,56},{72,6... | collective-permute-start | bytes 49160 | tf_op jit(solution)/shard_map/ppermute | solution.py:368
